TPU v7x, 32 devices: a whole 2x2x4 slice. The times are simulated.
32 devices in a mesh: path: 8 (over y, x, core), fac: 4 (over z).
Axes of the slice: x: 2, y: 2, z: 4, core: 2. Of those that a mesh axis runs over, the one named last changes fastest.
Arguments:
- shocks: bfloat16 [4, 512, 8192], P(None, 'path', 'fac'), may hold values from -6 to 6
- chol_factor: bfloat16 [8192, 8192], P('path', 'fac')
- factor_vol: float32 [8192], P('fac'), may hold values from 0.3 to 1.5
- trade_loading: bfloat16 [8192, 2048], P(None, 'fac'), may hold values from -0.0625 to 0.0625
- basis_loading: bfloat16 [8192, 64], replicated, may hold values from -0.0625 to 0.0625
- trade_set: int32 [2048], P('fac'), may hold values from 0 to 4095, as said below
Outputs:
- exposure: float32 [4, 512, 4096], P(None, 'path', 'fac')
Inputs may be any that keep to these rules, and one draw needn't show every extreme that they name: Each trade belongs to a netting set of its own block: trade_set[k] // 1024 equals k // 512.
All inputs are finite; a program needn't handle non-finite values.
Results may differ from a plain program's by a relative error of at most 0.0047.
Values may be sent and summed in bfloat16 or wider, within the bound.
No kernel may reach another device: no remote copies, remote signals or barrier semaphores. Data moves between devices by JAX's collectives and lax.ppermute only.
A program may use at most 128 MiB of HBM per device.

v0:
```python
import math

import jax
import jax.numpy as jnp
from jax import lax
from jax.sharding import PartitionSpec as P

F = 8192
NSETS = 4096


def solve_step(gram, moment, basis, total_paths):
    ridged = gram + 0.01 * total_paths * jnp.eye(gram.shape[0], dtype=jnp.float32)
    factor = jnp.linalg.cholesky(ridged)
    coef = jax.scipy.linalg.cho_solve((factor, True), moment)
    predicted = jnp.dot(
        basis, coef, precision=lax.Precision.HIGHEST, preferred_element_type=jnp.float32
    )
    return jnp.maximum(predicted, 0.0)


def on_device(shocks, chol_factor, factor_vol, trade_loading, basis_loading, trade_set):
    step_count, path_count, fac_width = shocks.shape
    row_count = step_count * path_count
    flat_shocks = shocks.reshape(row_count, fac_width)
    factor_share = F // lax.axis_size("fac")
    contract_last = (((1,), (1,)), ((), ()))
    partial_value = lax.dot_general(
        chol_factor,
        lax.all_gather(flat_shocks, "path", axis=0, tiled=True),
        contract_last,
        preferred_element_type=jnp.float32,
    )
    regrouped = lax.all_to_all(partial_value, "path", split_axis=1, concat_axis=0, tiled=True)
    increments = lax.psum_scatter(regrouped, "fac", scatter_dimension=0, tiled=True)
    scaled = increments.reshape(factor_share, step_count, path_count) * (
        factor_vol[:, None, None] / math.sqrt(step_count)
    )
    levels = jnp.cumsum(scaled, axis=1).astype(jnp.bfloat16).reshape(factor_share, row_count)
    basis_count = basis_loading.shape[1]
    contract_first = (((0,), (0,)), ((), ()))
    piece = lax.all_gather(levels, "fac", axis=0, tiled=True)
    trade_sum = lax.dot_general(
        piece, trade_loading, contract_first, preferred_element_type=jnp.float32
    )
    basis_sum = lax.dot_general(
        piece, basis_loading, contract_first, preferred_element_type=jnp.float32
    )
    values = jax.nn.softplus(trade_sum) - 1.0
    sets_here = NSETS // lax.axis_size("fac")
    local_set = trade_set % sets_here
    member = (local_set[:, None] == jnp.arange(sets_here, dtype=jnp.int32)[None, :]).astype(
        jnp.float32
    )
    netting = jnp.dot(
        values, member, precision=lax.Precision.HIGHEST, preferred_element_type=jnp.float32
    )
    basis = jnp.tanh(basis_sum).reshape(step_count, path_count, basis_count)
    netting = netting.reshape(step_count, path_count, sets_here)
    gram = jnp.einsum(
        "tpm,tpn->tmn",
        basis,
        basis,
        precision=lax.Precision.HIGHEST,
        preferred_element_type=jnp.float32,
    )
    moment = jnp.einsum(
        "tpm,tpn->tmn",
        basis,
        netting,
        precision=lax.Precision.HIGHEST,
        preferred_element_type=jnp.float32,
    )
    total_paths = path_count * lax.axis_size("path")
    results = []
    for step in range(step_count):
        gram_total, moment_total = lax.psum((gram[step], moment[step]), "path")
        results.append(solve_step(gram_total, moment_total, basis[step], total_paths))
    return jnp.stack(results)


def solution(mesh):
    in_specs = (P(None, "path", "fac"), P("path", "fac"), P("fac"), P(None, "fac"), P(), P("fac"))
    out_specs = P(None, "path", "fac")
    return jax.shard_map(
        on_device, mesh=mesh, in_specs=in_specs, out_specs=out_specs, check_vma=False
    )
```

profile of v0, /device:TPU:0, one launch (start us, length us, event | category | flops | bytes accessed | tf_op | source)
XLA Modules:
  0.0 548.1 jit_solution(77378516006781580)
XLA Ops:
  6.5 0.7 all-gather.3.cloned.1.call-update
  7.3 59.1 %all-gather.3.cloned.1.call-done = bf16[2048,2048]{1,0:T(8,128)(2,1)} async-done(((bf16[256,2048]{1,0:T(8,128)(2,1)}), bf16[2048,2048]{1,0:T(8,128)(2,1)}) %all-gather.3.cloned.1.call-update) | async-done | bytes 8388624 | tf_op jit(solution)/shard_map/all_gather | solution.py:30
  66.4 12.6 %fusion.53 = f32[1024,2048]{1,0:T(8,128)S(1)} fusion(bf16[1024,2048]{1,0:T(8,128)(2,1)} %param.10, bf16[2048,2048]{1,0:T(8,128)(2,1)} %all-gather.3.cloned.1.call-done), kind=kOutput, calls=%fused_computation.97 | convolution fusion | flops 8589934592 | bytes 20971520 | tf_op jit(solution)/shard_map/dot_general | solution.py:28
  78.9 0.8 copy.38
  79.7 97.5 %all_to_all.19 = f32[1024,8,256]{2,0,1:T(8,128)} all-to-all(f32[1024,8,256]{2,0,1:T(8,128)S(1)} %bitcast.101), channel_id=1, replica_groups=mesh['path'=8,'fac'=4] {'path'}, dimensions={1} | all-to-all | bytes 16777216 | tf_op jit(solution)/shard_map/all_to_all | solution.py:34
  177.3 0.6 copy-done.2
  177.9 143.1 %reduce-scatter.2.cloned.1.call-done = f32[2048,256]{1,0:T(8,128)} async-done(((f32[8192,256]{1,0:T(8,128)}), f32[2048,256]{1,0:T(8,128)}) %reduce-scatter.2.cloned.1.call-update) | async-done | bytes 2097168 | tf_op jit(solution)/shard_map/reduce_scatter | solution.py:35
  321.0 1.9 copy.19
  322.9 1.1 reduce-window_convert_fusion
  324.1 81.6 %all-gather.5.cloned.1.call-done = bf16[8192,256]{0,1:T(8,128)(2,1)} async-done(((bf16[2048,256]{0,1:T(8,128)(2,1)}), bf16[8192,256]{0,1:T(8,128)(2,1)}) %all-gather.5.cloned.1.call-update) | async-done | bytes 4194320 | tf_op jit(solution)/shard_map/all_gather | solution.py:42
  405.7 3.6 convolution_tanh_fusion
  409.7 0.6 slice_bitcast_fusion.7
  410.4 7.0 %fusion.54 = f32[256,512]{1,0:T(8,128)S(1)} fusion(bf16[8192,256]{0,1:T(8,128)(2,1)} %all-gather.5.cloned.1.call-done, bf16[8192,512]{1,0:T(8,128)(2,1)} %param.12), kind=kOutput, calls=%fused_computation.98 | convolution fusion | flops 2147483648 | bytes 13107200 | tf_op jit(solution)/shard_map/dot_general | solution.py:43
  417.4 1.5 fusion.1
  418.9 1.0 fusion.18
  420.2 1.0 slice_bitcast_fusion.3
  421.2 50.9 %all-reduce.5.cloned.1.call-done = (f32[64,64]{0,1:T(8,128)}, f32[64,64]{0,1:T(8,128)}, f32[64,64]{0,1:T(8,128)}, f32[64,64]{0,1:T(8,128)}) async-done(((f32[64,64]{0,1:T(8,128)}, f32[64,64]{0,1:T(8,128)}, f32[64,64]{0,1:T(8,128)}, f32[64,64]{0,1:T(8,128)}), (f32[64,64]{0,1:T(8,128)}, f32[64,64]{0,1:T(8,128)}, f32[64,64]{0,1:T(8,128)}, f32[64,64]{0,1:T(8,128)})) %all-reduce.5.cloned.1.call-update) | async-done | bytes 65552 | tf_op jit(solution)/shard_map/psum | solution.py:77
  472.1 0.8 select_add_fusion.2
  473.0 0.8 fusion.49
  473.8 5.8 %cholesky.74 = f32[64,64]{1,0:T(8,128)S(1)} custom-call(f32[64,64]{1,0:T(8,128)S(1)} %fusion.49), custom_call_target="Cholesky" | custom-call | tf_op jit(solution)/shard_map/jit(cholesky)/cholesky | solution.py:14
  479.7 0.6 compare_reduce_fusion.3
  480.3 0.6 fusion.22
  481.0 0.8 fusion.44
  481.8 5.8 %cholesky.85 = f32[64,64]{1,0:T(8,128)S(1)} custom-call(f32[64,64]{1,0:T(8,128)S(1)} %fusion.44), custom_call_target="Cholesky" | custom-call | tf_op jit(solution)/shard_map/jit(cholesky)/cholesky | solution.py:14
  487.7 0.7 compare_reduce_fusion.2
  488.4 0.7 fusion.23
  489.1 0.8 select_add_fusion
  489.9 0.8 fusion.39
  490.7 5.8 %cholesky.96 = f32[64,64]{1,0:T(8,128)S(1)} custom-call(f32[64,64]{1,0:T(8,128)S(1)} %fusion.39), custom_call_target="Cholesky" | custom-call | tf_op jit(solution)/shard_map/jit(cholesky)/cholesky | solution.py:14
  496.6 0.7 compare_reduce_fusion.1
  497.4 0.8 fusion.34
  498.2 0.7 fusion.24
  498.9 4.9 custom-call.10
  503.8 4.9 custom-call.11
  508.7 4.9 custom-call.12
  513.6 5.8 %cholesky.107 = f32[64,64]{1,0:T(8,128)S(1)} custom-call(f32[64,64]{1,0:T(8,128)S(1)} %fusion.34), custom_call_target="Cholesky" | custom-call | tf_op jit(solution)/shard_map/jit(cholesky)/cholesky | solution.py:14
  519.5 0.7 compare_reduce_fusion
  520.2 0.6 fusion.25
  520.8 4.9 custom-call.13
  525.6 6.9 %all-reduce.7.cloned.1.call-done = (f32[64,1024]{1,0:T(8,128)}, f32[64,1024]{1,0:T(8,128)}, f32[64,1024]{1,0:T(8,128)}, f32[64,1024]{1,0:T(8,128)}) async-done(((f32[64,1024]{1,0:T(8,128)}, f32[64,1024]{1,0:T(8,128)}, f32[64,1024]{1,0:T(8,128)}, f32[64,1024]{1,0:T(8,128)}), (f32[64,1024]{1,0:T(8,128)}, f32[64,1024]{1,0:T(8,128)}, f32[64,1024]{1,0:T(8,128)}, ...) | async-done | bytes 1048592 | tf_op jit(solution)/shard_map/psum | solution.py:77
  532.6 1.4 fusion.47
  534.4 0.4 fusion.5
  534.8 1.4 fusion.42
  536.5 0.5 fusion.4
  537.0 1.4 fusion.37
  538.7 0.4 fusion.3
  540.0 0.5 fusion.2
  540.4 1.1 pad_maximum_fusion
  (33 shorter events, 3.1 us)
Async XLA Ops:
  6.5 399.2 %copy-start = (bf16[8192,64]{0,1:T(8,128)(2,1)S(1)}, bf16[8192,64]{0,1:T(8,128)(2,1)}, u32[]{:S(2)}) copy-start(bf16[8192,64]{0,1:T(8,128)(2,1)} %param.13) | copy-start | bytes 3145732
  6.5 59.8 %all-gather.3.cloned.1.call-start = ((), (), s32[]{:S(2)}) async-start(), calls=%async_computation.2 | async-start | bytes 9437184 | tf_op jit(solution)/shard_map/all_gather | solution.py:30
  7.3 313.7 %reduce-scatter.2.cloned.1.call-start = ((), (), s32[]{:S(2)}) async-start(), calls=%async_computation.3 | async-start | bytes 10485760 | tf_op jit(solution)/shard_map/reduce_scatter | solution.py:35
  177.2 0.7 copy-start.2
  177.2 228.5 %all-gather.5.cloned.1.call-start = ((), (), s32[]{:S(2)}) async-start(), calls=%async_computation.4 | async-start | bytes 5242880 | tf_op jit(solution)/shard_map/all_gather | solution.py:42
  177.9 146.2 %copy-start.3 = (s32[512]{0:T(512)S(1)}, s32[512]{0:T(512)}, u32[]{:S(2)}) copy-start(s32[512]{0:T(512)} %param.14) | copy-start | bytes 6148
  324.0 148.1 %all-reduce.5.cloned.1.call-start = ((), (), s32[]{:S(2)}) async-start(), calls=%async_computation.5 | async-start | bytes 262144 | tf_op jit(solution)/shard_map/psum | solution.py:77
  419.9 112.6 %all-reduce.7.cloned.1.call-start = ((), (), s32[]{:S(2)}) async-start(), calls=%async_computation.6 | async-start | bytes 2097152 | tf_op jit(solution)/shard_map/psum | solution.py:77
  532.6 6.6 %copy-start.1 = (f32[64,1024]{1,0:T(8,128)S(1)}, f32[64,1024]{1,0:T(8,128)}, u32[]{:S(2)}) copy-start(f32[64,1024]{1,0:T(8,128)} %get-tuple-element.11) | copy-start | bytes 786436
Sparse Core Ops, SparseCore 0:
  9.2 57.0 all-gather.2
  177.3 143.5 reduce-scatter.1
  324.2 81.4 all-gather.4
  420.1 52.0 all-reduce.4
  475.8 56.7 all-reduce.6
where the time goes:
time: 549 us; the launch traced here: 548 us
  waiting for transfers between devices  342 us (62%)
  blocking collectives  97.5 us (18%)
  other arithmetic  55.4 us (10%)
  matrix products  33.7 us (6%)
  between operations  13.4 us (2%)
    reduce_scatter x1, waiting for transfers between devices, on_device(): lax.psum_scatter(regrouped, 'fac', scatter_dimension=0, tiled=True)  143 us
    all_to_all x1, blocking collectives, on_device(): lax.all_to_all(partial_value, 'path', split_axis=1, concat_axis=0, tiled=...  97.5 us
    all_gather x1, waiting for transfers between devices, on_device(): piece = lax.all_gather(levels, 'fac', axis=0, tiled=True)  81.6 us
    all_gather x1, waiting for transfers between devices, on_device(): lax.all_gather(flat_shocks, 'path', axis=0, tiled=True)  59.1 us
    psum x2, waiting for transfers between devices, on_device(): gram_total, moment_total = lax.psum((gram[step], moment[step]), 'path')  57.9 us
    another operation x12, other arithmetic, solve_step(): factor = jnp.linalg.cholesky(ridged)  26.2 us
    another operation x8, other arithmetic, solve_step(): coef = jax.scipy.linalg.cho_solve((factor, True), moment)  22.2 us
    dot_general x1, matrix products, on_device(): lax.dot_general(chol_factor, lax.all_gather(flat_shocks, 'path', axis=0,...  12.6 us
  transfers between devices with their start and end apart: 5, of which 5 were waited for; matrix products, arithmetic and copies ran while one was open for 10% of the time, Pallas kernels for 0%

commit v1 on v0

v1 whole, which is shorter than its diff:
```python
import functools
import math

import jax
import jax.numpy as jnp
from jax import lax
from jax.experimental import pallas as pl
from jax.experimental.pallas import tpu as pltpu
from jax.sharding import PartitionSpec as P

NSETS = 4096
HALVES = 2
VMEM_LIMIT = 24 * 2**20
HIGHEST = lax.Precision.HIGHEST
CONTRACT_LAST = (((1,), (1,)), ((), ()))
CONTRACT_FIRST = (((0,), (0,)), ((), ()))


def dot(a, b, dims, precision=None):
    return lax.dot_general(a, b, dims, precision=precision, preferred_element_type=jnp.float32)


def price_kernel(place, *refs):
    trade, basis_load, kept, given, ordered = refs[-5:]
    pieces = refs[:-5]
    fac_size = len(pieces)
    blocks, rows, _ = pieces[0].shape
    drivers = jnp.zeros((fac_size * rows, trade.shape[2]), jnp.float32)
    projected = jnp.zeros((fac_size * rows, basis_load.shape[1]), jnp.float32)
    for n in range(blocks):
        levels = jnp.concatenate([piece[n] for piece in pieces], axis=0)
        factors = place[2 + n]
        drivers += jnp.dot(levels, trade[factors], preferred_element_type=jnp.float32)
        projected += dot(levels, basis_load[factors], CONTRACT_LAST)
    values = jnp.maximum(drivers, 0.0) + jnp.log1p(jnp.exp(-jnp.abs(drivers))) - 1.0
    basis = jnp.tanh(projected)
    steps, paths, basis_count = ordered.shape
    share = paths // fac_size
    fac_index, core = place[0], place[1]
    sums = []
    for step in range(steps):
        spans = [
            slice((hop * steps + step) * share, (hop * steps + step + 1) * share)
            for hop in range(fac_size)
        ]
        for hop in range(fac_size):
            source = lax.rem(fac_index - hop + fac_size, fac_size)
            at = pl.multiple_of(source * share, share)
            ordered[step, pl.ds(at, share), :] = basis[spans[hop]]
        step_basis = jnp.concatenate([basis[s] for s in spans], axis=0)
        step_values = jnp.concatenate([values[s] for s in spans], axis=0)
        joint = jnp.concatenate([step_values, step_basis, step_basis], axis=1)
        sums.append(dot(step_basis, joint, CONTRACT_FIRST, HIGHEST))
    kept[...] = jnp.where(core == 0, sums[0], sums[1])
    given[...] = jnp.where(core == 0, sums[1], sums[0])


def price(pieces, trade_blocks, basis_blocks, place, steps, paths):
    fac_size = len(pieces)
    blocks, rows, width = pieces[0].shape
    trades, basis_count = trade_blocks.shape[2], basis_blocks.shape[1]
    sums = jax.ShapeDtypeStruct((basis_count, trades + 2 * basis_count), jnp.float32)
    vmem = pl.BlockSpec(memory_space=pltpu.VMEM)
    return pl.pallas_call(
        price_kernel,
        in_specs=[pl.BlockSpec(memory_space=pltpu.SMEM)] + [vmem] * (fac_size + 2),
        out_specs=[vmem] * 3,
        out_shape=[sums, sums, jax.ShapeDtypeStruct((steps, paths, basis_count), jnp.float32)],
        compiler_params=pltpu.CompilerParams(vmem_limit_bytes=VMEM_LIMIT),
        cost_estimate=pl.CostEstimate(
            flops=2 * fac_size * rows * blocks * width * (trades + basis_count),
            bytes_accessed=2 * blocks * width * (trades + fac_size * rows),
            transcendentals=2 * fac_size * rows * trades,
        ),
        name="price",
    )(place, *pieces, trade_blocks, basis_blocks)


def solve_kernel(ridge, first_top, first_bottom, second_top, second_bottom, coef):
    count, trades = coef.shape
    sums = jnp.concatenate(
        [first_top[...] + second_top[...], first_bottom[...] + second_bottom[...]], axis=0
    )
    row = lax.broadcasted_iota(jnp.int32, (count, 2 * count), 0)
    lane = lax.broadcasted_iota(jnp.int32, (count, 2 * count), 1)
    work = jnp.where(lane < count, sums[:, trades:], 0.0)
    work = work + jnp.where(lane == row, ridge, 0.0) + jnp.where(lane == row + count, 1.0, 0.0)
    for j in range(0, count, 2):
        left = jnp.broadcast_to(work[:, j : j + 1], work.shape)
        right = jnp.broadcast_to(work[:, j + 1 : j + 2], work.shape)
        upper, lower = work[j : j + 1, :], work[j + 1 : j + 2, :]
        a, b = left[j : j + 1, :], right[j : j + 1, :]
        c, d = left[j + 1 : j + 2, :], right[j + 1 : j + 2, :]
        scale = 1.0 / (a * d - b * c)
        new_upper = (d * upper - b * lower) * scale
        new_lower = (a * lower - c * upper) * scale
        work = work - left * new_upper - right * new_lower
        work = jnp.where(row == j, new_upper, jnp.where(row == j + 1, new_lower, work))
    coef[...] = jnp.dot(
        work[:, count:], sums[:, :trades], precision=HIGHEST, preferred_element_type=jnp.float32
    )


def solve(parts, trades, ridge):
    count = 2 * parts[0].shape[0]
    return pl.pallas_call(
        functools.partial(solve_kernel, ridge),
        out_shape=jax.ShapeDtypeStruct((count, trades), jnp.float32),
        compiler_params=pltpu.CompilerParams(vmem_limit_bytes=VMEM_LIMIT),
        cost_estimate=pl.CostEstimate(
            flops=2 * count**3 + 12 * count * count * trades,
            bytes_accessed=4 * count * trades * 3,
            transcendentals=0,
        ),
        name="solve",
    )(*parts)


def expose_kernel(place, basis, mine, other, member, *refs):
    out = refs[-1]
    core = place[1]
    steps, paths, sets = out.shape
    by_trade = jnp.concatenate(
        [
            jnp.dot(
                basis[step],
                jnp.where(core == step, mine[...], other[...]),
                precision=HIGHEST,
                preferred_element_type=jnp.float32,
            )
            for step in range(steps)
        ],
        axis=0,
    )
    terms = []
    for _ in range(3):
        term = by_trade.astype(jnp.bfloat16)
        by_trade = by_trade - term.astype(jnp.float32)
        terms.append(term)
    spread = [jnp.dot(t, member[...], preferred_element_type=jnp.float32) for t in terms]
    total = jnp.maximum(spread[0] + (spread[1] + spread[2]), 0.0)
    for step in range(steps):
        out[step] = total[step * paths : (step + 1) * paths]


def expose(place, basis, mine, other, member, half, so_far):
    steps, paths, _ = basis.shape
    trades, sets = member.shape
    vmem = pl.BlockSpec(memory_space=pltpu.VMEM)
    block = pl.BlockSpec((steps, paths, sets), lambda i: (half, 0, 0))
    earlier = [] if so_far is None else [so_far]
    return pl.pallas_call(
        expose_kernel,
        grid=(1,),
        in_specs=[pl.BlockSpec(memory_space=pltpu.SMEM)]
        + [vmem] * 4
        + [pl.BlockSpec(memory_space=pl.ANY)] * len(earlier),
        out_specs=block,
        out_shape=jax.ShapeDtypeStruct((HALVES * steps, paths, sets), jnp.float32),
        input_output_aliases={5: 0} if earlier else {},
        compiler_params=pltpu.CompilerParams(vmem_limit_bytes=VMEM_LIMIT),
        cost_estimate=pl.CostEstimate(
            flops=6 * steps * paths * trades * sets,
            bytes_accessed=4 * steps * paths * sets * 2,
            transcendentals=0,
        ),
        name="expose",
    )(place, basis, mine, other, member, *earlier)


def on_device(shocks, chol_factor, factor_vol, trade_loading, basis_loading, trade_set):
    step_count, path_count, fac_width = shocks.shape
    row_block = chol_factor.shape[0]
    factor_count, trade_count = trade_loading.shape
    path_size, fac_size = lax.axis_size("path"), lax.axis_size("fac")
    path_index, fac_index = lax.axis_index("path"), lax.axis_index("fac")
    share = path_count // fac_size
    half_steps = step_count // HALVES
    chunk_rows = half_steps * share
    sets_here = NSETS // fac_size
    ridge = 0.01 * path_count * path_size
    even = list(range(2, path_size, 2))
    bits = [2**n for n in range(1, path_size.bit_length() - 1)]
    place = jnp.concatenate(
        [
            jnp.stack([fac_index, path_index & 1]),
            path_index ^ jnp.arange(path_size, dtype=jnp.int32),
        ]
    ).astype(jnp.int32)

    def exchange(x, k):
        return lax.ppermute(x, "path", [(i, i ^ k) for i in range(path_size)])

    def pass_on(x, hops=1):
        return lax.ppermute(x, "fac", [(i, (i + hops) % fac_size) for i in range(fac_size)])

    last = []

    def gate(*values):
        held = lax.optimization_barrier((values, tuple(last)))[0]
        return held[0] if len(held) == 1 else held

    def mark(*values):
        last[:] = values
        return values[0]

    def partial_sums(block, scale):
        product = dot(block.reshape(-1, fac_width), chol_factor, CONTRACT_LAST)
        if scale is not None:
            product = product * scale
        return product.reshape(block.shape[0], fac_size, chunk_rows, row_block)

    def reduce_over_fac(block, scale, kind):
        terms = partial_sums(gate(block), scale)
        running = None
        for hop in range(fac_size):
            term = terms[:, hop]
            if running is not None:
                term = term + gate(running).astype(jnp.float32)
            if hop < fac_size - 1:
                running = pass_on(mark(term.astype(kind)))
                yield None
        yield mark(term).reshape(-1, half_steps, share, row_block)

    def gather_over_fac(piece):
        pieces = [mark(piece)]
        for _ in range(fac_size - 1):
            pieces.append(pass_on(pieces[-1]))
            yield None
            pieces[-1] = mark(gate(pieces[-1]))
        yield pieces

    by_share = shocks.reshape(HALVES, half_steps, fac_size, share, fac_width)
    ordered = jnp.stack(
        [
            lax.dynamic_index_in_dim(by_share, (fac_index - 1 - s) % fac_size, axis=2, keepdims=False)
            for s in range(fac_size)
        ],
        axis=1,
    ).reshape(HALVES, fac_size * chunk_rows, fac_width)

    own = mark(ordered[0])
    received = [exchange(own, k) for k in even]
    chain_a = reduce_over_fac(jnp.stack([own, exchange(own, 1)]), None, jnp.float32)
    next(chain_a)

    row_peak = jnp.max(jnp.abs(chol_factor), axis=1).astype(jnp.float32)
    vols, note = gate(factor_vol), None
    bit = 1
    while bit < fac_size:
        note = mark(jnp.concatenate([vols, row_peak]))
        swap = [(i, i ^ bit) for i in range(fac_size)]
        arrived = lax.ppermute(note, "fac", swap)
        next(chain_a)
        arrived = gate(arrived)
        split = arrived.shape[0] - row_block
        lower = (fac_index & bit) == 0
        vols = jnp.where(
            lower,
            jnp.concatenate([vols, arrived[:split]]),
            jnp.concatenate([arrived[:split], vols]),
        )
        row_peak = jnp.maximum(row_peak, arrived[split:])
        bit *= 2
    vol = lax.dynamic_slice(vols, (path_index * row_block,), (row_block,)) / math.sqrt(step_count)
    peak = jnp.clip(row_peak, 1e-30, 1e37) * (6.0 * factor_count / 49152.0)
    shrink = 1.0 / peak
    mark(shrink)

    trade_blocks = trade_loading.reshape(path_size, row_block, trade_count)
    basis_blocks = basis_loading.T.reshape(-1, path_size, row_block).transpose(1, 0, 2)
    local_set = trade_set % sets_here
    member = (local_set[:, None] == jnp.arange(sets_here, dtype=jnp.int32)[None, :]).astype(
        jnp.bfloat16
    )

    def levels_of(increments, carry):
        levels = []
        for step in range(half_steps):
            carry = carry + increments[:, step]
            levels.append((carry * vol).astype(jnp.bfloat16))
        return jnp.stack(levels, axis=1).reshape(-1, chunk_rows, row_block), carry

    def regroup(mine, others):
        arrived = exchange(mark(others), 1)
        yield None
        pairs = mark(jnp.stack([mine, gate(arrived)], axis=1))
        pairs = [pairs[0]] + [exchange(pairs[k // 2], k) for k in even]
        yield None
        yield jnp.concatenate(gate(*pairs), axis=0)

    def priced(pieces):
        kept, given, basis = price(pieces, trade_blocks, basis_blocks, place, half_steps, path_count)
        mark(given)
        return kept, given, basis

    def finish(kept, given, basis, half):
        arrived = exchange(given, 1)
        yield None
        total = mark(kept + gate(arrived))
        rows = total.shape[0] // 2
        top, bottom = total[:rows], total[rows:]
        for n, bit in enumerate(bits):
            more = exchange(top, bit), exchange(bottom, bits[-1 - n])
            yield None
            more = gate(*more)
            if n < len(bits) - 1:
                top, bottom = top + more[0], bottom + more[1]
                mark(top, bottom)
        coef = mark(solve((top, bottom, *more), trade_count, ridge))
        other = exchange(coef, 1)
        so_far = yield None
        yield mark(expose(place, basis, coef, gate(other), member, half, so_far))

    for _ in range(fac_size - 2 - (fac_size.bit_length() - 1)):
        next(chain_a)
    rest = mark(jnp.stack(gate(*received)))
    arrived = exchange(rest, 1)
    own = gate(ordered[1])
    received = [exchange(own, k) for k in even]
    chain_b = reduce_over_fac(rest, shrink, jnp.float16)
    next(chain_b)
    near_sum = next(chain_a)
    chain_c = reduce_over_fac(arrived, shrink, jnp.float16)
    next(chain_c)
    for hop in range(1, fac_size - 1):
        next(chain_b)
        next(chain_c)
    block = mark(jnp.stack([own, *gate(*received)]))
    arrived = exchange(block, 1)
    chain_d = reduce_over_fac(block, shrink, jnp.float16)
    next(chain_d)
    mine = jnp.concatenate([near_sum[:1], next(chain_b) * peak])
    mine, carry = levels_of(mine, 0.0)
    others = jnp.concatenate([near_sum[1:], next(chain_c) * peak])
    others, other_carry = levels_of(others, 0.0)
    first = regroup(mine, others)
    next(first)
    chain_e = reduce_over_fac(arrived, shrink, jnp.float16)
    next(chain_e)
    next(first)
    next(chain_d)
    next(chain_e)
    ring_first = gather_over_fac(next(first))
    next(ring_first)
    for hop in range(2, fac_size - 1):
        next(chain_d)
        next(chain_e)
    mine, _ = levels_of(next(chain_d) * peak, carry)
    others, _ = levels_of(next(chain_e) * peak, other_carry)
    second = regroup(mine, others)
    next(second)
    next(ring_first)
    next(second)
    for hop in range(2, fac_size - 1):
        next(ring_first)
    ring_second = gather_over_fac(next(second))
    next(ring_second)
    first = finish(*priced(next(ring_first)), 0)
    next(first)
    to_do = len(bits)
    for hop in range(1, fac_size - 1):
        next(ring_second)
        if to_do > 0:
            next(first)
            to_do -= 1
    for _ in range(to_do):
        next(first)
    second = finish(*priced(next(ring_second)), 1)
    next(second)
    next(second)
    next(first)
    for _ in range(len(bits) - 1):
        next(second)
    result = next(first)
    next(second)
    return second.send(result)


def solution(mesh):
    in_specs = (P(None, "path", "fac"), P("path", "fac"), P("fac"), P(None, "fac"), P(), P("fac"))
    out_specs = P(None, "path", "fac")
    return jax.shard_map(
        on_device, mesh=mesh, in_specs=in_specs, out_specs=out_specs, check_vma=False
    )
```

time: 549 us -> 214 us (0.39)
  waiting for transfers between devices: 342 us -> 135 us
  blocking collectives: 97.5 us -> 0 us
  other arithmetic: 55.4 us -> 4.69 us
  starting transfers between devices: 0.35 us -> 34.8 us
  matrix products: 33.7 us -> 9.77 us
  Pallas kernels: 0 us -> 17.9 us
  between operations: 13.4 us -> 0.79 us
  local copies, waits for them, and re-layouts: 5.39 us -> 11.4 us
    reduce_scatter x1 -> x0, waiting for transfers between devices: 143 us -> none  [on_device(): lax.psum_scatter(regrouped, 'fac', scatter_dimension=0, tiled=True)]
    all_gather x2 -> x0, waiting for transfers between devices: 141 us -> none  [the longest x1 81.6 us: on_device(): piece = lax.all_gather(levels, 'fac', axis=0, tiled=True)]
    ppermute x0 -> x52, waiting for transfers between devices: none -> 135 us  [the longest x21 122 us: pass_on(): lax.ppermute(x, 'fac', [(i, (i + hops) % fac_size) for i in range(fac_siz...]
    all_to_all x1 -> x0, blocking collectives: 97.5 us -> none  [on_device(): lax.all_to_all(partial_value, 'path', split_axis=1, concat_axis=0, tiled=...]
    psum x2 -> x0, waiting for transfers between devices: 57.9 us -> none  [on_device(): gram_total, moment_total = lax.psum((gram[step], moment[step]), 'path')]
    another operation x22 -> x8, other arithmetic: 50.7 us -> 1.82 us  [the longest x1 1.21 us: on_device(): rest = mark(jnp.stack(gate(*received)))]
    ppermute x0 -> x52, starting transfers between devices: none -> 34.8 us  [the longest x29 23.9 us: exchange(): return lax.ppermute(x, 'path', [(i, i ^ k) for i in range(path_size)])]
    dot_general x10 -> x5, matrix products: 27.8 us -> 9.77 us  [dot(): lax.dot_general(a, b, dims, precision=precision, preferred_element_type=j...]
  transfers between devices with their start and end apart: 5 -> 52, of which waited for: 5 -> 31; matrix products, arithmetic and copies ran while one was open for 10% -> 8% of each run, Pallas kernels for 0% -> 4%
where the time goes in v1:
time: 214 us
  waiting for transfers between devices  135 us (63%)
  starting transfers between devices  34.8 us (16%)
  Pallas kernels  17.9 us (8%)
  local copies, waits for them, and re-layouts  11.4 us (5%)
  matrix products  9.77 us (5%)
  other arithmetic  4.69 us (2%)
    ppermute x21, waiting for transfers between devices, pass_on(): lax.ppermute(x, 'fac', [(i, (i + hops) % fac_size) for i in range(fac_siz...  122 us
    ppermute x29, starting transfers between devices, exchange(): return lax.ppermute(x, 'path', [(i, i ^ k) for i in range(path_size)])  23.9 us
    ppermute x29, waiting for transfers between devices, exchange(): return lax.ppermute(x, 'path', [(i, i ^ k) for i in range(path_size)])  12.5 us
    dot_general x5, matrix products, dot(): lax.dot_general(a, b, dims, precision=precision, preferred_element_type=j...  9.77 us
    ppermute x21, starting transfers between devices, pass_on(): lax.ppermute(x, 'fac', [(i, (i + hops) % fac_size) for i in range(fac_siz...  7 us
    unnamed x20, local copies, waits for them, and re-layouts  6.85 us
    pallas_call x2, Pallas kernels, solve(): pl.pallas_call(functools.partial(solve_kernel, ridge), out_shape=jax.Shap...  6.72 us
    pallas_call x2, Pallas kernels, price(): pl.pallas_call(price_kernel, in_specs=[pl.BlockSpec(memory_space=pltpu.SM...  6.71 us
  transfers between devices with their start and end apart: 52, of which 31 were waited for; matrix products, arithmetic and copies ran while one was open for 8% of the time, Pallas kernels for 4%

profile of v1, /device:TPU:0, one launch (start us, length us, event | category | flops | bytes accessed | tf_op | source)
XLA Modules:
  0.0 214.0 jit_solution(629770263947016097)
XLA Ops:
  2.0 2.6 %collective-permute-start.5 = (bf16[128,2048]{1,0:T(8,128)(2,1)S(1)}, bf16[128,2048]{1,0:T(8,128)(2,1)S(1)}, u32[]{:S(2)}, u32[]{:S(2)}) collective-permute-start(bf16[128,2048]{1,0:T(8,128)(2,1)S(1)} %bitcast.188), channel_id=1, source_target_pairs={{0,8},{4,12},{8,0},{12,4},{16,24},{20,28},{24,16},{28,20},{1,9},{5... | collective-permute-start | bytes 1572872 | tf_op jit(solution)/shard_map/ppermute | solution.py:192
  4.6 1.5 collective-permute-start.6
  8.4 2.0 collective-permute-start.1
  11.3 1.6 collective-permute-start.3
  13.0 5.9 %collective-permute-done.1 = f32[2,32,1024]{2,1,0:T(8,128)S(1)} collective-permute-done((f32[2,32,1024]{2,1,0:T(8,128)}, f32[2,32,1024]{2,1,0:T(8,128)S(1)}, u32[]{:S(2)}, u32[]{:S(2)}) %collective-permute-start.1) | collective-permute-done | bytes 262176 | tf_op jit(solution)/shard_map/ppermute | solution.py:195
  19.1 2.3 %collective-permute-start.8 = (f32[5120]{0:T(1024)S(1)}, f32[5120]{0:T(1024)S(1)}, u32[]{:S(2)}, u32[]{:S(2)}) collective-permute-start(f32[5120]{0:T(1024)S(1)} %pad_maximum_fusion.12), channel_id=1, source_target_pairs={{0,2},{1,3},{2,0},{3,1},{4,6},{5,7},{6,4},{7,5},{8,10},{9,11},{10,... | collective-permute-start | bytes 61448 | tf_op jit(solution)/shard_map/ppermute | solution.py:253
  21.4 6.8 %collective-permute-done.2 = f32[2,32,1024]{2,1,0:T(8,128)S(1)} collective-permute-done((f32[2,32,1024]{2,1,0:T(8,128)S(1)}, f32[2,32,1024]{2,1,0:T(8,128)S(1)}, u32[]{:S(2)}, u32[]{:S(2)}) %collective-permute-start.2) | collective-permute-done | bytes 262176 | tf_op jit(solution)/shard_map/ppermute | solution.py:195
  31.1 1.4 collective-permute-start.14
  33.3 1.4 collective-permute-start.16
  34.7 1.8 convolution_multiply_fusion.3
  37.3 1.6 collective-permute-start.9
  39.0 1.8 convolution_multiply_fusion.2
  41.0 1.6 collective-permute-start.12
  42.6 3.9 %collective-permute-done.9 = f16[3,32,1024]{2,1,0:T(8,128)(2,1)S(1)} collective-permute-done((f16[3,32,1024]{2,1,0:T(8,128)(2,1)S(1)}, f16[3,32,1024]{2,1,0:T(8,128)(2,1)S(1)}, u32[]{:S(2)}, u32[]{:S(2)}) %collective-permute-start.9) | collective-permute-done | bytes 196640 | tf_op jit(solution)/shard_map/ppermute | solution.py:195
  46.6 4.1 %collective-permute-done.12 = f16[3,32,1024]{2,1,0:T(8,128)(2,1)S(1)} collective-permute-done((f16[3,32,1024]{2,1,0:T(8,128)(2,1)S(1)}, f16[3,32,1024]{2,1,0:T(8,128)(2,1)S(1)}, u32[]{:S(2)}, u32[]{:S(2)}) %collective-permute-start.12) | collective-permute-done | bytes 196640 | tf_op jit(solution)/shard_map/ppermute | solution.py:195
  50.8 3.6 %collective-permute-done.11 = f16[3,32,1024]{2,1,0:T(8,128)(2,1)S(1)} collective-permute-done((f16[3,32,1024]{2,1,0:T(8,128)(2,1)S(1)}, f16[3,32,1024]{2,1,0:T(8,128)(2,1)S(1)}, u32[]{:S(2)}, u32[]{:S(2)}) %collective-permute-start.11) | collective-permute-done | bytes 196640 | tf_op jit(solution)/shard_map/ppermute | solution.py:195
  54.8 5.5 %collective-permute-done.17 = f16[3,32,1024]{2,1,0:T(8,128)(2,1)S(1)} collective-permute-done((f16[3,32,1024]{2,1,0:T(8,128)(2,1)S(1)}, f16[3,32,1024]{2,1,0:T(8,128)(2,1)S(1)}, u32[]{:S(2)}, u32[]{:S(2)}) %collective-permute-start.17) | collective-permute-done | bytes 196640 | tf_op jit(solution)/shard_map/ppermute | solution.py:195
  60.8 2.4 %convolution_multiply_fusion.1 = f32[512,1024]{1,0:T(8,128)S(1)} fusion(bf16[512,2048]{1,0:T(8,128)(2,1)S(1)} %bitcast.184, bf16[1024,2048]{1,0:T(8,128)(2,1)S(1)} %copy-done.3, f32[1024]{0:T(1024)S(1)} %get-tuple-element.137), kind=kOutput, calls=%fused_computation.7 | convolution fusion | flops 2148007936 | bytes 8392704 | tf_op jit(solution)/shard_map/dot_general | solution.py:20
  64.5 3.3 %collective-permute-done.19 = f16[3,32,1024]{2,1,0:T(8,128)(2,1)S(1)} collective-permute-done((f16[3,32,1024]{2,1,0:T(8,128)(2,1)S(1)}, f16[3,32,1024]{2,1,0:T(8,128)(2,1)S(1)}, u32[]{:S(2)}, u32[]{:S(2)}) %collective-permute-start.19) | collective-permute-done | bytes 196640 | tf_op jit(solution)/shard_map/ppermute | solution.py:195
  68.3 6.1 %collective-permute-done.18 = f16[4,32,1024]{2,1,0:T(8,128)(2,1)S(1)} collective-permute-done((f16[4,32,1024]{2,1,0:T(8,128)(2,1)S(1)}, f16[4,32,1024]{2,1,0:T(8,128)(2,1)S(1)}, u32[]{:S(2)}, u32[]{:S(2)}) %collective-permute-start.18) | collective-permute-done | bytes 262176 | tf_op jit(solution)/shard_map/ppermute | solution.py:195
  74.3 2.4 %convolution_multiply_fusion = f32[512,1024]{1,0:T(8,128)S(1)} fusion(bf16[512,2048]{1,0:T(8,128)(2,1)S(1)} %bitcast.220, bf16[1024,2048]{1,0:T(8,128)(2,1)S(1)} %copy-done.3, f32[1024]{0:T(1024)S(1)} %get-tuple-element.137), kind=kOutput, calls=%fused_computation.6 | convolution fusion | flops 2148007936 | bytes 8392704 | tf_op jit(solution)/shard_map/dot_general | solution.py:20
  79.7 1.4 collective-permute-start.25
  81.1 6.9 %collective-permute-done.26 = f16[4,32,1024]{2,1,0:T(8,128)(2,1)S(1)} collective-permute-done((f16[4,32,1024]{2,1,0:T(8,128)(2,1)S(1)}, f16[4,32,1024]{2,1,0:T(8,128)(2,1)S(1)}, u32[]{:S(2)}, u32[]{:S(2)}) %collective-permute-start.26) | collective-permute-done | bytes 262176 | tf_op jit(solution)/shard_map/ppermute | solution.py:195
  88.2 5.4 %collective-permute-done.22 = f16[4,32,1024]{2,1,0:T(8,128)(2,1)S(1)} collective-permute-done((f16[4,32,1024]{2,1,0:T(8,128)(2,1)S(1)}, f16[4,32,1024]{2,1,0:T(8,128)(2,1)S(1)}, u32[]{:S(2)}, u32[]{:S(2)}) %collective-permute-start.22) | collective-permute-done | bytes 262176 | tf_op jit(solution)/shard_map/ppermute | solution.py:195
  93.7 5.5 %collective-permute-done.28 = f16[4,32,1024]{2,1,0:T(8,128)(2,1)S(1)} collective-permute-done((f16[4,32,1024]{2,1,0:T(8,128)(2,1)S(1)}, f16[4,32,1024]{2,1,0:T(8,128)(2,1)S(1)}, u32[]{:S(2)}, u32[]{:S(2)}) %collective-permute-start.28) | collective-permute-done | bytes 262176 | tf_op jit(solution)/shard_map/ppermute | solution.py:195
  99.4 5.4 %collective-permute-done.27 = f16[4,32,1024]{2,1,0:T(8,128)(2,1)S(1)} collective-permute-done((f16[4,32,1024]{2,1,0:T(8,128)(2,1)S(1)}, f16[4,32,1024]{2,1,0:T(8,128)(2,1)S(1)}, u32[]{:S(2)}, u32[]{:S(2)}) %collective-permute-start.27) | collective-permute-done | bytes 262176 | tf_op jit(solution)/shard_map/ppermute | solution.py:195
  104.9 5.5 %collective-permute-done.29 = f16[4,32,1024]{2,1,0:T(8,128)(2,1)S(1)} collective-permute-done((f16[4,32,1024]{2,1,0:T(8,128)(2,1)S(1)}, f16[4,32,1024]{2,1,0:T(8,128)(2,1)S(1)}, u32[]{:S(2)}, u32[]{:S(2)}) %collective-permute-start.29) | collective-permute-done | bytes 262176 | tf_op jit(solution)/shard_map/ppermute | solution.py:195
  110.9 9.7 %collective-permute-done.31.refs_1_ = bf16[8,32,1024]{2,1,0:T(8,128)(2,1)S(1)} collective-permute-done((bf16[8,32,1024]{2,1,0:T(8,128)(2,1)S(1)}, bf16[8,32,1024]{2,1,0:T(8,128)(2,1)S(1)}, u32[]{:S(2)}, u32[]{:S(2)}) %collective-permute-start.31) | collective-permute-done | bytes 524320 | tf_op jit(solution)/shard_map/ppermute | solution.py:195
  120.6 1.5 collective-permute-done.30
  124.3 1.4 collective-permute-start.34
  125.7 9.5 %collective-permute-done.35.refs_2_ = bf16[8,32,1024]{2,1,0:T(8,128)(2,1)S(1)} collective-permute-done((bf16[8,32,1024]{2,1,0:T(8,128)(2,1)S(1)}, bf16[8,32,1024]{2,1,0:T(8,128)(2,1)S(1)}, u32[]{:S(2)}, u32[]{:S(2)}) %collective-permute-start.35) | collective-permute-done | bytes 524320 | tf_op jit(solution)/shard_map/ppermute | solution.py:195
  136.8 15.1 %collective-permute-done.37.refs_3_ = bf16[8,32,1024]{2,1,0:T(8,128)(2,1)S(1)} collective-permute-done((bf16[8,32,1024]{2,1,0:T(8,128)(2,1)S(1)}, bf16[8,32,1024]{2,1,0:T(8,128)(2,1)S(1)}, u32[]{:S(2)}, u32[]{:S(2)}) %collective-permute-start.37) | collective-permute-done | bytes 524320 | tf_op jit(solution)/shard_map/ppermute | solution.py:195
  151.9 3.4 %copy-done = bf16[8192,512]{1,0:T(8,128)(2,1)S(1)} copy-done((bf16[8192,512]{1,0:T(8,128)(2,1)S(1)}, bf16[8192,512]{1,0:T(8,128)(2,1)}, u32[]{:S(2)}) %copy-start) | copy-done | bytes 8388632
  155.3 3.4 %price.2 = (f32[64,640]{1,0:T(8,128)S(1)}, f32[64,640]{1,0:T(8,128)S(1)}, f32[2,64,64]{2,1,0:T(8,128)S(1)}) custom-call(s32[10]{0:T(128)S(1)} %pad_add_fusion.place, bf16[8,32,1024]{2,1,0:T(8,128)(2,1)S(1)} %constant_dynamic-update-slice_fusion.refs_0_, bf16[8,32,1024]{2,1,0:T(8,128)(2,1)S(1)} %collective-permute-done.31.refs_1_, ...), custom_call_target="tpu_custom_call" | custom-call | flops 1207959552 | bytes 10485760 | tf_op jit(solution)/shard_map/price/pallas_call | solution.py:64
  158.7 1.5 collective-permute-done.36.refs_1_
  161.6 11.4 %collective-permute-done.38.refs_2_ = bf16[8,32,1024]{2,1,0:T(8,128)(2,1)S(1)} collective-permute-done((bf16[8,32,1024]{2,1,0:T(8,128)(2,1)S(1)}, bf16[8,32,1024]{2,1,0:T(8,128)(2,1)S(1)}, u32[]{:S(2)}, u32[]{:S(2)}) %collective-permute-start.38) | collective-permute-done | bytes 524320 | tf_op jit(solution)/shard_map/ppermute | solution.py:195
  175.1 2.4 %collective-permute-done.41 = f32[32,640]{1,0:T(8,128)S(1)} collective-permute-done((f32[32,640]{1,0:T(8,128)S(1)}, f32[32,640]{1,0:T(8,128)S(1)}, u32[]{:S(2)}, u32[]{:S(2)}) %collective-permute-start.41) | collective-permute-done | bytes 81952 | tf_op jit(solution)/shard_map/ppermute | solution.py:192
  178.9 6.0 %collective-permute-done.40.refs_3_ = bf16[8,32,1024]{2,1,0:T(8,128)(2,1)S(1)} collective-permute-done((bf16[8,32,1024]{2,1,0:T(8,128)(2,1)S(1)}, bf16[8,32,1024]{2,1,0:T(8,128)(2,1)S(1)}, u32[]{:S(2)}, u32[]{:S(2)}) %collective-permute-start.40) | collective-permute-done | bytes 524320 | tf_op jit(solution)/shard_map/ppermute | solution.py:195
  184.9 3.4 %copy-done.1 = bf16[8192,512]{1,0:T(8,128)(2,1)S(1)} copy-done((bf16[8192,512]{1,0:T(8,128)(2,1)S(1)}, bf16[8192,512]{1,0:T(8,128)(2,1)}, u32[]{:S(2)}) %copy-start.1) | copy-done | bytes 8388632
  188.3 3.3 %price.3 = (f32[64,640]{1,0:T(8,128)S(1)}, f32[64,640]{1,0:T(8,128)S(1)}, f32[2,64,64]{2,1,0:T(8,128)S(1)}) custom-call(s32[10]{0:T(128)S(1)} %pad_add_fusion.place, bf16[8,32,1024]{2,1,0:T(8,128)(2,1)S(1)} %constant_dynamic-update-slice_fusion.4.refs_0_, bf16[8,32,1024]{2,1,0:T(8,128)(2,1)S(1)} %collective-permute-done.36.refs_1_, ...), custom_call_target="tpu_custom_call" | custom-call | flops 1207959552 | bytes 10485760 | tf_op jit(solution)/shard_map/price/pallas_call | solution.py:64
  191.7 1.6 collective-permute-start.46
  193.8 1.6 collective-permute-start.44
  196.5 2.0 collective-permute-done.47.second_bottom
  198.5 3.4 %solve.2.mine = f32[64,512]{1,0:T(8,128)S(1)} custom-call(f32[32,640]{1,0:T(8,128)S(1)} %get-tuple-element.178.first_top, f32[32,640]{1,0:T(8,128)S(1)} %get-tuple-element.177.first_bottom, f32[32,640]{1,0:T(8,128)S(1)} %collective-permute-done.46.second_top, f32[32,640]{1,0:T(8,128)S(1)} %collective-permute-done.47.second_bottom), custom_call_target="tpu_custom_call" | custom-call | flops 25690112 | bytes 393216 | tf_op jit(solution)/shard_map/solve/pallas_call | solution.py:106
  202.4 1.5 collective-permute-start.49
  204.2 2.2 %expose.2.refs_0_ = f32[4,64,1024]{2,1,0:T(8,128)} custom-call(s32[10]{0:T(128)S(1)} %pad_add_fusion.place, f32[2,64,64]{2,1,0:T(8,128)S(1)} %get-tuple-element.128.basis, f32[64,512]{1,0:T(8,128)S(1)} %solve.2.mine, f32[64,512]{1,0:T(8,128)S(1)} %collective-permute-done.50.other, bf16[512,1024]{1,0:T(8,128)(2,1)S(1)} %fusion.2.member), custom_call_target="tpu_custom_call" | custom-call | flops 402653184 | bytes 1048576 | tf_op jit(solution)/shard_map/expose/pallas_call | solution.py:152
  207.0 3.4 %solve.3.mine = f32[64,512]{1,0:T(8,128)S(1)} custom-call(f32[32,640]{1,0:T(8,128)S(1)} %get-tuple-element.174.first_top, f32[32,640]{1,0:T(8,128)S(1)} %get-tuple-element.173.first_bottom, f32[32,640]{1,0:T(8,128)S(1)} %collective-permute-done.48.second_top, f32[32,640]{1,0:T(8,128)S(1)} %collective-permute-done.49.second_bottom), custom_call_target="tpu_custom_call" | custom-call | flops 25690112 | bytes 393216 | tf_op jit(solution)/shard_map/solve/pallas_call | solution.py:106
  211.8 2.2 %expose.3 = f32[4,64,1024]{2,1,0:T(8,128)} custom-call(s32[10]{0:T(128)S(1)} %pad_add_fusion.place, f32[2,64,64]{2,1,0:T(8,128)S(1)} %get-tuple-element.120.basis, f32[64,512]{1,0:T(8,128)S(1)} %solve.3.mine, f32[64,512]{1,0:T(8,128)S(1)} %collective-permute-done.51.other, bf16[512,1024]{1,0:T(8,128)(2,1)S(1)} %fusion.2.member, ...), custom_call_target="tpu_custom_call", output_to_operand_aliasing={{}: (5, {})} | custom-call | flops 402653184 | bytes 1048576 | tf_op jit(solution)/shard_map/expose/pallas_call | solution.py:152
  (152 shorter events, 29.5 us)
Async XLA Ops:
  1.5 4.6 %collective-permute-start = (bf16[128,2048]{1,0:T(8,128)(2,1)S(1)}, bf16[128,2048]{1,0:T(8,128)(2,1)S(1)}, u32[]{:S(2)}, u32[]{:S(2)}) collective-permute-start(bf16[128,2048]{1,0:T(8,128)(2,1)S(1)} %bitcast.187), channel_id=1, source_target_pairs={{0,4},{4,0},{8,12},{12,8},{16,20},{20,16},{24,28},{28,24},{1,5},{5... | collective-permute-start | bytes 1572872 | tf_op jit(solution)/shard_map/ppermute | solution.py:192
  2.0 26.5 %collective-permute-start.5 = (bf16[128,2048]{1,0:T(8,128)(2,1)S(1)}, bf16[128,2048]{1,0:T(8,128)(2,1)S(1)}, u32[]{:S(2)}, u32[]{:S(2)}) collective-permute-start(bf16[128,2048]{1,0:T(8,128)(2,1)S(1)} %bitcast.188), channel_id=1, source_target_pairs={{0,8},{4,12},{8,0},{12,4},{16,24},{20,28},{24,16},{28,20},{1,9},{5... | collective-permute-start | bytes 1572872 | tf_op jit(solution)/shard_map/ppermute | solution.py:192
  4.6 25.2 %collective-permute-start.6 = (bf16[128,2048]{1,0:T(8,128)(2,1)S(1)}, bf16[128,2048]{1,0:T(8,128)(2,1)S(1)}, u32[]{:S(2)}, u32[]{:S(2)}) collective-permute-start(bf16[128,2048]{1,0:T(8,128)(2,1)S(1)} %bitcast.189), channel_id=1, source_target_pairs={{0,16},{4,20},{8,24},{12,28},{16,0},{20,4},{24,8},{28,12},{1,17},{... | collective-permute-start | bytes 1572872 | tf_op jit(solution)/shard_map/ppermute | solution.py:192
  6.1 23.7 %collective-permute-start.7 = (bf16[128,2048]{1,0:T(8,128)(2,1)S(1)}, bf16[128,2048]{1,0:T(8,128)(2,1)}, u32[]{:S(2)}, u32[]{:S(2)}) collective-permute-start(bf16[128,2048]{1,0:T(8,128)(2,1)S(1)} %bitcast.190), channel_id=1, source_target_pairs={{0,24},{4,28},{8,16},{12,20},{16,8},{20,12},{24,0},{28,4},{1,25},{... | collective-permute-start | bytes 1572872 | tf_op jit(solution)/shard_map/ppermute | solution.py:192
  8.4 10.5 %collective-permute-start.1 = (f32[2,32,1024]{2,1,0:T(8,128)}, f32[2,32,1024]{2,1,0:T(8,128)S(1)}, u32[]{:S(2)}, u32[]{:S(2)}) collective-permute-start(f32[2,32,1024]{2,1,0:T(8,128)} %slice_bitcast_fusion.4), channel_id=1, source_target_pairs={{0,1},{1,2},{2,3},{3,0},{4,5},{5,6},{6,7},{7,4},{8,9},{9,10},{10,1... | collective-permute-start | bytes 786440 | tf_op jit(solution)/shard_map/ppermute | solution.py:195
  11.3 7.7 %collective-permute-start.3 = (f32[3072]{0:T(1024)S(1)}, f32[3072]{0:T(1024)S(1)}, u32[]{:S(2)}, u32[]{:S(2)}) collective-permute-start(f32[3072]{0:T(1024)S(1)} %pad_maximum_fusion.13), channel_id=1, source_target_pairs={{0,1},{1,0},{2,3},{3,2},{4,5},{5,4},{6,7},{7,6},{8,9},{9,8},{10,11... | collective-permute-start | bytes 36872 | tf_op jit(solution)/shard_map/ppermute | solution.py:253
  19.0 9.2 %collective-permute-start.2 = (f32[2,32,1024]{2,1,0:T(8,128)S(1)}, f32[2,32,1024]{2,1,0:T(8,128)S(1)}, u32[]{:S(2)}, u32[]{:S(2)}) collective-permute-start(f32[2,32,1024]{2,1,0:T(8,128)S(1)} %fusion.33), channel_id=1, source_target_pairs={{0,1},{1,2},{2,3},{3,0},{4,5},{5,6},{6,7},{7,4},{8,9},{9,10},{10,1... | collective-permute-start | bytes 786440 | tf_op jit(solution)/shard_map/ppermute | solution.py:195
  19.1 9.4 %collective-permute-start.8 = (f32[5120]{0:T(1024)S(1)}, f32[5120]{0:T(1024)S(1)}, u32[]{:S(2)}, u32[]{:S(2)}) collective-permute-start(f32[5120]{0:T(1024)S(1)} %pad_maximum_fusion.12), channel_id=1, source_target_pairs={{0,2},{1,3},{2,0},{3,1},{4,6},{5,7},{6,4},{7,5},{8,10},{9,11},{10,... | collective-permute-start | bytes 61448 | tf_op jit(solution)/shard_map/ppermute | solution.py:253
  28.2 9.1 %collective-permute-start.4 = (f32[2,32,1024]{2,1,0:T(8,128)S(1)}, f32[2,32,1024]{2,1,0:T(8,128)S(1)}, u32[]{:S(2)}, u32[]{:S(2)}) collective-permute-start(f32[2,32,1024]{2,1,0:T(8,128)S(1)} %fusion.34), channel_id=1, source_target_pairs={{0,1},{1,2},{2,3},{3,0},{4,5},{5,6},{6,7},{7,4},{8,9},{9,10},{10,1... | collective-permute-start | bytes 786440 | tf_op jit(solution)/shard_map/ppermute | solution.py:195
  31.1 7.9 %collective-permute-start.10 = (bf16[3,128,2048]{2,1,0:T(8,128)(2,1)S(1)}, bf16[3,128,2048]{2,1,0:T(8,128)(2,1)S(1)}, u32[]{:S(2)}, u32[]{:S(2)}) collective-permute-start(bf16[3,128,2048]{2,1,0:T(8,128)(2,1)S(1)} %pad_maximum_fusion.1), channel_id=1, source_target_pairs={{0,4},{4,0},{8,12},{12,8},{16,20},{20,16},{24,28},{28,24},{1,5},{5... | collective-permute-start | bytes 4718600 | tf_op jit(solution)/shard_map/ppermute | solution.py:192
  31.1 29.3 %collective-permute-start.14 = (bf16[128,2048]{1,0:T(8,128)(2,1)S(1)}, bf16[128,2048]{1,0:T(8,128)(2,1)S(1)}, u32[]{:S(2)}, u32[]{:S(2)}) collective-permute-start(bf16[128,2048]{1,0:T(8,128)(2,1)S(1)} %bitcast.192), channel_id=1, source_target_pairs={{0,8},{4,12},{8,0},{12,4},{16,24},{20,28},{24,16},{28,20},{1,9},{5... | collective-permute-start | bytes 1572872 | tf_op jit(solution)/shard_map/ppermute | solution.py:192
  32.5 27.9 %collective-permute-start.15 = (bf16[128,2048]{1,0:T(8,128)(2,1)S(1)}, bf16[128,2048]{1,0:T(8,128)(2,1)S(1)}, u32[]{:S(2)}, u32[]{:S(2)}) collective-permute-start(bf16[128,2048]{1,0:T(8,128)(2,1)S(1)} %bitcast.193), channel_id=1, source_target_pairs={{0,16},{4,20},{8,24},{12,28},{16,0},{20,4},{24,8},{28,12},{1,17},{... | collective-permute-start | bytes 1572872 | tf_op jit(solution)/shard_map/ppermute | solution.py:192
  33.3 27.2 %collective-permute-start.16 = (bf16[128,2048]{1,0:T(8,128)(2,1)S(1)}, bf16[128,2048]{1,0:T(8,128)(2,1)S(1)}, u32[]{:S(2)}, u32[]{:S(2)}) collective-permute-start(bf16[128,2048]{1,0:T(8,128)(2,1)S(1)} %bitcast.194), channel_id=1, source_target_pairs={{0,24},{4,28},{8,16},{12,20},{16,8},{20,12},{24,0},{28,4},{1,25},{... | collective-permute-start | bytes 1572872 | tf_op jit(solution)/shard_map/ppermute | solution.py:192
  37.3 9.2 %collective-permute-start.9 = (f16[3,32,1024]{2,1,0:T(8,128)(2,1)S(1)}, f16[3,32,1024]{2,1,0:T(8,128)(2,1)S(1)}, u32[]{:S(2)}, u32[]{:S(2)}) collective-permute-start(f16[3,32,1024]{2,1,0:T(8,128)(2,1)S(1)} %fusion.36), channel_id=1, source_target_pairs={{0,1},{1,2},{2,3},{3,0},{4,5},{5,6},{6,7},{7,4},{8,9},{9,10},{10,1... | collective-permute-start | bytes 589832 | tf_op jit(solution)/shard_map/ppermute | solution.py:195
  41.0 9.7 %collective-permute-start.12 = (f16[3,32,1024]{2,1,0:T(8,128)(2,1)S(1)}, f16[3,32,1024]{2,1,0:T(8,128)(2,1)S(1)}, u32[]{:S(2)}, u32[]{:S(2)}) collective-permute-start(f16[3,32,1024]{2,1,0:T(8,128)(2,1)S(1)} %fusion.37), channel_id=1, source_target_pairs={{0,1},{1,2},{2,3},{3,0},{4,5},{5,6},{6,7},{7,4},{8,9},{9,10},{10,1... | collective-permute-start | bytes 589832 | tf_op jit(solution)/shard_map/ppermute | solution.py:195
  46.5 7.9 %collective-permute-start.11 = (f16[3,32,1024]{2,1,0:T(8,128)(2,1)S(1)}, f16[3,32,1024]{2,1,0:T(8,128)(2,1)S(1)}, u32[]{:S(2)}, u32[]{:S(2)}) collective-permute-start(f16[3,32,1024]{2,1,0:T(8,128)(2,1)S(1)} %fusion.22), channel_id=1, source_target_pairs={{0,1},{1,2},{2,3},{3,0},{4,5},{5,6},{6,7},{7,4},{8,9},{9,10},{10,1... | collective-permute-start | bytes 589832 | tf_op jit(solution)/shard_map/ppermute | solution.py:195
  50.7 9.5 %collective-permute-start.17 = (f16[3,32,1024]{2,1,0:T(8,128)(2,1)S(1)}, f16[3,32,1024]{2,1,0:T(8,128)(2,1)S(1)}, u32[]{:S(2)}, u32[]{:S(2)}) collective-permute-start(f16[3,32,1024]{2,1,0:T(8,128)(2,1)S(1)} %fusion.16), channel_id=1, source_target_pairs={{0,1},{1,2},{2,3},{3,0},{4,5},{5,6},{6,7},{7,4},{8,9},{9,10},{10,1... | collective-permute-start | bytes 589832 | tf_op jit(solution)/shard_map/ppermute | solution.py:195
  54.5 10.0 %collective-permute-start.13 = (f16[3,32,1024]{2,1,0:T(8,128)(2,1)S(1)}, f16[3,32,1024]{2,1,0:T(8,128)(2,1)S(1)}, u32[]{:S(2)}, u32[]{:S(2)}) collective-permute-start(f16[3,32,1024]{2,1,0:T(8,128)(2,1)S(1)} %fusion.18), channel_id=1, source_target_pairs={{0,1},{1,2},{2,3},{3,0},{4,5},{5,6},{6,7},{7,4},{8,9},{9,10},{10,1... | collective-permute-start | bytes 589832 | tf_op jit(solution)/shard_map/ppermute | solution.py:195
  60.3 7.5 %collective-permute-start.19 = (f16[3,32,1024]{2,1,0:T(8,128)(2,1)S(1)}, f16[3,32,1024]{2,1,0:T(8,128)(2,1)S(1)}, u32[]{:S(2)}, u32[]{:S(2)}) collective-permute-start(f16[3,32,1024]{2,1,0:T(8,128)(2,1)S(1)} %fusion.14), channel_id=1, source_target_pairs={{0,1},{1,2},{2,3},{3,0},{4,5},{5,6},{6,7},{7,4},{8,9},{9,10},{10,1... | collective-permute-start | bytes 589832 | tf_op jit(solution)/shard_map/ppermute | solution.py:195
  60.7 13.7 %collective-permute-start.21 = (bf16[4,128,2048]{2,1,0:T(8,128)(2,1)S(1)}, bf16[4,128,2048]{2,1,0:T(8,128)(2,1)S(1)}, u32[]{:S(2)}, u32[]{:S(2)}) collective-permute-start(bf16[4,128,2048]{2,1,0:T(8,128)(2,1)S(1)} %pad_maximum_fusion), channel_id=1, source_target_pairs={{0,4},{4,0},{8,12},{12,8},{16,20},{20,16},{24,28},{28,24},{1,5},{5... | collective-permute-start | bytes 6291464 | tf_op jit(solution)/shard_map/ppermute | solution.py:192
  63.4 11.0 %collective-permute-start.18 = (f16[4,32,1024]{2,1,0:T(8,128)(2,1)S(1)}, f16[4,32,1024]{2,1,0:T(8,128)(2,1)S(1)}, u32[]{:S(2)}, u32[]{:S(2)}) collective-permute-start(f16[4,32,1024]{2,1,0:T(8,128)(2,1)S(1)} %fusion.25), channel_id=1, source_target_pairs={{0,1},{1,2},{2,3},{3,0},{4,5},{5,6},{6,7},{7,4},{8,9},{9,10},{10,1... | collective-permute-start | bytes 786440 | tf_op jit(solution)/shard_map/ppermute | solution.py:195
  68.1 9.4 %collective-permute-start.20 = (bf16[4,32,1024]{2,1,0:T(8,128)(2,1)S(1)}, bf16[4,32,1024]{2,1,0:T(8,128)(2,1)S(1)}, u32[]{:S(2)}, u32[]{:S(2)}) collective-permute-start(bf16[4,32,1024]{2,1,0:T(8,128)(2,1)S(1)} %bitcast.216), channel_id=1, source_target_pairs={{0,4},{4,0},{8,12},{12,8},{16,20},{20,16},{24,28},{28,24},{1,5},{5... | collective-permute-start | bytes 786440 | tf_op jit(solution)/shard_map/ppermute | solution.py:192
  76.9 11.0 %collective-permute-start.26 = (f16[4,32,1024]{2,1,0:T(8,128)(2,1)S(1)}, f16[4,32,1024]{2,1,0:T(8,128)(2,1)S(1)}, u32[]{:S(2)}, u32[]{:S(2)}) collective-permute-start(f16[4,32,1024]{2,1,0:T(8,128)(2,1)S(1)} %fusion.26), channel_id=1, source_target_pairs={{0,1},{1,2},{2,3},{3,0},{4,5},{5,6},{6,7},{7,4},{8,9},{9,10},{10,1... | collective-permute-start | bytes 786440 | tf_op jit(solution)/shard_map/ppermute | solution.py:195
  77.1 16.5 %collective-permute-start.22 = (f16[4,32,1024]{2,1,0:T(8,128)(2,1)S(1)}, f16[4,32,1024]{2,1,0:T(8,128)(2,1)S(1)}, u32[]{:S(2)}, u32[]{:S(2)}) collective-permute-start(f16[4,32,1024]{2,1,0:T(8,128)(2,1)S(1)} %fusion.12), channel_id=1, source_target_pairs={{0,1},{1,2},{2,3},{3,0},{4,5},{5,6},{6,7},{7,4},{8,9},{9,10},{10,1... | collective-permute-start | bytes 786440 | tf_op jit(solution)/shard_map/ppermute | solution.py:195
  77.6 10.6 %collective-permute-start.23 = (bf16[2,32,1024]{2,1,0:T(8,128)(2,1)S(1)}, bf16[2,32,1024]{2,1,0:T(8,128)(2,1)S(1)}, u32[]{:S(2)}, u32[]{:S(2)}) collective-permute-start(bf16[2,32,1024]{2,1,0:T(8,128)(2,1)S(1)} %get-tuple-element.168), channel_id=1, source_target_pairs={{0,8},{4,12},{8,0},{12,4},{16,24},{20,28},{24,16},{28,20},{1,9},{5... | collective-permute-start | bytes 393224 | tf_op jit(solution)/shard_map/ppermute | solution.py:192
  79.0 9.2 %collective-permute-start.24 = (bf16[2,32,1024]{2,1,0:T(8,128)(2,1)S(1)}, bf16[2,32,1024]{2,1,0:T(8,128)(2,1)S(1)}, u32[]{:S(2)}, u32[]{:S(2)}) collective-permute-start(bf16[2,32,1024]{2,1,0:T(8,128)(2,1)S(1)} %get-tuple-element.169), channel_id=1, source_target_pairs={{0,16},{4,20},{8,24},{12,28},{16,0},{20,4},{24,8},{28,12},{1,17},{... | collective-permute-start | bytes 393224 | tf_op jit(solution)/shard_map/ppermute | solution.py:192
  79.7 8.5 %collective-permute-start.25 = (bf16[2,32,1024]{2,1,0:T(8,128)(2,1)S(1)}, bf16[2,32,1024]{2,1,0:T(8,128)(2,1)S(1)}, u32[]{:S(2)}, u32[]{:S(2)}) collective-permute-start(bf16[2,32,1024]{2,1,0:T(8,128)(2,1)S(1)} %get-tuple-element.167), channel_id=1, source_target_pairs={{0,24},{4,28},{8,16},{12,20},{16,8},{20,12},{24,0},{28,4},{1,25},{... | collective-permute-start | bytes 393224 | tf_op jit(solution)/shard_map/ppermute | solution.py:192
  88.1 11.2 %collective-permute-start.28 = (f16[4,32,1024]{2,1,0:T(8,128)(2,1)S(1)}, f16[4,32,1024]{2,1,0:T(8,128)(2,1)S(1)}, u32[]{:S(2)}, u32[]{:S(2)}) collective-permute-start(f16[4,32,1024]{2,1,0:T(8,128)(2,1)S(1)} %fusion.6), channel_id=1, source_target_pairs={{0,1},{1,2},{2,3},{3,0},{4,5},{5,6},{6,7},{7,4},{8,9},{9,10},{10,1... | collective-permute-start | bytes 786440 | tf_op jit(solution)/shard_map/ppermute | solution.py:195
  93.7 11.2 %collective-permute-start.27 = (f16[4,32,1024]{2,1,0:T(8,128)(2,1)S(1)}, f16[4,32,1024]{2,1,0:T(8,128)(2,1)S(1)}, u32[]{:S(2)}, u32[]{:S(2)}) collective-permute-start(f16[4,32,1024]{2,1,0:T(8,128)(2,1)S(1)} %fusion.8), channel_id=1, source_target_pairs={{0,1},{1,2},{2,3},{3,0},{4,5},{5,6},{6,7},{7,4},{8,9},{9,10},{10,1... | collective-permute-start | bytes 786440 | tf_op jit(solution)/shard_map/ppermute | solution.py:195
  99.3 11.2 %collective-permute-start.29 = (f16[4,32,1024]{2,1,0:T(8,128)(2,1)S(1)}, f16[4,32,1024]{2,1,0:T(8,128)(2,1)S(1)}, u32[]{:S(2)}, u32[]{:S(2)}) collective-permute-start(f16[4,32,1024]{2,1,0:T(8,128)(2,1)S(1)} %fusion.4), channel_id=1, source_target_pairs={{0,1},{1,2},{2,3},{3,0},{4,5},{5,6},{6,7},{7,4},{8,9},{9,10},{10,1... | collective-permute-start | bytes 786440 | tf_op jit(solution)/shard_map/ppermute | solution.py:195
  99.4 21.2 %collective-permute-start.31 = (bf16[8,32,1024]{2,1,0:T(8,128)(2,1)S(1)}, bf16[8,32,1024]{2,1,0:T(8,128)(2,1)S(1)}, u32[]{:S(2)}, u32[]{:S(2)}) collective-permute-start(bf16[8,32,1024]{2,1,0:T(8,128)(2,1)S(1)} %constant_dynamic-update-slice_fusion.refs_0_), channel_id=1, source_target_pairs={{0,1},{1,2},{2,3},{3,0},{4,5},{5,6},{6,7},{7,4},{8,9},{9,10},{10,1... | collective-permute-start | bytes 1572872 | tf_op jit(solution)/shard_map/ppermute | solution.py:195
  120.6 14.6 %collective-permute-start.35 = (bf16[8,32,1024]{2,1,0:T(8,128)(2,1)S(1)}, bf16[8,32,1024]{2,1,0:T(8,128)(2,1)S(1)}, u32[]{:S(2)}, u32[]{:S(2)}) collective-permute-start(bf16[8,32,1024]{2,1,0:T(8,128)(2,1)S(1)} %collective-permute-done.31.refs_1_), channel_id=1, source_target_pairs={{0,1},{1,2},{2,3},{3,0},{4,5},{5,6},{6,7},{7,4},{8,9},{9,10},{10,1... | collective-permute-start | bytes 1572872 | tf_op jit(solution)/shard_map/ppermute | solution.py:195
  122.2 13.1 %collective-permute-start.32 = (bf16[2,32,1024]{2,1,0:T(8,128)(2,1)S(1)}, bf16[2,32,1024]{2,1,0:T(8,128)(2,1)S(1)}, u32[]{:S(2)}, u32[]{:S(2)}) collective-permute-start(bf16[2,32,1024]{2,1,0:T(8,128)(2,1)S(1)} %get-tuple-element.164), channel_id=1, source_target_pairs={{0,8},{4,12},{8,0},{12,4},{16,24},{20,28},{24,16},{28,20},{1,9},{5... | collective-permute-start | bytes 393224 | tf_op jit(solution)/shard_map/ppermute | solution.py:192
  123.6 11.7 %collective-permute-start.33 = (bf16[2,32,1024]{2,1,0:T(8,128)(2,1)S(1)}, bf16[2,32,1024]{2,1,0:T(8,128)(2,1)S(1)}, u32[]{:S(2)}, u32[]{:S(2)}) collective-permute-start(bf16[2,32,1024]{2,1,0:T(8,128)(2,1)S(1)} %get-tuple-element.165), channel_id=1, source_target_pairs={{0,16},{4,20},{8,24},{12,28},{16,0},{20,4},{24,8},{28,12},{1,17},{... | collective-permute-start | bytes 393224 | tf_op jit(solution)/shard_map/ppermute | solution.py:192
  124.3 11.0 %collective-permute-start.34 = (bf16[2,32,1024]{2,1,0:T(8,128)(2,1)S(1)}, bf16[2,32,1024]{2,1,0:T(8,128)(2,1)S(1)}, u32[]{:S(2)}, u32[]{:S(2)}) collective-permute-start(bf16[2,32,1024]{2,1,0:T(8,128)(2,1)S(1)} %get-tuple-element.163), channel_id=1, source_target_pairs={{0,24},{4,28},{8,16},{12,20},{16,8},{20,12},{24,0},{28,4},{1,25},{... | collective-permute-start | bytes 393224 | tf_op jit(solution)/shard_map/ppermute | solution.py:192
  135.2 16.7 %collective-permute-start.37 = (bf16[8,32,1024]{2,1,0:T(8,128)(2,1)S(1)}, bf16[8,32,1024]{2,1,0:T(8,128)(2,1)S(1)}, u32[]{:S(2)}, u32[]{:S(2)}) collective-permute-start(bf16[8,32,1024]{2,1,0:T(8,128)(2,1)S(1)} %collective-permute-done.35.refs_2_), channel_id=1, source_target_pairs={{0,1},{1,2},{2,3},{3,0},{4,5},{5,6},{6,7},{7,4},{8,9},{9,10},{10,1... | collective-permute-start | bytes 1572872 | tf_op jit(solution)/shard_map/ppermute | solution.py:195
  135.3 24.9 %collective-permute-start.36 = (bf16[8,32,1024]{2,1,0:T(8,128)(2,1)S(1)}, bf16[8,32,1024]{2,1,0:T(8,128)(2,1)S(1)}, u32[]{:S(2)}, u32[]{:S(2)}) collective-permute-start(bf16[8,32,1024]{2,1,0:T(8,128)(2,1)S(1)} %constant_dynamic-update-slice_fusion.4.refs_0_), channel_id=1, source_target_pairs={{0,1},{1,2},{2,3},{3,0},{4,5},{5,6},{6,7},{7,4},{8,9},{9,10},{10,1... | collective-permute-start | bytes 1572872 | tf_op jit(solution)/shard_map/ppermute | solution.py:195
  160.2 12.8 %collective-permute-start.38 = (bf16[8,32,1024]{2,1,0:T(8,128)(2,1)S(1)}, bf16[8,32,1024]{2,1,0:T(8,128)(2,1)S(1)}, u32[]{:S(2)}, u32[]{:S(2)}) collective-permute-start(bf16[8,32,1024]{2,1,0:T(8,128)(2,1)S(1)} %collective-permute-done.36.refs_1_), channel_id=1, source_target_pairs={{0,1},{1,2},{2,3},{3,0},{4,5},{5,6},{6,7},{7,4},{8,9},{9,10},{10,1... | collective-permute-start | bytes 1572872 | tf_op jit(solution)/shard_map/ppermute | solution.py:195
  173.0 11.9 %collective-permute-start.40 = (bf16[8,32,1024]{2,1,0:T(8,128)(2,1)S(1)}, bf16[8,32,1024]{2,1,0:T(8,128)(2,1)S(1)}, u32[]{:S(2)}, u32[]{:S(2)}) collective-permute-start(bf16[8,32,1024]{2,1,0:T(8,128)(2,1)S(1)} %collective-permute-done.38.refs_2_), channel_id=1, source_target_pairs={{0,1},{1,2},{2,3},{3,0},{4,5},{5,6},{6,7},{7,4},{8,9},{9,10},{10,1... | collective-permute-start | bytes 1572872 | tf_op jit(solution)/shard_map/ppermute | solution.py:195
  173.0 4.5 %collective-permute-start.41 = (f32[32,640]{1,0:T(8,128)S(1)}, f32[32,640]{1,0:T(8,128)S(1)}, u32[]{:S(2)}, u32[]{:S(2)}) collective-permute-start(f32[32,640]{1,0:T(8,128)S(1)} %get-tuple-element.180), channel_id=1, source_target_pairs={{0,8},{4,12},{8,0},{12,4},{16,24},{20,28},{24,16},{28,20},{1,9},{5... | collective-permute-start | bytes 245768 | tf_op jit(solution)/shard_map/ppermute | solution.py:192
  174.4 4.4 %collective-permute-start.42 = (f32[32,640]{1,0:T(8,128)S(1)}, f32[32,640]{1,0:T(8,128)S(1)}, u32[]{:S(2)}, u32[]{:S(2)}) collective-permute-start(f32[32,640]{1,0:T(8,128)S(1)} %get-tuple-element.179), channel_id=1, source_target_pairs={{0,16},{4,20},{8,24},{12,28},{16,0},{20,4},{24,8},{28,12},{1,17},{... | collective-permute-start | bytes 245768 | tf_op jit(solution)/shard_map/ppermute | solution.py:192
  191.7 4.9 %collective-permute-start.46 = (f32[32,640]{1,0:T(8,128)S(1)}, f32[32,640]{1,0:T(8,128)S(1)}, u32[]{:S(2)}, u32[]{:S(2)}) collective-permute-start(f32[32,640]{1,0:T(8,128)S(1)} %get-tuple-element.178.first_top), channel_id=1, source_target_pairs={{0,16},{4,20},{8,24},{12,28},{16,0},{20,4},{24,8},{28,12},{1,17},{... | collective-permute-start | bytes 245768 | tf_op jit(solution)/shard_map/ppermute | solution.py:192
  193.3 5.3 %collective-permute-start.47 = (f32[32,640]{1,0:T(8,128)S(1)}, f32[32,640]{1,0:T(8,128)S(1)}, u32[]{:S(2)}, u32[]{:S(2)}) collective-permute-start(f32[32,640]{1,0:T(8,128)S(1)} %get-tuple-element.177.first_bottom), channel_id=1, source_target_pairs={{0,8},{4,12},{8,0},{12,4},{16,24},{20,28},{24,16},{28,20},{1,9},{5... | collective-permute-start | bytes 245768 | tf_op jit(solution)/shard_map/ppermute | solution.py:192
  193.8 8.2 %collective-permute-start.44 = (f32[32,640]{1,0:T(8,128)S(1)}, f32[32,640]{1,0:T(8,128)S(1)}, u32[]{:S(2)}, u32[]{:S(2)}) collective-permute-start(f32[32,640]{1,0:T(8,128)S(1)} %get-tuple-element.176), channel_id=1, source_target_pairs={{0,8},{4,12},{8,0},{12,4},{16,24},{20,28},{24,16},{28,20},{1,9},{5... | collective-permute-start | bytes 245768 | tf_op jit(solution)/shard_map/ppermute | solution.py:192
  195.4 6.6 %collective-permute-start.45 = (f32[32,640]{1,0:T(8,128)S(1)}, f32[32,640]{1,0:T(8,128)S(1)}, u32[]{:S(2)}, u32[]{:S(2)}) collective-permute-start(f32[32,640]{1,0:T(8,128)S(1)} %get-tuple-element.175), channel_id=1, source_target_pairs={{0,16},{4,20},{8,24},{12,28},{16,0},{20,4},{24,8},{28,12},{1,17},{... | collective-permute-start | bytes 245768 | tf_op jit(solution)/shard_map/ppermute | solution.py:192
  201.9 2.3 %collective-permute-start.50 = (f32[64,512]{1,0:T(8,128)S(1)}, f32[64,512]{1,0:T(8,128)S(1)}, u32[]{:S(2)}, u32[]{:S(2)}) collective-permute-start(f32[64,512]{1,0:T(8,128)S(1)} %solve.2.mine), channel_id=1, source_target_pairs={{0,4},{4,0},{8,12},{12,8},{16,20},{20,16},{24,28},{28,24},{1,5},{5... | collective-permute-start | bytes 393224 | tf_op jit(solution)/shard_map/ppermute | solution.py:192
  202.0 4.9 %collective-permute-start.48 = (f32[32,640]{1,0:T(8,128)S(1)}, f32[32,640]{1,0:T(8,128)S(1)}, u32[]{:S(2)}, u32[]{:S(2)}) collective-permute-start(f32[32,640]{1,0:T(8,128)S(1)} %get-tuple-element.174.first_top), channel_id=1, source_target_pairs={{0,16},{4,20},{8,24},{12,28},{16,0},{20,4},{24,8},{28,12},{1,17},{... | collective-permute-start | bytes 245768 | tf_op jit(solution)/shard_map/ppermute | solution.py:192
  202.4 4.6 %collective-permute-start.49 = (f32[32,640]{1,0:T(8,128)S(1)}, f32[32,640]{1,0:T(8,128)S(1)}, u32[]{:S(2)}, u32[]{:S(2)}) collective-permute-start(f32[32,640]{1,0:T(8,128)S(1)} %get-tuple-element.173.first_bottom), channel_id=1, source_target_pairs={{0,8},{4,12},{8,0},{12,4},{16,24},{20,28},{24,16},{28,20},{1,9},{5... | collective-permute-start | bytes 245768 | tf_op jit(solution)/shard_map/ppermute | solution.py:192
  (12 other events, 53.2 us)

commit v2 on v1

--- a/solution.py
+++ b/solution.py
@@ -20,20 +20,31 @@
     return lax.dot_general(a, b, dims, precision=precision, preferred_element_type=jnp.float32)
 
 
-def price_kernel(place, *refs):
-    trade, basis_load, kept, given, ordered = refs[-5:]
-    pieces = refs[:-5]
-    fac_size = len(pieces)
+def accumulate(place, pieces, trade, basis_load):
+    fac_parts = len(pieces)
     blocks, rows, _ = pieces[0].shape
-    drivers = jnp.zeros((fac_size * rows, trade.shape[2]), jnp.float32)
-    projected = jnp.zeros((fac_size * rows, basis_load.shape[1]), jnp.float32)
+    drivers = jnp.zeros((fac_parts * rows, trade.shape[2]), jnp.float32)
+    projected = jnp.zeros((fac_parts * rows, basis_load.shape[1]), jnp.float32)
     for n in range(blocks):
         levels = jnp.concatenate([piece[n] for piece in pieces], axis=0)
         factors = place[2 + n]
         drivers += jnp.dot(levels, trade[factors], preferred_element_type=jnp.float32)
         projected += dot(levels, basis_load[factors], CONTRACT_LAST)
+    return drivers, projected
+
+
+def start_price_kernel(place, *refs):
+    trade, basis_load, drivers, projected = refs[-4:]
+    drivers[...], projected[...] = accumulate(place, refs[:-4], trade, basis_load)
+
+
+def price_kernel(place, piece, trade, basis_load, drivers, projected, kept, given, ordered):
+    rows = piece.shape[1]
+    fac_size = drivers.shape[0] // rows + 1
+    last_drivers, last_projected = accumulate(place, [piece], trade, basis_load)
+    drivers = jnp.concatenate([drivers[...], last_drivers], axis=0)
     values = jnp.maximum(drivers, 0.0) + jnp.log1p(jnp.exp(-jnp.abs(drivers))) - 1.0
-    basis = jnp.tanh(projected)
+    basis = jnp.tanh(jnp.concatenate([projected[...], last_projected], axis=0))
     steps, paths, basis_count = ordered.shape
     share = paths // fac_size
     fac_index, core = place[0], place[1]
@@ -55,25 +66,47 @@
     given[...] = jnp.where(core == 0, sums[1], sums[0])
 
 
-def price(pieces, trade_blocks, basis_blocks, place, steps, paths):
-    fac_size = len(pieces)
+def start_price(pieces, trade_blocks, basis_blocks, place):
     blocks, rows, width = pieces[0].shape
+    rows = len(pieces) * rows
+    trades, basis_count = trade_blocks.shape[2], basis_blocks.shape[1]
+    vmem = pl.BlockSpec(memory_space=pltpu.VMEM)
+    return pl.pallas_call(
+        start_price_kernel,
+        in_specs=[pl.BlockSpec(memory_space=pltpu.SMEM)] + [vmem] * (len(pieces) + 2),
+        out_specs=[vmem] * 2,
+        out_shape=[
+            jax.ShapeDtypeStruct((rows, trades), jnp.float32),
+            jax.ShapeDtypeStruct((rows, basis_count), jnp.float32),
+        ],
+        compiler_params=pltpu.CompilerParams(vmem_limit_bytes=VMEM_LIMIT),
+        cost_estimate=pl.CostEstimate(
+            flops=2 * rows * blocks * width * (trades + basis_count),
+            bytes_accessed=2 * blocks * width * (trades + rows),
+            transcendentals=0,
+        ),
+        name="start_price",
+    )(place, *pieces, trade_blocks, basis_blocks)
+
+
+def price(piece, trade_blocks, basis_blocks, started, place, steps, paths):
+    blocks, rows, width = piece.shape
     trades, basis_count = trade_blocks.shape[2], basis_blocks.shape[1]
     sums = jax.ShapeDtypeStruct((basis_count, trades + 2 * basis_count), jnp.float32)
     vmem = pl.BlockSpec(memory_space=pltpu.VMEM)
     return pl.pallas_call(
         price_kernel,
-        in_specs=[pl.BlockSpec(memory_space=pltpu.SMEM)] + [vmem] * (fac_size + 2),
+        in_specs=[pl.BlockSpec(memory_space=pltpu.SMEM)] + [vmem] * 5,
         out_specs=[vmem] * 3,
         out_shape=[sums, sums, jax.ShapeDtypeStruct((steps, paths, basis_count), jnp.float32)],
         compiler_params=pltpu.CompilerParams(vmem_limit_bytes=VMEM_LIMIT),
         cost_estimate=pl.CostEstimate(
-            flops=2 * fac_size * rows * blocks * width * (trades + basis_count),
-            bytes_accessed=2 * blocks * width * (trades + fac_size * rows),
-            transcendentals=2 * fac_size * rows * trades,
+            flops=2 * rows * blocks * width * (trades + basis_count),
+            bytes_accessed=2 * blocks * width * (trades + rows),
+            transcendentals=2 * steps * paths * trades,
         ),
         name="price",
-    )(place, *pieces, trade_blocks, basis_blocks)
+    )(place, piece, trade_blocks, basis_blocks, *started)
 
 
 def solve_kernel(ridge, first_top, first_bottom, second_top, second_bottom, coef):
@@ -226,7 +259,7 @@
         pieces = [mark(piece)]
         for _ in range(fac_size - 1):
             pieces.append(pass_on(pieces[-1]))
-            yield None
+            yield pieces[:-1]
             pieces[-1] = mark(gate(pieces[-1]))
         yield pieces
 
@@ -289,8 +322,15 @@
         yield None
         yield jnp.concatenate(gate(*pairs), axis=0)
 
-    def priced(pieces):
-        kept, given, basis = price(pieces, trade_blocks, basis_blocks, place, half_steps, path_count)
+    def started(pieces):
+        sums = start_price(gate(*pieces), trade_blocks, basis_blocks, place)
+        mark(*sums)
+        return sums
+
+    def priced(pieces, sums):
+        kept, given, basis = price(
+            pieces[-1], trade_blocks, basis_blocks, sums, place, half_steps, path_count
+        )
         mark(given)
         return kept, given, basis
 
@@ -316,10 +356,10 @@
         next(chain_a)
     rest = mark(jnp.stack(gate(*received)))
     arrived = exchange(rest, 1)
+    chain_b = reduce_over_fac(rest, shrink, jnp.float16)
+    next(chain_b)
     own = gate(ordered[1])
     received = [exchange(own, k) for k in even]
-    chain_b = reduce_over_fac(rest, shrink, jnp.float16)
-    next(chain_b)
     near_sum = next(chain_a)
     chain_c = reduce_over_fac(arrived, shrink, jnp.float16)
     next(chain_c)
@@ -336,9 +376,9 @@
     others, other_carry = levels_of(others, 0.0)
     first = regroup(mine, others)
     next(first)
+    next(first)
     chain_e = reduce_over_fac(arrived, shrink, jnp.float16)
     next(chain_e)
-    next(first)
     next(chain_d)
     next(chain_e)
     ring_first = gather_over_fac(next(first))
@@ -346,31 +386,29 @@
     for hop in range(2, fac_size - 1):
         next(chain_d)
         next(chain_e)
-    mine, _ = levels_of(next(chain_d) * peak, carry)
-    others, _ = levels_of(next(chain_e) * peak, other_carry)
+    mine, others = next(chain_d) * peak, next(chain_e) * peak
+    others, _ = levels_of(others, other_carry)
+    mine, _ = levels_of(mine, carry)
     second = regroup(mine, others)
     next(second)
+    next(second)
     next(ring_first)
-    next(second)
-    for hop in range(2, fac_size - 1):
-        next(ring_first)
     ring_second = gather_over_fac(next(second))
     next(ring_second)
-    first = finish(*priced(next(ring_first)), 0)
+    for hop in range(2, fac_size - 1):
+        pieces = next(ring_first)
+        next(ring_second)
+    head = started(pieces)
+    first = finish(*priced(next(ring_first), head), 0)
     next(first)
-    to_do = len(bits)
-    for hop in range(1, fac_size - 1):
-        next(ring_second)
-        if to_do > 0:
-            next(first)
-            to_do -= 1
-    for _ in range(to_do):
+    next(first)
+    pieces = next(ring_second)
+    for _ in bits[1:]:
         next(first)
-    second = finish(*priced(next(ring_second)), 1)
-    next(second)
-    next(second)
+    head = started(pieces)
     next(first)
-    for _ in range(len(bits) - 1):
+    second = finish(*priced(next(ring_second), head), 1)
+    for _ in range(len(bits) + 1):
         next(second)
     result = next(first)
     next(second)

time: 214 us -> 204 us (0.953)
  waiting for transfers between devices: 135 us -> 123 us
  Pallas kernels: 17.9 us -> 22.8 us
  local copies, waits for them, and re-layouts: 11.4 us -> 7.49 us
    ppermute x21, waiting for transfers between devices: 122 us -> 103 us  [pass_on(): lax.ppermute(x, 'fac', [(i, (i + hops) % fac_size) for i in range(fac_siz...]
    ppermute x29, waiting for transfers between devices: 12.5 us -> 19.1 us  [exchange(): return lax.ppermute(x, 'path', [(i, i ^ k) for i in range(path_size)])]
    pallas_call x0 -> x2, Pallas kernels: none -> 4.61 us  [start_price(): pl.pallas_call(start_price_kernel, in_specs=[pl.BlockSpec(memory_space=pl...]
    unnamed x20 -> x22, local copies, waits for them, and re-layouts: 6.85 us -> 3.48 us
  transfers between devices with their start and end apart: 52 -> 52, of which waited for: 31 -> 34; matrix products, arithmetic and copies ran while one was open for 8% -> 8% of each run, Pallas kernels for 4% -> 7%
where the time goes in v2:
time: 204 us
  waiting for transfers between devices  123 us (60%)
  starting transfers between devices  35.7 us (18%)
  Pallas kernels  22.8 us (11%)
  matrix products  9.77 us (5%)
  local copies, waits for them, and re-layouts  7.49 us (4%)
  other arithmetic  4.65 us (2%)
    ppermute x21, waiting for transfers between devices, pass_on(): lax.ppermute(x, 'fac', [(i, (i + hops) % fac_size) for i in range(fac_siz...  103 us
    ppermute x29, starting transfers between devices, exchange(): return lax.ppermute(x, 'path', [(i, i ^ k) for i in range(path_size)])  24.5 us
    ppermute x29, waiting for transfers between devices, exchange(): return lax.ppermute(x, 'path', [(i, i ^ k) for i in range(path_size)])  19.1 us
    dot_general x5, matrix products, dot(): lax.dot_general(a, b, dims, precision=precision, preferred_element_type=j...  9.77 us
    ppermute x21, starting transfers between devices, pass_on(): lax.ppermute(x, 'fac', [(i, (i + hops) % fac_size) for i in range(fac_siz...  7.29 us
    pallas_call x2, Pallas kernels, price(): pl.pallas_call(price_kernel, in_specs=[pl.BlockSpec(memory_space=pltpu.SM...  7.02 us
    pallas_call x2, Pallas kernels, solve(): pl.pallas_call(functools.partial(solve_kernel, ridge), out_shape=jax.Shap...  6.72 us
    pallas_call x2, Pallas kernels, start_price(): pl.pallas_call(start_price_kernel, in_specs=[pl.BlockSpec(memory_space=pl...  4.61 us
  transfers between devices with their start and end apart: 52, of which 34 were waited for; matrix products, arithmetic and copies ran while one was open for 8% of the time, Pallas kernels for 7%

profile of v2, /device:TPU:0, one launch (start us, length us, event | category | flops | bytes accessed | tf_op | source)
XLA Modules:
  0.0 204.0 jit_solution(5884201794289392667)
XLA Ops:
  2.0 2.6 %collective-permute-start.5 = (bf16[128,2048]{1,0:T(8,128)(2,1)S(1)}, bf16[128,2048]{1,0:T(8,128)(2,1)S(1)}, u32[]{:S(2)}, u32[]{:S(2)}) collective-permute-start(bf16[128,2048]{1,0:T(8,128)(2,1)S(1)} %bitcast.194), channel_id=1, source_target_pairs={{0,8},{4,12},{8,0},{12,4},{16,24},{20,28},{24,16},{28,20},{1,9},{5... | collective-permute-start | bytes 1572872 | tf_op jit(solution)/shard_map/ppermute | solution.py:225
  4.6 1.5 collective-permute-start.6
  6.3 1.4 fusion
  8.4 2.0 collective-permute-start.1
  11.3 1.6 collective-permute-start.3
  13.0 5.9 %collective-permute-done.1 = f32[2,32,1024]{2,1,0:T(8,128)S(1)} collective-permute-done((f32[2,32,1024]{2,1,0:T(8,128)}, f32[2,32,1024]{2,1,0:T(8,128)S(1)}, u32[]{:S(2)}, u32[]{:S(2)}) %collective-permute-start.1) | collective-permute-done | bytes 262176 | tf_op jit(solution)/shard_map/ppermute | solution.py:228
  19.1 2.3 %collective-permute-start.8 = (f32[5120]{0:T(1024)S(1)}, f32[5120]{0:T(1024)S(1)}, u32[]{:S(2)}, u32[]{:S(2)}) collective-permute-start(f32[5120]{0:T(1024)S(1)} %pad_maximum_fusion.12), channel_id=1, source_target_pairs={{0,2},{1,3},{2,0},{3,1},{4,6},{5,7},{6,4},{7,5},{8,10},{9,11},{10,... | collective-permute-start | bytes 61448 | tf_op jit(solution)/shard_map/ppermute | solution.py:286
  21.4 6.8 %collective-permute-done.2 = f32[2,32,1024]{2,1,0:T(8,128)S(1)} collective-permute-done((f32[2,32,1024]{2,1,0:T(8,128)S(1)}, f32[2,32,1024]{2,1,0:T(8,128)S(1)}, u32[]{:S(2)}, u32[]{:S(2)}) %collective-permute-start.2) | collective-permute-done | bytes 262176 | tf_op jit(solution)/shard_map/ppermute | solution.py:228
  31.1 1.8 convolution_multiply_fusion.3
  33.2 1.6 collective-permute-start.9
  36.9 1.8 collective-permute-start.16
  38.7 1.8 convolution_multiply_fusion.2
  43.7 6.5 %collective-permute-done.12 = f16[3,32,1024]{2,1,0:T(8,128)(2,1)S(1)} collective-permute-done((f16[3,32,1024]{2,1,0:T(8,128)(2,1)S(1)}, f16[3,32,1024]{2,1,0:T(8,128)(2,1)S(1)}, u32[]{:S(2)}, u32[]{:S(2)}) %collective-permute-start.12) | collective-permute-done | bytes 196640 | tf_op jit(solution)/shard_map/ppermute | solution.py:228
  50.3 3.8 %collective-permute-done.11 = f16[3,32,1024]{2,1,0:T(8,128)(2,1)S(1)} collective-permute-done((f16[3,32,1024]{2,1,0:T(8,128)(2,1)S(1)}, f16[3,32,1024]{2,1,0:T(8,128)(2,1)S(1)}, u32[]{:S(2)}, u32[]{:S(2)}) %collective-permute-start.11) | collective-permute-done | bytes 196640 | tf_op jit(solution)/shard_map/ppermute | solution.py:228
  54.2 5.7 %collective-permute-done.17 = f16[3,32,1024]{2,1,0:T(8,128)(2,1)S(1)} collective-permute-done((f16[3,32,1024]{2,1,0:T(8,128)(2,1)S(1)}, f16[3,32,1024]{2,1,0:T(8,128)(2,1)S(1)}, u32[]{:S(2)}, u32[]{:S(2)}) %collective-permute-start.17) | collective-permute-done | bytes 196640 | tf_op jit(solution)/shard_map/ppermute | solution.py:228
  61.5 2.4 %convolution_multiply_fusion.1 = f32[512,1024]{1,0:T(8,128)S(1)} fusion(bf16[512,2048]{1,0:T(8,128)(2,1)S(1)} %bitcast.190, bf16[1024,2048]{1,0:T(8,128)(2,1)S(1)} %copy-done.2, f32[1024]{0:T(1024)S(1)} %get-tuple-element.157), kind=kOutput, calls=%fused_computation.7 | convolution fusion | flops 2148007936 | bytes 8392704 | tf_op jit(solution)/shard_map/dot_general | solution.py:20
  64.1 3.4 %collective-permute-done.20 = f16[3,32,1024]{2,1,0:T(8,128)(2,1)S(1)} collective-permute-done((f16[3,32,1024]{2,1,0:T(8,128)(2,1)S(1)}, f16[3,32,1024]{2,1,0:T(8,128)(2,1)S(1)}, u32[]{:S(2)}, u32[]{:S(2)}) %collective-permute-start.20) | collective-permute-done | bytes 196640 | tf_op jit(solution)/shard_map/ppermute | solution.py:228
  69.4 2.4 %convolution_multiply_fusion = f32[512,1024]{1,0:T(8,128)S(1)} fusion(bf16[512,2048]{1,0:T(8,128)(2,1)S(1)} %bitcast.226, bf16[1024,2048]{1,0:T(8,128)(2,1)S(1)} %copy-done.2, f32[1024]{0:T(1024)S(1)} %get-tuple-element.157), kind=kOutput, calls=%fused_computation.6 | convolution fusion | flops 2148007936 | bytes 8392704 | tf_op jit(solution)/shard_map/dot_general | solution.py:20
  74.1 1.6 collective-permute-start.25
  75.6 3.4 %collective-permute-done.18 = f16[4,32,1024]{2,1,0:T(8,128)(2,1)S(1)} collective-permute-done((f16[4,32,1024]{2,1,0:T(8,128)(2,1)S(1)}, f16[4,32,1024]{2,1,0:T(8,128)(2,1)S(1)}, u32[]{:S(2)}, u32[]{:S(2)}) %collective-permute-start.18) | collective-permute-done | bytes 262176 | tf_op jit(solution)/shard_map/ppermute | solution.py:228
  79.2 5.5 %collective-permute-done.26 = f16[4,32,1024]{2,1,0:T(8,128)(2,1)S(1)} collective-permute-done((f16[4,32,1024]{2,1,0:T(8,128)(2,1)S(1)}, f16[4,32,1024]{2,1,0:T(8,128)(2,1)S(1)}, u32[]{:S(2)}, u32[]{:S(2)}) %collective-permute-start.26) | collective-permute-done | bytes 262176 | tf_op jit(solution)/shard_map/ppermute | solution.py:228
  84.9 5.4 %collective-permute-done.22 = f16[4,32,1024]{2,1,0:T(8,128)(2,1)S(1)} collective-permute-done((f16[4,32,1024]{2,1,0:T(8,128)(2,1)S(1)}, f16[4,32,1024]{2,1,0:T(8,128)(2,1)S(1)}, u32[]{:S(2)}, u32[]{:S(2)}) %collective-permute-start.22) | collective-permute-done | bytes 262176 | tf_op jit(solution)/shard_map/ppermute | solution.py:228
  90.4 5.5 %collective-permute-done.28 = f16[4,32,1024]{2,1,0:T(8,128)(2,1)S(1)} collective-permute-done((f16[4,32,1024]{2,1,0:T(8,128)(2,1)S(1)}, f16[4,32,1024]{2,1,0:T(8,128)(2,1)S(1)}, u32[]{:S(2)}, u32[]{:S(2)}) %collective-permute-start.28) | collective-permute-done | bytes 262176 | tf_op jit(solution)/shard_map/ppermute | solution.py:228
  96.1 5.4 %collective-permute-done.27 = f16[4,32,1024]{2,1,0:T(8,128)(2,1)S(1)} collective-permute-done((f16[4,32,1024]{2,1,0:T(8,128)(2,1)S(1)}, f16[4,32,1024]{2,1,0:T(8,128)(2,1)S(1)}, u32[]{:S(2)}, u32[]{:S(2)}) %collective-permute-start.27) | collective-permute-done | bytes 262176 | tf_op jit(solution)/shard_map/ppermute | solution.py:228
  101.6 5.5 %collective-permute-done.29 = f16[4,32,1024]{2,1,0:T(8,128)(2,1)S(1)} collective-permute-done((f16[4,32,1024]{2,1,0:T(8,128)(2,1)S(1)}, f16[4,32,1024]{2,1,0:T(8,128)(2,1)S(1)}, u32[]{:S(2)}, u32[]{:S(2)}) %collective-permute-start.29) | collective-permute-done | bytes 262176 | tf_op jit(solution)/shard_map/ppermute | solution.py:228
  107.6 1.5 collective-permute-done.30
  111.1 1.6 collective-permute-start.33
  112.7 5.0 %collective-permute-done.34.refs_1_ = bf16[8,32,1024]{2,1,0:T(8,128)(2,1)S(1)} collective-permute-done((bf16[8,32,1024]{2,1,0:T(8,128)(2,1)S(1)}, bf16[8,32,1024]{2,1,0:T(8,128)(2,1)S(1)}, u32[]{:S(2)}, u32[]{:S(2)}) %collective-permute-start.34) | collective-permute-done | bytes 524320 | tf_op jit(solution)/shard_map/ppermute | solution.py:228
  118.6 15.7 %collective-permute-done.36.refs_2_ = bf16[8,32,1024]{2,1,0:T(8,128)(2,1)S(1)} collective-permute-done((bf16[8,32,1024]{2,1,0:T(8,128)(2,1)S(1)}, bf16[8,32,1024]{2,1,0:T(8,128)(2,1)S(1)}, u32[]{:S(2)}, u32[]{:S(2)}) %collective-permute-start.36) | collective-permute-done | bytes 524320 | tf_op jit(solution)/shard_map/ppermute | solution.py:228
  134.3 11.2 %collective-permute-done.35.refs_1_ = bf16[8,32,1024]{2,1,0:T(8,128)(2,1)S(1)} collective-permute-done((bf16[8,32,1024]{2,1,0:T(8,128)(2,1)S(1)}, bf16[8,32,1024]{2,1,0:T(8,128)(2,1)S(1)}, u32[]{:S(2)}, u32[]{:S(2)}) %collective-permute-start.35) | collective-permute-done | bytes 524320 | tf_op jit(solution)/shard_map/ppermute | solution.py:228
  147.0 3.4 %copy-done = bf16[8192,512]{1,0:T(8,128)(2,1)S(1)} copy-done((bf16[8192,512]{1,0:T(8,128)(2,1)S(1)}, bf16[8192,512]{1,0:T(8,128)(2,1)}, u32[]{:S(2)}) %copy-start) | copy-done | bytes 8388632
  150.4 2.3 %start_price.2 = (f32[96,512]{1,0:T(8,128)S(1)}, f32[96,64]{1,0:T(8,128)S(1)}) custom-call(s32[10]{0:T(128)S(1)} %pad_add_fusion.place, bf16[8,32,1024]{2,1,0:T(8,128)(2,1)S(1)} %constant_dynamic-update-slice_fusion.refs_0_, bf16[8,32,1024]{2,1,0:T(8,128)(2,1)S(1)} %collective-permute-done.34.refs_1_, ...), custom_call_target="tpu_custom_call" | custom-call | flops 905969664 | bytes 9961472 | tf_op jit(solution)/shard_map/start_price/pallas_call | solution.py:74
  152.7 4.2 %collective-permute-done.38.piece = bf16[8,32,1024]{2,1,0:T(8,128)(2,1)} collective-permute-done((bf16[8,32,1024]{2,1,0:T(8,128)(2,1)S(1)}, bf16[8,32,1024]{2,1,0:T(8,128)(2,1)}, u32[]{:S(2)}, u32[]{:S(2)}) %collective-permute-start.38) | collective-permute-done | bytes 524320 | tf_op jit(solution)/shard_map/ppermute | solution.py:228
  156.9 3.8 %price.2 = (f32[64,640]{1,0:T(8,128)S(1)}, f32[64,640]{1,0:T(8,128)S(1)}, f32[2,64,64]{2,1,0:T(8,128)S(1)}) custom-call(s32[10]{0:T(128)S(1)} %pad_add_fusion.place, bf16[8,32,1024]{2,1,0:T(8,128)(2,1)} %collective-permute-done.38.piece, bf16[8,1024,512]{2,1,0:T(8,128)(2,1)S(1)} %bitcast.177, bf16[8,64,1024]{2,1,0:T(8,128)(2,1)S(1)} %bitcast.183, ...), custom_call_target="tpu_custom_call" | custom-call | flops 301989888 | bytes 8912896 | tf_op jit(solution)/shard_map/price/pallas_call | solution.py:97
  160.8 1.4 collective-permute-done.39
  162.3 4.2 %collective-permute-done.37.refs_2_ = bf16[8,32,1024]{2,1,0:T(8,128)(2,1)S(1)} collective-permute-done((bf16[8,32,1024]{2,1,0:T(8,128)(2,1)S(1)}, bf16[8,32,1024]{2,1,0:T(8,128)(2,1)S(1)}, u32[]{:S(2)}, u32[]{:S(2)}) %collective-permute-start.37) | collective-permute-done | bytes 524320 | tf_op jit(solution)/shard_map/ppermute | solution.py:228
  168.5 2.5 %collective-permute-done.41 = f32[32,640]{1,0:T(8,128)S(1)} collective-permute-done((f32[32,640]{1,0:T(8,128)S(1)}, f32[32,640]{1,0:T(8,128)S(1)}, u32[]{:S(2)}, u32[]{:S(2)}) %collective-permute-start.41) | collective-permute-done | bytes 81952 | tf_op jit(solution)/shard_map/ppermute | solution.py:225
  171.0 1.5 collective-permute-done.42
  173.3 1.5 collective-permute-start.44
  174.8 2.3 %start_price.3 = (f32[96,512]{1,0:T(8,128)S(1)}, f32[96,64]{1,0:T(8,128)S(1)}) custom-call(s32[10]{0:T(128)S(1)} %pad_add_fusion.place, bf16[8,32,1024]{2,1,0:T(8,128)(2,1)S(1)} %constant_dynamic-update-slice_fusion.4.refs_0_, bf16[8,32,1024]{2,1,0:T(8,128)(2,1)S(1)} %collective-permute-done.35.refs_1_, ...), custom_call_target="tpu_custom_call" | custom-call | flops 905969664 | bytes 9961472 | tf_op jit(solution)/shard_map/start_price/pallas_call | solution.py:74
  177.7 3.4 %solve.2.mine = f32[64,512]{1,0:T(8,128)S(1)} custom-call(f32[32,640]{1,0:T(8,128)S(1)} %get-tuple-element.198.first_top, f32[32,640]{1,0:T(8,128)S(1)} %get-tuple-element.197.first_bottom, f32[32,640]{1,0:T(8,128)S(1)} %collective-permute-done.43.second_top, f32[32,640]{1,0:T(8,128)S(1)} %collective-permute-done.44.second_bottom), custom_call_target="tpu_custom_call" | custom-call | flops 25690112 | bytes 393216 | tf_op jit(solution)/shard_map/solve/pallas_call | solution.py:139
  181.1 3.2 %price.3 = (f32[64,640]{1,0:T(8,128)S(1)}, f32[64,640]{1,0:T(8,128)S(1)}, f32[2,64,64]{2,1,0:T(8,128)S(1)}) custom-call(s32[10]{0:T(128)S(1)} %pad_add_fusion.place, bf16[8,32,1024]{2,1,0:T(8,128)(2,1)S(1)} %collective-permute-done.40.piece, bf16[8,1024,512]{2,1,0:T(8,128)(2,1)S(1)} %bitcast.181, bf16[8,64,1024]{2,1,0:T(8,128)(2,1)S(1)} %bitcast.185, ...), custom_call_target="tpu_custom_call" | custom-call | flops 301989888 | bytes 8912896 | tf_op jit(solution)/shard_map/price/pallas_call | solution.py:97
  185.8 1.5 collective-permute-start.46
  188.1 2.3 %collective-permute-done.46 = f32[32,640]{1,0:T(8,128)S(1)} collective-permute-done((f32[32,640]{1,0:T(8,128)S(1)}, f32[32,640]{1,0:T(8,128)S(1)}, u32[]{:S(2)}, u32[]{:S(2)}) %collective-permute-start.46) | collective-permute-done | bytes 81952 | tf_op jit(solution)/shard_map/ppermute | solution.py:225
  190.3 1.4 collective-permute-done.47
  194.0 2.2 %expose.2.refs_0_ = f32[4,64,1024]{2,1,0:T(8,128)} custom-call(s32[10]{0:T(128)S(1)} %pad_add_fusion.place, f32[2,64,64]{2,1,0:T(8,128)S(1)} %get-tuple-element.148.basis, f32[64,512]{1,0:T(8,128)S(1)} %solve.2.mine, f32[64,512]{1,0:T(8,128)S(1)} %collective-permute-done.50.other, bf16[512,1024]{1,0:T(8,128)(2,1)S(1)} %fusion.2.member), custom_call_target="tpu_custom_call" | custom-call | flops 402653184 | bytes 1048576 | tf_op jit(solution)/shard_map/expose/pallas_call | solution.py:185
  196.9 3.4 %solve.3.mine = f32[64,512]{1,0:T(8,128)S(1)} custom-call(f32[32,640]{1,0:T(8,128)S(1)} %get-tuple-element.194.first_top, f32[32,640]{1,0:T(8,128)S(1)} %get-tuple-element.193.first_bottom, f32[32,640]{1,0:T(8,128)S(1)} %collective-permute-done.48.second_top, f32[32,640]{1,0:T(8,128)S(1)} %collective-permute-done.49.second_bottom), custom_call_target="tpu_custom_call" | custom-call | flops 25690112 | bytes 393216 | tf_op jit(solution)/shard_map/solve/pallas_call | solution.py:139
  201.7 2.2 %expose.3 = f32[4,64,1024]{2,1,0:T(8,128)} custom-call(s32[10]{0:T(128)S(1)} %pad_add_fusion.place, f32[2,64,64]{2,1,0:T(8,128)S(1)} %get-tuple-element.142.basis, f32[64,512]{1,0:T(8,128)S(1)} %solve.3.mine, f32[64,512]{1,0:T(8,128)S(1)} %collective-permute-done.51.other, bf16[512,1024]{1,0:T(8,128)(2,1)S(1)} %fusion.2.member, ...), custom_call_target="tpu_custom_call", output_to_operand_aliasing={{}: (5, {})} | custom-call | flops 402653184 | bytes 1048576 | tf_op jit(solution)/shard_map/expose/pallas_call | solution.py:185
  (157 shorter events, 33.9 us)
Async XLA Ops:
  1.5 4.6 %collective-permute-start = (bf16[128,2048]{1,0:T(8,128)(2,1)S(1)}, bf16[128,2048]{1,0:T(8,128)(2,1)S(1)}, u32[]{:S(2)}, u32[]{:S(2)}) collective-permute-start(bf16[128,2048]{1,0:T(8,128)(2,1)S(1)} %bitcast.193), channel_id=1, source_target_pairs={{0,4},{4,0},{8,12},{12,8},{16,20},{20,16},{24,28},{28,24},{1,5},{5... | collective-permute-start | bytes 1572872 | tf_op jit(solution)/shard_map/ppermute | solution.py:225
  2.0 26.5 %collective-permute-start.5 = (bf16[128,2048]{1,0:T(8,128)(2,1)S(1)}, bf16[128,2048]{1,0:T(8,128)(2,1)S(1)}, u32[]{:S(2)}, u32[]{:S(2)}) collective-permute-start(bf16[128,2048]{1,0:T(8,128)(2,1)S(1)} %bitcast.194), channel_id=1, source_target_pairs={{0,8},{4,12},{8,0},{12,4},{16,24},{20,28},{24,16},{28,20},{1,9},{5... | collective-permute-start | bytes 1572872 | tf_op jit(solution)/shard_map/ppermute | solution.py:225
  4.6 25.2 %collective-permute-start.6 = (bf16[128,2048]{1,0:T(8,128)(2,1)S(1)}, bf16[128,2048]{1,0:T(8,128)(2,1)S(1)}, u32[]{:S(2)}, u32[]{:S(2)}) collective-permute-start(bf16[128,2048]{1,0:T(8,128)(2,1)S(1)} %bitcast.195), channel_id=1, source_target_pairs={{0,16},{4,20},{8,24},{12,28},{16,0},{20,4},{24,8},{28,12},{1,17},{... | collective-permute-start | bytes 1572872 | tf_op jit(solution)/shard_map/ppermute | solution.py:225
  6.1 23.7 %collective-permute-start.7 = (bf16[128,2048]{1,0:T(8,128)(2,1)S(1)}, bf16[128,2048]{1,0:T(8,128)(2,1)}, u32[]{:S(2)}, u32[]{:S(2)}) collective-permute-start(bf16[128,2048]{1,0:T(8,128)(2,1)S(1)} %bitcast.196), channel_id=1, source_target_pairs={{0,24},{4,28},{8,16},{12,20},{16,8},{20,12},{24,0},{28,4},{1,25},{... | collective-permute-start | bytes 1572872 | tf_op jit(solution)/shard_map/ppermute | solution.py:225
  8.4 10.5 %collective-permute-start.1 = (f32[2,32,1024]{2,1,0:T(8,128)}, f32[2,32,1024]{2,1,0:T(8,128)S(1)}, u32[]{:S(2)}, u32[]{:S(2)}) collective-permute-start(f32[2,32,1024]{2,1,0:T(8,128)} %slice_bitcast_fusion.4), channel_id=1, source_target_pairs={{0,1},{1,2},{2,3},{3,0},{4,5},{5,6},{6,7},{7,4},{8,9},{9,10},{10,1... | collective-permute-start | bytes 786440 | tf_op jit(solution)/shard_map/ppermute | solution.py:228
  11.3 7.7 %collective-permute-start.3 = (f32[3072]{0:T(1024)S(1)}, f32[3072]{0:T(1024)S(1)}, u32[]{:S(2)}, u32[]{:S(2)}) collective-permute-start(f32[3072]{0:T(1024)S(1)} %pad_maximum_fusion.13), channel_id=1, source_target_pairs={{0,1},{1,0},{2,3},{3,2},{4,5},{5,4},{6,7},{7,6},{8,9},{9,8},{10,11... | collective-permute-start | bytes 36872 | tf_op jit(solution)/shard_map/ppermute | solution.py:286
  19.0 9.2 %collective-permute-start.2 = (f32[2,32,1024]{2,1,0:T(8,128)S(1)}, f32[2,32,1024]{2,1,0:T(8,128)S(1)}, u32[]{:S(2)}, u32[]{:S(2)}) collective-permute-start(f32[2,32,1024]{2,1,0:T(8,128)S(1)} %fusion.33), channel_id=1, source_target_pairs={{0,1},{1,2},{2,3},{3,0},{4,5},{5,6},{6,7},{7,4},{8,9},{9,10},{10,1... | collective-permute-start | bytes 786440 | tf_op jit(solution)/shard_map/ppermute | solution.py:228
  19.1 9.4 %collective-permute-start.8 = (f32[5120]{0:T(1024)S(1)}, f32[5120]{0:T(1024)S(1)}, u32[]{:S(2)}, u32[]{:S(2)}) collective-permute-start(f32[5120]{0:T(1024)S(1)} %pad_maximum_fusion.12), channel_id=1, source_target_pairs={{0,2},{1,3},{2,0},{3,1},{4,6},{5,7},{6,4},{7,5},{8,10},{9,11},{10,... | collective-permute-start | bytes 61448 | tf_op jit(solution)/shard_map/ppermute | solution.py:286
  28.2 8.7 %collective-permute-start.4 = (f32[2,32,1024]{2,1,0:T(8,128)S(1)}, f32[2,32,1024]{2,1,0:T(8,128)S(1)}, u32[]{:S(2)}, u32[]{:S(2)}) collective-permute-start(f32[2,32,1024]{2,1,0:T(8,128)S(1)} %fusion.34), channel_id=1, source_target_pairs={{0,1},{1,2},{2,3},{3,0},{4,5},{5,6},{6,7},{7,4},{8,9},{9,10},{10,1... | collective-permute-start | bytes 786440 | tf_op jit(solution)/shard_map/ppermute | solution.py:228
  31.1 7.6 %collective-permute-start.10 = (bf16[3,128,2048]{2,1,0:T(8,128)(2,1)S(1)}, bf16[3,128,2048]{2,1,0:T(8,128)(2,1)S(1)}, u32[]{:S(2)}, u32[]{:S(2)}) collective-permute-start(bf16[3,128,2048]{2,1,0:T(8,128)(2,1)S(1)} %pad_maximum_fusion.1), channel_id=1, source_target_pairs={{0,4},{4,0},{8,12},{12,8},{16,20},{20,16},{24,28},{28,24},{1,5},{5... | collective-permute-start | bytes 4718600 | tf_op jit(solution)/shard_map/ppermute | solution.py:225
  33.2 9.2 %collective-permute-start.9 = (f16[3,32,1024]{2,1,0:T(8,128)(2,1)S(1)}, f16[3,32,1024]{2,1,0:T(8,128)(2,1)S(1)}, u32[]{:S(2)}, u32[]{:S(2)}) collective-permute-start(f16[3,32,1024]{2,1,0:T(8,128)(2,1)S(1)} %fusion.36), channel_id=1, source_target_pairs={{0,1},{1,2},{2,3},{3,0},{4,5},{5,6},{6,7},{7,4},{8,9},{9,10},{10,1... | collective-permute-start | bytes 589832 | tf_op jit(solution)/shard_map/ppermute | solution.py:228
  34.8 25.2 %collective-permute-start.14 = (bf16[128,2048]{1,0:T(8,128)(2,1)S(1)}, bf16[128,2048]{1,0:T(8,128)(2,1)S(1)}, u32[]{:S(2)}, u32[]{:S(2)}) collective-permute-start(bf16[128,2048]{1,0:T(8,128)(2,1)S(1)} %bitcast.198), channel_id=1, source_target_pairs={{0,8},{4,12},{8,0},{12,4},{16,24},{20,28},{24,16},{28,20},{1,9},{5... | collective-permute-start | bytes 1572872 | tf_op jit(solution)/shard_map/ppermute | solution.py:225
  36.1 23.9 %collective-permute-start.15 = (bf16[128,2048]{1,0:T(8,128)(2,1)S(1)}, bf16[128,2048]{1,0:T(8,128)(2,1)S(1)}, u32[]{:S(2)}, u32[]{:S(2)}) collective-permute-start(bf16[128,2048]{1,0:T(8,128)(2,1)S(1)} %bitcast.199), channel_id=1, source_target_pairs={{0,16},{4,20},{8,24},{12,28},{16,0},{20,4},{24,8},{28,12},{1,17},{... | collective-permute-start | bytes 1572872 | tf_op jit(solution)/shard_map/ppermute | solution.py:225
  36.9 24.2 %collective-permute-start.16 = (bf16[128,2048]{1,0:T(8,128)(2,1)S(1)}, bf16[128,2048]{1,0:T(8,128)(2,1)S(1)}, u32[]{:S(2)}, u32[]{:S(2)}) collective-permute-start(bf16[128,2048]{1,0:T(8,128)(2,1)S(1)} %bitcast.200), channel_id=1, source_target_pairs={{0,24},{4,28},{8,16},{12,20},{16,8},{20,12},{24,0},{28,4},{1,25},{... | collective-permute-start | bytes 1572872 | tf_op jit(solution)/shard_map/ppermute | solution.py:225
  40.7 9.5 %collective-permute-start.12 = (f16[3,32,1024]{2,1,0:T(8,128)(2,1)S(1)}, f16[3,32,1024]{2,1,0:T(8,128)(2,1)S(1)}, u32[]{:S(2)}, u32[]{:S(2)}) collective-permute-start(f16[3,32,1024]{2,1,0:T(8,128)(2,1)S(1)} %fusion.37), channel_id=1, source_target_pairs={{0,1},{1,2},{2,3},{3,0},{4,5},{5,6},{6,7},{7,4},{8,9},{9,10},{10,1... | collective-permute-start | bytes 589832 | tf_op jit(solution)/shard_map/ppermute | solution.py:228
  42.4 11.7 %collective-permute-start.11 = (f16[3,32,1024]{2,1,0:T(8,128)(2,1)S(1)}, f16[3,32,1024]{2,1,0:T(8,128)(2,1)S(1)}, u32[]{:S(2)}, u32[]{:S(2)}) collective-permute-start(f16[3,32,1024]{2,1,0:T(8,128)(2,1)S(1)} %fusion.22), channel_id=1, source_target_pairs={{0,1},{1,2},{2,3},{3,0},{4,5},{5,6},{6,7},{7,4},{8,9},{9,10},{10,1... | collective-permute-start | bytes 589832 | tf_op jit(solution)/shard_map/ppermute | solution.py:228
  50.3 9.6 %collective-permute-start.17 = (f16[3,32,1024]{2,1,0:T(8,128)(2,1)S(1)}, f16[3,32,1024]{2,1,0:T(8,128)(2,1)S(1)}, u32[]{:S(2)}, u32[]{:S(2)}) collective-permute-start(f16[3,32,1024]{2,1,0:T(8,128)(2,1)S(1)} %fusion.16), channel_id=1, source_target_pairs={{0,1},{1,2},{2,3},{3,0},{4,5},{5,6},{6,7},{7,4},{8,9},{9,10},{10,1... | collective-permute-start | bytes 589832 | tf_op jit(solution)/shard_map/ppermute | solution.py:228
  54.2 9.9 %collective-permute-start.13 = (f16[3,32,1024]{2,1,0:T(8,128)(2,1)S(1)}, f16[3,32,1024]{2,1,0:T(8,128)(2,1)S(1)}, u32[]{:S(2)}, u32[]{:S(2)}) collective-permute-start(f16[3,32,1024]{2,1,0:T(8,128)(2,1)S(1)} %fusion.18), channel_id=1, source_target_pairs={{0,1},{1,2},{2,3},{3,0},{4,5},{5,6},{6,7},{7,4},{8,9},{9,10},{10,1... | collective-permute-start | bytes 589832 | tf_op jit(solution)/shard_map/ppermute | solution.py:228
  60.0 7.5 %collective-permute-start.20 = (f16[3,32,1024]{2,1,0:T(8,128)(2,1)S(1)}, f16[3,32,1024]{2,1,0:T(8,128)(2,1)S(1)}, u32[]{:S(2)}, u32[]{:S(2)}) collective-permute-start(f16[3,32,1024]{2,1,0:T(8,128)(2,1)S(1)} %fusion.14), channel_id=1, source_target_pairs={{0,1},{1,2},{2,3},{3,0},{4,5},{5,6},{6,7},{7,4},{8,9},{9,10},{10,1... | collective-permute-start | bytes 589832 | tf_op jit(solution)/shard_map/ppermute | solution.py:228
  61.4 8.0 %collective-permute-start.19 = (bf16[4,128,2048]{2,1,0:T(8,128)(2,1)S(1)}, bf16[4,128,2048]{2,1,0:T(8,128)(2,1)S(1)}, u32[]{:S(2)}, u32[]{:S(2)}) collective-permute-start(bf16[4,128,2048]{2,1,0:T(8,128)(2,1)S(1)} %pad_maximum_fusion), channel_id=1, source_target_pairs={{0,4},{4,0},{8,12},{12,8},{16,20},{20,16},{24,28},{28,24},{1,5},{5... | collective-permute-start | bytes 6291464 | tf_op jit(solution)/shard_map/ppermute | solution.py:225
  67.8 1.6 collective-permute-start.21
  67.9 11.2 %collective-permute-start.18 = (f16[4,32,1024]{2,1,0:T(8,128)(2,1)S(1)}, f16[4,32,1024]{2,1,0:T(8,128)(2,1)S(1)}, u32[]{:S(2)}, u32[]{:S(2)}) collective-permute-start(f16[4,32,1024]{2,1,0:T(8,128)(2,1)S(1)} %fusion.25), channel_id=1, source_target_pairs={{0,1},{1,2},{2,3},{3,0},{4,5},{5,6},{6,7},{7,4},{8,9},{9,10},{10,1... | collective-permute-start | bytes 786440 | tf_op jit(solution)/shard_map/ppermute | solution.py:228
  72.0 12.7 %collective-permute-start.26 = (f16[4,32,1024]{2,1,0:T(8,128)(2,1)S(1)}, f16[4,32,1024]{2,1,0:T(8,128)(2,1)S(1)}, u32[]{:S(2)}, u32[]{:S(2)}) collective-permute-start(f16[4,32,1024]{2,1,0:T(8,128)(2,1)S(1)} %fusion.26), channel_id=1, source_target_pairs={{0,1},{1,2},{2,3},{3,0},{4,5},{5,6},{6,7},{7,4},{8,9},{9,10},{10,1... | collective-permute-start | bytes 786440 | tf_op jit(solution)/shard_map/ppermute | solution.py:228
  72.1 12.7 %collective-permute-start.23 = (bf16[2,32,1024]{2,1,0:T(8,128)(2,1)S(1)}, bf16[2,32,1024]{2,1,0:T(8,128)(2,1)S(1)}, u32[]{:S(2)}, u32[]{:S(2)}) collective-permute-start(bf16[2,32,1024]{2,1,0:T(8,128)(2,1)S(1)} %get-tuple-element.188), channel_id=1, source_target_pairs={{0,8},{4,12},{8,0},{12,4},{16,24},{20,28},{24,16},{28,20},{1,9},{5... | collective-permute-start | bytes 393224 | tf_op jit(solution)/shard_map/ppermute | solution.py:225
  73.4 11.4 %collective-permute-start.24 = (bf16[2,32,1024]{2,1,0:T(8,128)(2,1)S(1)}, bf16[2,32,1024]{2,1,0:T(8,128)(2,1)S(1)}, u32[]{:S(2)}, u32[]{:S(2)}) collective-permute-start(bf16[2,32,1024]{2,1,0:T(8,128)(2,1)S(1)} %get-tuple-element.189), channel_id=1, source_target_pairs={{0,16},{4,20},{8,24},{12,28},{16,0},{20,4},{24,8},{28,12},{1,17},{... | collective-permute-start | bytes 393224 | tf_op jit(solution)/shard_map/ppermute | solution.py:225
  74.1 10.7 %collective-permute-start.25 = (bf16[2,32,1024]{2,1,0:T(8,128)(2,1)S(1)}, bf16[2,32,1024]{2,1,0:T(8,128)(2,1)S(1)}, u32[]{:S(2)}, u32[]{:S(2)}) collective-permute-start(bf16[2,32,1024]{2,1,0:T(8,128)(2,1)S(1)} %get-tuple-element.187), channel_id=1, source_target_pairs={{0,24},{4,28},{8,16},{12,20},{16,8},{20,12},{24,0},{28,4},{1,25},{... | collective-permute-start | bytes 393224 | tf_op jit(solution)/shard_map/ppermute | solution.py:225
  79.1 11.2 %collective-permute-start.22 = (f16[4,32,1024]{2,1,0:T(8,128)(2,1)S(1)}, f16[4,32,1024]{2,1,0:T(8,128)(2,1)S(1)}, u32[]{:S(2)}, u32[]{:S(2)}) collective-permute-start(f16[4,32,1024]{2,1,0:T(8,128)(2,1)S(1)} %fusion.12), channel_id=1, source_target_pairs={{0,1},{1,2},{2,3},{3,0},{4,5},{5,6},{6,7},{7,4},{8,9},{9,10},{10,1... | collective-permute-start | bytes 786440 | tf_op jit(solution)/shard_map/ppermute | solution.py:228
  84.7 11.2 %collective-permute-start.28 = (f16[4,32,1024]{2,1,0:T(8,128)(2,1)S(1)}, f16[4,32,1024]{2,1,0:T(8,128)(2,1)S(1)}, u32[]{:S(2)}, u32[]{:S(2)}) collective-permute-start(f16[4,32,1024]{2,1,0:T(8,128)(2,1)S(1)} %fusion.6), channel_id=1, source_target_pairs={{0,1},{1,2},{2,3},{3,0},{4,5},{5,6},{6,7},{7,4},{8,9},{9,10},{10,1... | collective-permute-start | bytes 786440 | tf_op jit(solution)/shard_map/ppermute | solution.py:228
  90.3 11.2 %collective-permute-start.27 = (f16[4,32,1024]{2,1,0:T(8,128)(2,1)S(1)}, f16[4,32,1024]{2,1,0:T(8,128)(2,1)S(1)}, u32[]{:S(2)}, u32[]{:S(2)}) collective-permute-start(f16[4,32,1024]{2,1,0:T(8,128)(2,1)S(1)} %fusion.8), channel_id=1, source_target_pairs={{0,1},{1,2},{2,3},{3,0},{4,5},{5,6},{6,7},{7,4},{8,9},{9,10},{10,1... | collective-permute-start | bytes 786440 | tf_op jit(solution)/shard_map/ppermute | solution.py:228
  96.0 11.2 %collective-permute-start.29 = (f16[4,32,1024]{2,1,0:T(8,128)(2,1)S(1)}, f16[4,32,1024]{2,1,0:T(8,128)(2,1)S(1)}, u32[]{:S(2)}, u32[]{:S(2)}) collective-permute-start(f16[4,32,1024]{2,1,0:T(8,128)(2,1)S(1)} %fusion.4), channel_id=1, source_target_pairs={{0,1},{1,2},{2,3},{3,0},{4,5},{5,6},{6,7},{7,4},{8,9},{9,10},{10,1... | collective-permute-start | bytes 786440 | tf_op jit(solution)/shard_map/ppermute | solution.py:228
  96.0 21.7 %collective-permute-start.34 = (bf16[8,32,1024]{2,1,0:T(8,128)(2,1)S(1)}, bf16[8,32,1024]{2,1,0:T(8,128)(2,1)S(1)}, u32[]{:S(2)}, u32[]{:S(2)}) collective-permute-start(bf16[8,32,1024]{2,1,0:T(8,128)(2,1)S(1)} %constant_dynamic-update-slice_fusion.refs_0_), channel_id=1, source_target_pairs={{0,1},{1,2},{2,3},{3,0},{4,5},{5,6},{6,7},{7,4},{8,9},{9,10},{10,1... | collective-permute-start | bytes 1572872 | tf_op jit(solution)/shard_map/ppermute | solution.py:228
  109.1 8.5 %collective-permute-start.31 = (bf16[2,32,1024]{2,1,0:T(8,128)(2,1)S(1)}, bf16[2,32,1024]{2,1,0:T(8,128)(2,1)S(1)}, u32[]{:S(2)}, u32[]{:S(2)}) collective-permute-start(bf16[2,32,1024]{2,1,0:T(8,128)(2,1)S(1)} %get-tuple-element.184), channel_id=1, source_target_pairs={{0,8},{4,12},{8,0},{12,4},{16,24},{20,28},{24,16},{28,20},{1,9},{5... | collective-permute-start | bytes 393224 | tf_op jit(solution)/shard_map/ppermute | solution.py:225
  110.4 8.1 %collective-permute-start.32 = (bf16[2,32,1024]{2,1,0:T(8,128)(2,1)S(1)}, bf16[2,32,1024]{2,1,0:T(8,128)(2,1)S(1)}, u32[]{:S(2)}, u32[]{:S(2)}) collective-permute-start(bf16[2,32,1024]{2,1,0:T(8,128)(2,1)S(1)} %get-tuple-element.185), channel_id=1, source_target_pairs={{0,16},{4,20},{8,24},{12,28},{16,0},{20,4},{24,8},{28,12},{1,17},{... | collective-permute-start | bytes 393224 | tf_op jit(solution)/shard_map/ppermute | solution.py:225
  111.1 7.4 %collective-permute-start.33 = (bf16[2,32,1024]{2,1,0:T(8,128)(2,1)S(1)}, bf16[2,32,1024]{2,1,0:T(8,128)(2,1)S(1)}, u32[]{:S(2)}, u32[]{:S(2)}) collective-permute-start(bf16[2,32,1024]{2,1,0:T(8,128)(2,1)S(1)} %get-tuple-element.183), channel_id=1, source_target_pairs={{0,24},{4,28},{8,16},{12,20},{16,8},{20,12},{24,0},{28,4},{1,25},{... | collective-permute-start | bytes 393224 | tf_op jit(solution)/shard_map/ppermute | solution.py:225
  117.7 16.7 %collective-permute-start.36 = (bf16[8,32,1024]{2,1,0:T(8,128)(2,1)S(1)}, bf16[8,32,1024]{2,1,0:T(8,128)(2,1)S(1)}, u32[]{:S(2)}, u32[]{:S(2)}) collective-permute-start(bf16[8,32,1024]{2,1,0:T(8,128)(2,1)S(1)} %collective-permute-done.34.refs_1_), channel_id=1, source_target_pairs={{0,1},{1,2},{2,3},{3,0},{4,5},{5,6},{6,7},{7,4},{8,9},{9,10},{10,1... | collective-permute-start | bytes 1572872 | tf_op jit(solution)/shard_map/ppermute | solution.py:228
  118.6 27.0 %collective-permute-start.35 = (bf16[8,32,1024]{2,1,0:T(8,128)(2,1)S(1)}, bf16[8,32,1024]{2,1,0:T(8,128)(2,1)S(1)}, u32[]{:S(2)}, u32[]{:S(2)}) collective-permute-start(bf16[8,32,1024]{2,1,0:T(8,128)(2,1)S(1)} %constant_dynamic-update-slice_fusion.4.refs_0_), channel_id=1, source_target_pairs={{0,1},{1,2},{2,3},{3,0},{4,5},{5,6},{6,7},{7,4},{8,9},{9,10},{10,1... | collective-permute-start | bytes 1572872 | tf_op jit(solution)/shard_map/ppermute | solution.py:228
  134.3 22.6 %collective-permute-start.38 = (bf16[8,32,1024]{2,1,0:T(8,128)(2,1)S(1)}, bf16[8,32,1024]{2,1,0:T(8,128)(2,1)}, u32[]{:S(2)}, u32[]{:S(2)}) collective-permute-start(bf16[8,32,1024]{2,1,0:T(8,128)(2,1)S(1)} %collective-permute-done.36.refs_2_), channel_id=1, source_target_pairs={{0,1},{1,2},{2,3},{3,0},{4,5},{5,6},{6,7},{7,4},{8,9},{9,10},{10,1... | collective-permute-start | bytes 1572872 | tf_op jit(solution)/shard_map/ppermute | solution.py:228
  145.6 20.9 %collective-permute-start.37 = (bf16[8,32,1024]{2,1,0:T(8,128)(2,1)S(1)}, bf16[8,32,1024]{2,1,0:T(8,128)(2,1)S(1)}, u32[]{:S(2)}, u32[]{:S(2)}) collective-permute-start(bf16[8,32,1024]{2,1,0:T(8,128)(2,1)S(1)} %collective-permute-done.35.refs_1_), channel_id=1, source_target_pairs={{0,1},{1,2},{2,3},{3,0},{4,5},{5,6},{6,7},{7,4},{8,9},{9,10},{10,1... | collective-permute-start | bytes 1572872 | tf_op jit(solution)/shard_map/ppermute | solution.py:228
  166.5 14.6 %collective-permute-start.40 = (bf16[8,32,1024]{2,1,0:T(8,128)(2,1)S(1)}, bf16[8,32,1024]{2,1,0:T(8,128)(2,1)S(1)}, u32[]{:S(2)}, u32[]{:S(2)}) collective-permute-start(bf16[8,32,1024]{2,1,0:T(8,128)(2,1)S(1)} %collective-permute-done.37.refs_2_), channel_id=1, source_target_pairs={{0,1},{1,2},{2,3},{3,0},{4,5},{5,6},{6,7},{7,4},{8,9},{9,10},{10,1... | collective-permute-start | bytes 1572872 | tf_op jit(solution)/shard_map/ppermute | solution.py:228
  166.5 4.5 %collective-permute-start.41 = (f32[32,640]{1,0:T(8,128)S(1)}, f32[32,640]{1,0:T(8,128)S(1)}, u32[]{:S(2)}, u32[]{:S(2)}) collective-permute-start(f32[32,640]{1,0:T(8,128)S(1)} %get-tuple-element.200), channel_id=1, source_target_pairs={{0,8},{4,12},{8,0},{12,4},{16,24},{20,28},{24,16},{28,20},{1,9},{5... | collective-permute-start | bytes 245768 | tf_op jit(solution)/shard_map/ppermute | solution.py:225
  167.8 4.7 %collective-permute-start.42 = (f32[32,640]{1,0:T(8,128)S(1)}, f32[32,640]{1,0:T(8,128)S(1)}, u32[]{:S(2)}, u32[]{:S(2)}) collective-permute-start(f32[32,640]{1,0:T(8,128)S(1)} %get-tuple-element.199), channel_id=1, source_target_pairs={{0,16},{4,20},{8,24},{12,28},{16,0},{20,4},{24,8},{28,12},{1,17},{... | collective-permute-start | bytes 245768 | tf_op jit(solution)/shard_map/ppermute | solution.py:225
  172.5 4.6 %collective-permute-start.43 = (f32[32,640]{1,0:T(8,128)S(1)}, f32[32,640]{1,0:T(8,128)S(1)}, u32[]{:S(2)}, u32[]{:S(2)}) collective-permute-start(f32[32,640]{1,0:T(8,128)S(1)} %get-tuple-element.198.first_top), channel_id=1, source_target_pairs={{0,16},{4,20},{8,24},{12,28},{16,0},{20,4},{24,8},{28,12},{1,17},{... | collective-permute-start | bytes 245768 | tf_op jit(solution)/shard_map/ppermute | solution.py:225
  173.3 4.4 %collective-permute-start.44 = (f32[32,640]{1,0:T(8,128)S(1)}, f32[32,640]{1,0:T(8,128)S(1)}, u32[]{:S(2)}, u32[]{:S(2)}) collective-permute-start(f32[32,640]{1,0:T(8,128)S(1)} %get-tuple-element.197.first_bottom), channel_id=1, source_target_pairs={{0,8},{4,12},{8,0},{12,4},{16,24},{20,28},{24,16},{28,20},{1,9},{5... | collective-permute-start | bytes 245768 | tf_op jit(solution)/shard_map/ppermute | solution.py:225
  185.8 4.6 %collective-permute-start.46 = (f32[32,640]{1,0:T(8,128)S(1)}, f32[32,640]{1,0:T(8,128)S(1)}, u32[]{:S(2)}, u32[]{:S(2)}) collective-permute-start(f32[32,640]{1,0:T(8,128)S(1)} %get-tuple-element.196), channel_id=1, source_target_pairs={{0,8},{4,12},{8,0},{12,4},{16,24},{20,28},{24,16},{28,20},{1,9},{5... | collective-permute-start | bytes 245768 | tf_op jit(solution)/shard_map/ppermute | solution.py:225
  187.3 4.4 %collective-permute-start.47 = (f32[32,640]{1,0:T(8,128)S(1)}, f32[32,640]{1,0:T(8,128)S(1)}, u32[]{:S(2)}, u32[]{:S(2)}) collective-permute-start(f32[32,640]{1,0:T(8,128)S(1)} %get-tuple-element.195), channel_id=1, source_target_pairs={{0,16},{4,20},{8,24},{12,28},{16,0},{20,4},{24,8},{28,12},{1,17},{... | collective-permute-start | bytes 245768 | tf_op jit(solution)/shard_map/ppermute | solution.py:225
  188.0 6.0 %collective-permute-start.50 = (f32[64,512]{1,0:T(8,128)S(1)}, f32[64,512]{1,0:T(8,128)S(1)}, u32[]{:S(2)}, u32[]{:S(2)}) collective-permute-start(f32[64,512]{1,0:T(8,128)S(1)} %solve.2.mine), channel_id=1, source_target_pairs={{0,4},{4,0},{8,12},{12,8},{16,20},{20,16},{24,28},{28,24},{1,5},{5... | collective-permute-start | bytes 393224 | tf_op jit(solution)/shard_map/ppermute | solution.py:225
  191.8 4.5 %collective-permute-start.48 = (f32[32,640]{1,0:T(8,128)S(1)}, f32[32,640]{1,0:T(8,128)S(1)}, u32[]{:S(2)}, u32[]{:S(2)}) collective-permute-start(f32[32,640]{1,0:T(8,128)S(1)} %get-tuple-element.194.first_top), channel_id=1, source_target_pairs={{0,16},{4,20},{8,24},{12,28},{16,0},{20,4},{24,8},{28,12},{1,17},{... | collective-permute-start | bytes 245768 | tf_op jit(solution)/shard_map/ppermute | solution.py:225
  192.5 4.4 %collective-permute-start.49 = (f32[32,640]{1,0:T(8,128)S(1)}, f32[32,640]{1,0:T(8,128)S(1)}, u32[]{:S(2)}, u32[]{:S(2)}) collective-permute-start(f32[32,640]{1,0:T(8,128)S(1)} %get-tuple-element.193.first_bottom), channel_id=1, source_target_pairs={{0,8},{4,12},{8,0},{12,4},{16,24},{20,28},{24,16},{28,20},{1,9},{5... | collective-permute-start | bytes 245768 | tf_op jit(solution)/shard_map/ppermute | solution.py:225
  (13 other events, 86.7 us)

commit v3 on v2

--- a/solution.py
+++ b/solution.py
@@ -214,6 +214,7 @@
     ridge = 0.01 * path_count * path_size
     even = list(range(2, path_size, 2))
     bits = [2**n for n in range(1, path_size.bit_length() - 1)]
+    core = path_index & 1
     place = jnp.concatenate(
         [
             jnp.stack([fac_index, path_index & 1]),
@@ -221,8 +222,9 @@
         ]
     ).astype(jnp.int32)
 
-    def exchange(x, k):
-        return lax.ppermute(x, "path", [(i, i ^ k) for i in range(path_size)])
+    def exchange(x, k, k_odd=None):
+        far = [k, k if k_odd is None else k_odd]
+        return lax.ppermute(x, "path", [(i, i ^ far[i & 1]) for i in range(path_size)])
 
     def pass_on(x, hops=1):
         return lax.ppermute(x, "fac", [(i, (i + hops) % fac_size) for i in range(fac_size)])
@@ -244,10 +246,14 @@
         return product.reshape(block.shape[0], fac_size, chunk_rows, row_block)
 
     def reduce_over_fac(block, scale, kind):
-        terms = partial_sums(gate(block), scale)
+        return ring_sum([partial_sums(gate(block), scale)], kind)
+
+    def ring_sum(terms, kind, scale=None):
         running = None
         for hop in range(fac_size):
-            term = terms[:, hop]
+            term = jnp.concatenate([t[:, hop] for t in terms])
+            if scale is not None:
+                term = term * scale
             if running is not None:
                 term = term + gate(running).astype(jnp.float32)
             if hop < fac_size - 1:
@@ -273,9 +279,9 @@
     ).reshape(HALVES, fac_size * chunk_rows, fac_width)
 
     own = mark(ordered[0])
-    received = [exchange(own, k) for k in even]
-    chain_a = reduce_over_fac(jnp.stack([own, exchange(own, 1)]), None, jnp.float32)
-    next(chain_a)
+    two_bits = len(bits) == 2
+    received = [exchange(own, k) for k in (bits if two_bits else even)]
+    siblings = exchange(ordered, 1)
 
     row_peak = jnp.max(jnp.abs(chol_factor), axis=1).astype(jnp.float32)
     vols, note = gate(factor_vol), None
@@ -284,7 +290,8 @@
         note = mark(jnp.concatenate([vols, row_peak]))
         swap = [(i, i ^ bit) for i in range(fac_size)]
         arrived = lax.ppermute(note, "fac", swap)
-        next(chain_a)
+        if 2 * bit >= fac_size:
+            near_terms = mark(partial_sums(gate(jnp.concatenate([ordered, siblings])), None))
         arrived = gate(arrived)
         split = arrived.shape[0] - row_block
         lower = (fac_index & bit) == 0
@@ -352,41 +359,71 @@
         so_far = yield None
         yield mark(expose(place, basis, coef, gate(other), member, half, so_far))
 
-    for _ in range(fac_size - 2 - (fac_size.bit_length() - 1)):
+    chain_a = ring_sum([near_terms], jnp.float16, shrink)
+    next(chain_a)
+    for _ in range(fac_size - 4):
         next(chain_a)
-    rest = mark(jnp.stack(gate(*received)))
-    arrived = exchange(rest, 1)
-    chain_b = reduce_over_fac(rest, shrink, jnp.float16)
+    if two_bits:
+        received = gate(*received)
+        third = exchange(mark(jnp.where(core == 0, *received)), bits[1], bits[0])
+        rest = mark(jnp.stack(received))
+        arrived_rest = exchange(rest, 1)
+        own_terms = [mark(partial_sums(rest, None))]
+        next(chain_a)
+        swapped_terms = [mark(partial_sums(gate(arrived_rest), None))]
+        rest = mark(gate(third)[None])
+        third = exchange(rest, 1)
+        own_terms.append(partial_sums(rest, None))
+        chain_b = ring_sum(own_terms, jnp.float16, shrink)
+        next(chain_b)
+    else:
+        next(chain_a)
+        rest = mark(jnp.stack(gate(*received)))
+        third = exchange(rest, 1)
+        swapped_terms = []
+        chain_b = ring_sum([partial_sums(rest, None)], jnp.float16, shrink)
+        next(chain_b)
+    own = gate(ordered[1])
+    received = [exchange(own, k) for k in (bits if two_bits else even)]
+    next(chain_a)
+    swapped_terms.append(partial_sums(gate(third), None))
+    chain_c = ring_sum(swapped_terms, jnp.float16, shrink)
+    next(chain_c)
     next(chain_b)
-    own = gate(ordered[1])
-    received = [exchange(own, k) for k in even]
-    near_sum = next(chain_a)
-    chain_c = reduce_over_fac(arrived, shrink, jnp.float16)
+    near_sum = next(chain_a) * peak
+    if two_bits:
+        received = list(gate(*received))
+        third_late = exchange(mark(jnp.where(core == 0, *received)), bits[1], bits[0])
     next(chain_c)
-    for hop in range(1, fac_size - 1):
+    for hop in range(2, fac_size - 1):
         next(chain_b)
         next(chain_c)
-    block = mark(jnp.stack([own, *gate(*received)]))
+    if two_bits:
+        received = [*received, gate(third_late)]
+        block = mark(jnp.stack(received))
+    else:
+        block = mark(jnp.stack(gate(*received)))
     arrived = exchange(block, 1)
     chain_d = reduce_over_fac(block, shrink, jnp.float16)
     next(chain_d)
-    mine = jnp.concatenate([near_sum[:1], next(chain_b) * peak])
+    chain_e = reduce_over_fac(arrived, shrink, jnp.float16)
+    next(chain_e)
+    next(chain_d)
+    mine = jnp.concatenate([near_sum[0:1], next(chain_b) * peak])
     mine, carry = levels_of(mine, 0.0)
-    others = jnp.concatenate([near_sum[1:], next(chain_c) * peak])
+    others = jnp.concatenate([near_sum[2:3], next(chain_c) * peak])
     others, other_carry = levels_of(others, 0.0)
     first = regroup(mine, others)
     next(first)
     next(first)
-    chain_e = reduce_over_fac(arrived, shrink, jnp.float16)
     next(chain_e)
-    next(chain_d)
-    next(chain_e)
-    ring_first = gather_over_fac(next(first))
-    next(ring_first)
     for hop in range(2, fac_size - 1):
         next(chain_d)
         next(chain_e)
-    mine, others = next(chain_d) * peak, next(chain_e) * peak
+    ring_first = gather_over_fac(next(first))
+    next(ring_first)
+    mine = jnp.concatenate([near_sum[1:2], next(chain_d) * peak])
+    others = jnp.concatenate([near_sum[3:4], next(chain_e) * peak])
     others, _ = levels_of(others, other_carry)
     mine, _ = levels_of(mine, carry)
     second = regroup(mine, others)

time: 204 us -> 197 us (0.966)
  waiting for transfers between devices: 123 us -> 112 us
  starting transfers between devices: 35.7 us -> 42 us
  local copies, waits for them, and re-layouts: 7.49 us -> 3.9 us
    ppermute x21, waiting for transfers between devices: 103 us -> 82 us  [pass_on(): lax.ppermute(x, 'fac', [(i, (i + hops) % fac_size) for i in range(fac_siz...]
    ppermute x29 -> x30, waiting for transfers between devices: 19.1 us -> 30 us  [exchange(): lax.ppermute(x, 'path', [(i, i ^ far[i & 1]) for i in range(path_size)])]
    ppermute x21, starting transfers between devices: 7.29 us -> 10.7 us  [pass_on(): lax.ppermute(x, 'fac', [(i, (i + hops) % fac_size) for i in range(fac_siz...]
    unnamed x22 -> x24, local copies, waits for them, and re-layouts: 3.48 us -> 0.96 us
    dot_general x5 -> x7, matrix products: 9.77 us -> 11.7 us  [dot(): lax.dot_general(a, b, dims, precision=precision, preferred_element_type=j...]
    ppermute x29 -> x30, starting transfers between devices: 24.5 us -> 25.5 us  [exchange(): lax.ppermute(x, 'path', [(i, i ^ far[i & 1]) for i in range(path_size)])]
  transfers between devices with their start and end apart: 52 -> 53, of which waited for: 34 -> 33; matrix products, arithmetic and copies ran while one was open for 8% -> 9% of each run, Pallas kernels for 7% -> 7%
where the time goes in v3:
time: 197 us
  waiting for transfers between devices  112 us (57%)
  starting transfers between devices  42 us (21%)
  Pallas kernels  22.2 us (11%)
  matrix products  11.7 us (6%)
  other arithmetic  3.92 us (2%)
  local copies, waits for them, and re-layouts  3.9 us (2%)
    ppermute x21, waiting for transfers between devices, pass_on(): lax.ppermute(x, 'fac', [(i, (i + hops) % fac_size) for i in range(fac_siz...  82 us
    ppermute x30, waiting for transfers between devices, exchange(): lax.ppermute(x, 'path', [(i, i ^ far[i & 1]) for i in range(path_size)])  30 us
    ppermute x30, starting transfers between devices, exchange(): lax.ppermute(x, 'path', [(i, i ^ far[i & 1]) for i in range(path_size)])  25.5 us
    dot_general x7, matrix products, dot(): lax.dot_general(a, b, dims, precision=precision, preferred_element_type=j...  11.7 us
    ppermute x21, starting transfers between devices, pass_on(): lax.ppermute(x, 'fac', [(i, (i + hops) % fac_size) for i in range(fac_siz...  10.7 us
    pallas_call x2, Pallas kernels, solve(): pl.pallas_call(functools.partial(solve_kernel, ridge), out_shape=jax.Shap...  6.72 us
    pallas_call x2, Pallas kernels, price(): pl.pallas_call(price_kernel, in_specs=[pl.BlockSpec(memory_space=pltpu.SM...  6.37 us
    ppermute x2, starting transfers between devices, on_device(): arrived = lax.ppermute(note, 'fac', swap)  5.74 us
  transfers between devices with their start and end apart: 53, of which 33 were waited for; matrix products, arithmetic and copies ran while one was open for 9% of the time, Pallas kernels for 7%

profile of v3, /device:TPU:0, one launch (start us, length us, event | category | flops | bytes accessed | tf_op | source)
XLA Modules:
  0.0 196.6 jit_solution(3711734365472794186)
XLA Ops:
  4.7 3.1 %collective-permute-start.1 = (f32[3072]{0:T(1024)S(1)}, f32[3072]{0:T(1024)S(1)}, u32[]{:S(2)}, u32[]{:S(2)}) collective-permute-start(f32[3072]{0:T(1024)S(1)} %pad_maximum_fusion.15), channel_id=1, source_target_pairs={{0,1},{1,0},{2,3},{3,2},{4,5},{5,4},{6,7},{7,6},{8,9},{9,8},{10,11... | collective-permute-start | bytes 36872 | tf_op jit(solution)/shard_map/ppermute | solution.py:292
  9.3 1.5 collective-permute-start.5
  10.9 2.7 %collective-permute-start.2 = (f32[5120]{0:T(1024)S(1)}, f32[5120]{0:T(1024)S(1)}, u32[]{:S(2)}, u32[]{:S(2)}) collective-permute-start(f32[5120]{0:T(1024)S(1)} %pad_maximum_fusion.14), channel_id=1, source_target_pairs={{0,2},{1,3},{2,0},{3,1},{4,6},{5,7},{6,4},{7,5},{8,10},{9,11},{10,... | collective-permute-start | bytes 61448 | tf_op jit(solution)/shard_map/ppermute | solution.py:292
  13.7 2.4 %fusion.6 = f32[4,4,32,1024]{3,2,1,0:T(8,128)S(1)} fusion(bf16[4,4,32,2048]{3,2,1,0:T(8,128)(2,1)S(1)} %bitcast.220, bf16[1024,2048]{1,0:T(8,128)(2,1)S(1)} %copy-done.1), kind=kOutput, calls=%fused_computation.6 | convolution fusion | flops 2147483648 | bytes 8388608 | tf_op jit(solution)/shard_map/dot_general | solution.py:20
  16.9 4.5 %collective-permute-done.4 = bf16[128,2048]{1,0:T(8,128)(2,1)S(1)} collective-permute-done((bf16[128,2048]{1,0:T(8,128)(2,1)}, bf16[128,2048]{1,0:T(8,128)(2,1)S(1)}, u32[]{:S(2)}, u32[]{:S(2)}) %collective-permute-start.4) | collective-permute-done | bytes 524320 | tf_op jit(solution)/shard_map/ppermute | solution.py:227
  22.9 1.6 collective-permute-start.7
  27.8 4.4 %collective-permute-done.7 = bf16[128,2048]{1,0:T(8,128)(2,1)S(1)} collective-permute-done((bf16[128,2048]{1,0:T(8,128)(2,1)S(1)}, bf16[128,2048]{1,0:T(8,128)(2,1)S(1)}, u32[]{:S(2)}, u32[]{:S(2)}) %collective-permute-start.7) | collective-permute-done | bytes 524320 | tf_op jit(solution)/shard_map/ppermute | solution.py:227
  32.1 1.5 fusion.93
  34.8 1.6 collective-permute-start.15
  36.5 2.8 %collective-permute-start.9 = (f16[4,32,1024]{2,1,0:T(8,128)(2,1)S(1)}, f16[4,32,1024]{2,1,0:T(8,128)(2,1)S(1)}, u32[]{:S(2)}, u32[]{:S(2)}) collective-permute-start(f16[4,32,1024]{2,1,0:T(8,128)(2,1)S(1)} %fusion.22), channel_id=1, source_target_pairs={{0,1},{1,2},{2,3},{3,0},{4,5},{5,6},{6,7},{7,4},{8,9},{9,10},{10,1... | collective-permute-start | bytes 786440 | tf_op jit(solution)/shard_map/ppermute | solution.py:230
  39.3 1.5 fusion.9
  41.5 1.9 collective-permute-done.10
  43.5 5.5 %collective-permute-done.9 = f16[4,32,1024]{2,1,0:T(8,128)(2,1)S(1)} collective-permute-done((f16[4,32,1024]{2,1,0:T(8,128)(2,1)S(1)}, f16[4,32,1024]{2,1,0:T(8,128)(2,1)S(1)}, u32[]{:S(2)}, u32[]{:S(2)}) %collective-permute-start.9) | collective-permute-done | bytes 262176 | tf_op jit(solution)/shard_map/ppermute | solution.py:230
  49.2 1.6 collective-permute-start.17
  50.7 2.5 %collective-permute-done.13 = f16[3,32,1024]{2,1,0:T(8,128)(2,1)S(1)} collective-permute-done((f16[3,32,1024]{2,1,0:T(8,128)(2,1)S(1)}, f16[3,32,1024]{2,1,0:T(8,128)(2,1)S(1)}, u32[]{:S(2)}, u32[]{:S(2)}) %collective-permute-start.13) | collective-permute-done | bytes 196640 | tf_op jit(solution)/shard_map/ppermute | solution.py:230
  53.4 3.7 %collective-permute-done.12 = f16[3,32,1024]{2,1,0:T(8,128)(2,1)S(1)} collective-permute-done((f16[3,32,1024]{2,1,0:T(8,128)(2,1)S(1)}, f16[3,32,1024]{2,1,0:T(8,128)(2,1)S(1)}, u32[]{:S(2)}, u32[]{:S(2)}) %collective-permute-start.12) | collective-permute-done | bytes 196640 | tf_op jit(solution)/shard_map/ppermute | solution.py:230
  57.1 4.2 %collective-permute-done.18 = f16[3,32,1024]{2,1,0:T(8,128)(2,1)S(1)} collective-permute-done((f16[3,32,1024]{2,1,0:T(8,128)(2,1)S(1)}, f16[3,32,1024]{2,1,0:T(8,128)(2,1)S(1)}, u32[]{:S(2)}, u32[]{:S(2)}) %collective-permute-start.18) | collective-permute-done | bytes 196640 | tf_op jit(solution)/shard_map/ppermute | solution.py:230
  63.1 1.8 convolution_multiply_fusion.1
  65.6 1.9 convolution_multiply_fusion
  67.6 3.2 %collective-permute-start.22 = (f16[3,32,1024]{2,1,0:T(8,128)(2,1)S(1)}, f16[3,32,1024]{2,1,0:T(8,128)(2,1)S(1)}, u32[]{:S(2)}, u32[]{:S(2)}) collective-permute-start(f16[3,32,1024]{2,1,0:T(8,128)(2,1)S(1)} %fusion.62), channel_id=1, source_target_pairs={{0,1},{1,2},{2,3},{3,0},{4,5},{5,6},{6,7},{7,4},{8,9},{9,10},{10,1... | collective-permute-start | bytes 589832 | tf_op jit(solution)/shard_map/ppermute | solution.py:230
  70.9 8.9 %collective-permute-done.19 = f16[3,32,1024]{2,1,0:T(8,128)(2,1)S(1)} collective-permute-done((f16[3,32,1024]{2,1,0:T(8,128)(2,1)S(1)}, f16[3,32,1024]{2,1,0:T(8,128)(2,1)S(1)}, u32[]{:S(2)}, u32[]{:S(2)}) %collective-permute-start.19) | collective-permute-done | bytes 196640 | tf_op jit(solution)/shard_map/ppermute | solution.py:230
  80.4 3.1 %collective-permute-done.22 = f16[3,32,1024]{2,1,0:T(8,128)(2,1)S(1)} collective-permute-done((f16[3,32,1024]{2,1,0:T(8,128)(2,1)S(1)}, f16[3,32,1024]{2,1,0:T(8,128)(2,1)S(1)}, u32[]{:S(2)}, u32[]{:S(2)}) %collective-permute-start.22) | collective-permute-done | bytes 196640 | tf_op jit(solution)/shard_map/ppermute | solution.py:230
  83.6 4.1 %collective-permute-done.21 = f16[3,32,1024]{2,1,0:T(8,128)(2,1)S(1)} collective-permute-done((f16[3,32,1024]{2,1,0:T(8,128)(2,1)S(1)}, f16[3,32,1024]{2,1,0:T(8,128)(2,1)S(1)}, u32[]{:S(2)}, u32[]{:S(2)}) %collective-permute-start.21) | collective-permute-done | bytes 196640 | tf_op jit(solution)/shard_map/ppermute | solution.py:230
  88.5 1.5 collective-permute-start.27
  91.5 1.8 collective-permute-done.29
  94.1 1.8 collective-permute-done.28
  97.0 5.9 %collective-permute-done.30 = f16[3,32,1024]{2,1,0:T(8,128)(2,1)S(1)} collective-permute-done((f16[3,32,1024]{2,1,0:T(8,128)(2,1)S(1)}, f16[3,32,1024]{2,1,0:T(8,128)(2,1)S(1)}, u32[]{:S(2)}, u32[]{:S(2)}) %collective-permute-start.30) | collective-permute-done | bytes 196640 | tf_op jit(solution)/shard_map/ppermute | solution.py:230
  105.1 2.0 %collective-permute-start.33 = (bf16[2,32,1024]{2,1,0:T(8,128)(2,1)S(1)}, bf16[2,32,1024]{2,1,0:T(8,128)(2,1)S(1)}, u32[]{:S(2)}, u32[]{:S(2)}) collective-permute-start(bf16[2,32,1024]{2,1,0:T(8,128)(2,1)S(1)} %get-tuple-element.187), channel_id=1, source_target_pairs={{0,16},{4,20},{8,24},{12,28},{16,0},{20,4},{24,8},{28,12},{1,17},{... | collective-permute-start | bytes 393224 | tf_op jit(solution)/shard_map/ppermute | solution.py:227
  107.0 1.5 collective-permute-start.34
  108.6 3.1 %collective-permute-done.35.refs_1_ = bf16[8,32,1024]{2,1,0:T(8,128)(2,1)S(1)} collective-permute-done((bf16[8,32,1024]{2,1,0:T(8,128)(2,1)S(1)}, bf16[8,32,1024]{2,1,0:T(8,128)(2,1)S(1)}, u32[]{:S(2)}, u32[]{:S(2)}) %collective-permute-start.35) | collective-permute-done | bytes 524320 | tf_op jit(solution)/shard_map/ppermute | solution.py:230
  111.6 2.7 %collective-permute-done.34 = bf16[2,32,1024]{2,1,0:T(8,128)(2,1)S(1)} collective-permute-done((bf16[2,32,1024]{2,1,0:T(8,128)(2,1)S(1)}, bf16[2,32,1024]{2,1,0:T(8,128)(2,1)S(1)}, u32[]{:S(2)}, u32[]{:S(2)}) %collective-permute-start.34) | collective-permute-done | bytes 131104 | tf_op jit(solution)/shard_map/ppermute | solution.py:227
  114.5 13.8 %collective-permute-done.37.refs_2_ = bf16[8,32,1024]{2,1,0:T(8,128)(2,1)S(1)} collective-permute-done((bf16[8,32,1024]{2,1,0:T(8,128)(2,1)S(1)}, bf16[8,32,1024]{2,1,0:T(8,128)(2,1)S(1)}, u32[]{:S(2)}, u32[]{:S(2)}) %collective-permute-start.37) | collective-permute-done | bytes 524320 | tf_op jit(solution)/shard_map/ppermute | solution.py:230
  128.3 11.2 %collective-permute-done.36.refs_1_ = bf16[8,32,1024]{2,1,0:T(8,128)(2,1)S(1)} collective-permute-done((bf16[8,32,1024]{2,1,0:T(8,128)(2,1)S(1)}, bf16[8,32,1024]{2,1,0:T(8,128)(2,1)S(1)}, u32[]{:S(2)}, u32[]{:S(2)}) %collective-permute-start.36) | collective-permute-done | bytes 524320 | tf_op jit(solution)/shard_map/ppermute | solution.py:230
  139.7 2.3 %start_price.2 = (f32[96,512]{1,0:T(8,128)S(1)}, f32[96,64]{1,0:T(8,128)S(1)}) custom-call(s32[10]{0:T(128)S(1)} %pad_add_fusion.place, bf16[8,32,1024]{2,1,0:T(8,128)(2,1)S(1)} %constant_dynamic-update-slice_fusion.refs_0_, bf16[8,32,1024]{2,1,0:T(8,128)(2,1)S(1)} %collective-permute-done.35.refs_1_, ...), custom_call_target="tpu_custom_call" | custom-call | flops 905969664 | bytes 9961472 | tf_op jit(solution)/shard_map/start_price/pallas_call | solution.py:74
  142.0 8.7 %collective-permute-done.39.piece = bf16[8,32,1024]{2,1,0:T(8,128)(2,1)S(1)} collective-permute-done((bf16[8,32,1024]{2,1,0:T(8,128)(2,1)S(1)}, bf16[8,32,1024]{2,1,0:T(8,128)(2,1)S(1)}, u32[]{:S(2)}, u32[]{:S(2)}) %collective-permute-start.39) | collective-permute-done | bytes 524320 | tf_op jit(solution)/shard_map/ppermute | solution.py:230
  150.7 3.2 %price.2 = (f32[64,640]{1,0:T(8,128)S(1)}, f32[64,640]{1,0:T(8,128)S(1)}, f32[2,64,64]{2,1,0:T(8,128)S(1)}) custom-call(s32[10]{0:T(128)S(1)} %pad_add_fusion.place, bf16[8,32,1024]{2,1,0:T(8,128)(2,1)S(1)} %collective-permute-done.39.piece, bf16[8,1024,512]{2,1,0:T(8,128)(2,1)S(1)} %bitcast.210, bf16[8,64,1024]{2,1,0:T(8,128)(2,1)S(1)} %bitcast.214, ...), custom_call_target="tpu_custom_call" | custom-call | flops 301989888 | bytes 8912896 | tf_op jit(solution)/shard_map/price/pallas_call | solution.py:97
  155.4 3.0 %collective-permute-done.38.refs_2_ = bf16[8,32,1024]{2,1,0:T(8,128)(2,1)S(1)} collective-permute-done((bf16[8,32,1024]{2,1,0:T(8,128)(2,1)S(1)}, bf16[8,32,1024]{2,1,0:T(8,128)(2,1)S(1)}, u32[]{:S(2)}, u32[]{:S(2)}) %collective-permute-start.38) | collective-permute-done | bytes 524320 | tf_op jit(solution)/shard_map/ppermute | solution.py:230
  158.5 2.1 %collective-permute-start.42 = (f32[32,640]{1,0:T(8,128)S(1)}, f32[32,640]{1,0:T(8,128)S(1)}, u32[]{:S(2)}, u32[]{:S(2)}) collective-permute-start(f32[32,640]{1,0:T(8,128)S(1)} %get-tuple-element.212), channel_id=1, source_target_pairs={{0,8},{4,12},{8,0},{12,4},{16,24},{20,28},{24,16},{28,20},{1,9},{5... | collective-permute-start | bytes 245768 | tf_op jit(solution)/shard_map/ppermute | solution.py:227
  161.1 1.8 collective-permute-done.42
  163.0 2.6 %collective-permute-done.43 = f32[32,640]{1,0:T(8,128)S(1)} collective-permute-done((f32[32,640]{1,0:T(8,128)S(1)}, f32[32,640]{1,0:T(8,128)S(1)}, u32[]{:S(2)}, u32[]{:S(2)}) %collective-permute-start.43) | collective-permute-done | bytes 81952 | tf_op jit(solution)/shard_map/ppermute | solution.py:227
  167.0 2.3 %start_price.3 = (f32[96,512]{1,0:T(8,128)S(1)}, f32[96,64]{1,0:T(8,128)S(1)}) custom-call(s32[10]{0:T(128)S(1)} %pad_add_fusion.place, bf16[8,32,1024]{2,1,0:T(8,128)(2,1)S(1)} %constant_dynamic-update-slice_fusion.4.refs_0_, bf16[8,32,1024]{2,1,0:T(8,128)(2,1)S(1)} %collective-permute-done.36.refs_1_, ...), custom_call_target="tpu_custom_call" | custom-call | flops 905969664 | bytes 9961472 | tf_op jit(solution)/shard_map/start_price/pallas_call | solution.py:74
  170.4 3.4 %solve.2.mine = f32[64,512]{1,0:T(8,128)S(1)} custom-call(f32[32,640]{1,0:T(8,128)S(1)} %get-tuple-element.210.first_top, f32[32,640]{1,0:T(8,128)S(1)} %get-tuple-element.209.first_bottom, f32[32,640]{1,0:T(8,128)S(1)} %collective-permute-done.44.second_top, f32[32,640]{1,0:T(8,128)S(1)} %collective-permute-done.45.second_bottom), custom_call_target="tpu_custom_call" | custom-call | flops 25690112 | bytes 393216 | tf_op jit(solution)/shard_map/solve/pallas_call | solution.py:139
  173.8 3.2 %price.3 = (f32[64,640]{1,0:T(8,128)S(1)}, f32[64,640]{1,0:T(8,128)S(1)}, f32[2,64,64]{2,1,0:T(8,128)S(1)}) custom-call(s32[10]{0:T(128)S(1)} %pad_add_fusion.place, bf16[8,32,1024]{2,1,0:T(8,128)(2,1)S(1)} %collective-permute-done.41.piece, bf16[8,1024,512]{2,1,0:T(8,128)(2,1)S(1)} %bitcast.212, bf16[8,64,1024]{2,1,0:T(8,128)(2,1)S(1)} %bitcast.216, ...), custom_call_target="tpu_custom_call" | custom-call | flops 301989888 | bytes 8912896 | tf_op jit(solution)/shard_map/price/pallas_call | solution.py:97
  180.7 2.3 %collective-permute-done.47 = f32[32,640]{1,0:T(8,128)S(1)} collective-permute-done((f32[32,640]{1,0:T(8,128)S(1)}, f32[32,640]{1,0:T(8,128)S(1)}, u32[]{:S(2)}, u32[]{:S(2)}) %collective-permute-start.47) | collective-permute-done | bytes 81952 | tf_op jit(solution)/shard_map/ppermute | solution.py:227
  185.1 1.7 collective-permute-start.50
  187.1 2.2 %expose.2.refs_0_ = f32[4,64,1024]{2,1,0:T(8,128)} custom-call(s32[10]{0:T(128)S(1)} %pad_add_fusion.place, f32[2,64,64]{2,1,0:T(8,128)S(1)} %get-tuple-element.148.basis, f32[64,512]{1,0:T(8,128)S(1)} %solve.2.mine, f32[64,512]{1,0:T(8,128)S(1)} %collective-permute-done.51.other, bf16[512,1024]{1,0:T(8,128)(2,1)S(1)} %fusion.8.member), custom_call_target="tpu_custom_call" | custom-call | flops 402653184 | bytes 1048576 | tf_op jit(solution)/shard_map/expose/pallas_call | solution.py:185
  189.6 3.4 %solve.3.mine = f32[64,512]{1,0:T(8,128)S(1)} custom-call(f32[32,640]{1,0:T(8,128)S(1)} %get-tuple-element.206.first_top, f32[32,640]{1,0:T(8,128)S(1)} %get-tuple-element.205.first_bottom, f32[32,640]{1,0:T(8,128)S(1)} %collective-permute-done.49.second_top, f32[32,640]{1,0:T(8,128)S(1)} %collective-permute-done.50.second_bottom), custom_call_target="tpu_custom_call" | custom-call | flops 25690112 | bytes 393216 | tf_op jit(solution)/shard_map/solve/pallas_call | solution.py:139
  194.4 2.2 %expose.3 = f32[4,64,1024]{2,1,0:T(8,128)} custom-call(s32[10]{0:T(128)S(1)} %pad_add_fusion.place, f32[2,64,64]{2,1,0:T(8,128)S(1)} %get-tuple-element.142.basis, f32[64,512]{1,0:T(8,128)S(1)} %solve.3.mine, f32[64,512]{1,0:T(8,128)S(1)} %collective-permute-done.52.other, bf16[512,1024]{1,0:T(8,128)(2,1)S(1)} %fusion.8.member, ...), custom_call_target="tpu_custom_call", output_to_operand_aliasing={{}: (5, {})} | custom-call | flops 402653184 | bytes 1048576 | tf_op jit(solution)/shard_map/expose/pallas_call | solution.py:185
  (168 shorter events, 36.3 us)
Async XLA Ops:
  1.4 12.1 %collective-permute-start = (bf16[2,128,2048]{2,1,0:T(8,128)(2,1)S(1)}, bf16[2,128,2048]{2,1,0:T(8,128)(2,1)S(1)}, u32[]{:S(2)}, u32[]{:S(2)}) collective-permute-start(bf16[2,128,2048]{2,1,0:T(8,128)(2,1)S(1)} %bitcast.217), channel_id=1, source_target_pairs={{0,4},{4,0},{8,12},{12,8},{16,20},{20,16},{24,28},{28,24},{1,5},{5... | collective-permute-start | bytes 3145736 | tf_op jit(solution)/shard_map/ppermute | solution.py:227
  4.7 6.1 %collective-permute-start.1 = (f32[3072]{0:T(1024)S(1)}, f32[3072]{0:T(1024)S(1)}, u32[]{:S(2)}, u32[]{:S(2)}) collective-permute-start(f32[3072]{0:T(1024)S(1)} %pad_maximum_fusion.15), channel_id=1, source_target_pairs={{0,1},{1,0},{2,3},{3,2},{4,5},{5,4},{6,7},{7,6},{8,9},{9,8},{10,11... | collective-permute-start | bytes 36872 | tf_op jit(solution)/shard_map/ppermute | solution.py:292
  7.8 13.6 %collective-permute-start.4 = (bf16[128,2048]{1,0:T(8,128)(2,1)}, bf16[128,2048]{1,0:T(8,128)(2,1)S(1)}, u32[]{:S(2)}, u32[]{:S(2)}) collective-permute-start(bf16[128,2048]{1,0:T(8,128)(2,1)} %bitcast.8), channel_id=1, source_target_pairs={{0,8},{4,12},{8,0},{12,4},{16,24},{20,28},{24,16},{28,20},{1,9},{5... | collective-permute-start | bytes 1572872 | tf_op jit(solution)/shard_map/ppermute | solution.py:227
  9.3 13.3 %collective-permute-start.5 = (bf16[128,2048]{1,0:T(8,128)(2,1)}, bf16[128,2048]{1,0:T(8,128)(2,1)S(1)}, u32[]{:S(2)}, u32[]{:S(2)}) collective-permute-start(bf16[128,2048]{1,0:T(8,128)(2,1)} %bitcast.8), channel_id=1, source_target_pairs={{0,16},{4,20},{8,24},{12,28},{16,0},{20,4},{24,8},{28,12},{1,17},{... | collective-permute-start | bytes 1572872 | tf_op jit(solution)/shard_map/ppermute | solution.py:227
  10.9 5.2 %collective-permute-start.2 = (f32[5120]{0:T(1024)S(1)}, f32[5120]{0:T(1024)S(1)}, u32[]{:S(2)}, u32[]{:S(2)}) collective-permute-start(f32[5120]{0:T(1024)S(1)} %pad_maximum_fusion.14), channel_id=1, source_target_pairs={{0,2},{1,3},{2,0},{3,1},{4,6},{5,7},{6,4},{7,5},{8,10},{9,11},{10,... | collective-permute-start | bytes 61448 | tf_op jit(solution)/shard_map/ppermute | solution.py:292
  16.2 9.7 %collective-permute-start.3 = (f16[4,32,1024]{2,1,0:T(8,128)(2,1)S(1)}, f16[4,32,1024]{2,1,0:T(8,128)(2,1)S(1)}, u32[]{:S(2)}, u32[]{:S(2)}) collective-permute-start(f16[4,32,1024]{2,1,0:T(8,128)(2,1)S(1)} %fusion.16), channel_id=1, source_target_pairs={{0,1},{1,2},{2,3},{3,0},{4,5},{5,6},{6,7},{7,4},{8,9},{9,10},{10,1... | collective-permute-start | bytes 786440 | tf_op jit(solution)/shard_map/ppermute | solution.py:230
  22.9 9.2 %collective-permute-start.7 = (bf16[128,2048]{1,0:T(8,128)(2,1)S(1)}, bf16[128,2048]{1,0:T(8,128)(2,1)S(1)}, u32[]{:S(2)}, u32[]{:S(2)}) collective-permute-start(bf16[128,2048]{1,0:T(8,128)(2,1)S(1)} %broadcast_select_fusion.1), channel_id=1, source_target_pairs={{0,16},{4,12},{8,24},{12,4},{16,0},{20,28},{24,8},{28,20},{1,17},{... | collective-permute-start | bytes 1572872 | tf_op jit(solution)/shard_map/ppermute | solution.py:227
  26.0 10.4 %collective-permute-start.6 = (f16[4,32,1024]{2,1,0:T(8,128)(2,1)S(1)}, f16[4,32,1024]{2,1,0:T(8,128)(2,1)S(1)}, u32[]{:S(2)}, u32[]{:S(2)}) collective-permute-start(f16[4,32,1024]{2,1,0:T(8,128)(2,1)S(1)} %fusion.19), channel_id=1, source_target_pairs={{0,1},{1,2},{2,3},{3,0},{4,5},{5,6},{6,7},{7,4},{8,9},{9,10},{10,1... | collective-permute-start | bytes 786440 | tf_op jit(solution)/shard_map/ppermute | solution.py:230
  33.7 5.6 %collective-permute-start.11 = (bf16[1,128,2048]{2,1,0:T(8,128)(2,1)S(1)}, bf16[1,128,2048]{2,1,0:T(8,128)(2,1)S(1)}, u32[]{:S(2)}, u32[]{:S(2)}) collective-permute-start(bf16[1,128,2048]{2,1,0:T(8,128)(2,1)S(1)} %bitcast.241), channel_id=1, source_target_pairs={{0,4},{4,0},{8,12},{12,8},{16,20},{20,16},{24,28},{28,24},{1,5},{5... | collective-permute-start | bytes 1572872 | tf_op jit(solution)/shard_map/ppermute | solution.py:227
  33.8 9.5 %collective-permute-start.10 = (f16[3,32,1024]{2,1,0:T(8,128)(2,1)S(1)}, f16[3,32,1024]{2,1,0:T(8,128)(2,1)S(1)}, u32[]{:S(2)}, u32[]{:S(2)}) collective-permute-start(f16[3,32,1024]{2,1,0:T(8,128)(2,1)S(1)} %fusion.35), channel_id=1, source_target_pairs={{0,1},{1,2},{2,3},{3,0},{4,5},{5,6},{6,7},{7,4},{8,9},{9,10},{10,1... | collective-permute-start | bytes 589832 | tf_op jit(solution)/shard_map/ppermute | solution.py:230
  34.3 14.8 %collective-permute-start.14 = (bf16[128,2048]{1,0:T(8,128)(2,1)S(1)}, bf16[128,2048]{1,0:T(8,128)(2,1)S(1)}, u32[]{:S(2)}, u32[]{:S(2)}) collective-permute-start(bf16[128,2048]{1,0:T(8,128)(2,1)S(1)} %bitcast.242), channel_id=1, source_target_pairs={{0,8},{4,12},{8,0},{12,4},{16,24},{20,28},{24,16},{28,20},{1,9},{5... | collective-permute-start | bytes 1572872 | tf_op jit(solution)/shard_map/ppermute | solution.py:227
  34.8 14.3 %collective-permute-start.15 = (bf16[128,2048]{1,0:T(8,128)(2,1)S(1)}, bf16[128,2048]{1,0:T(8,128)(2,1)S(1)}, u32[]{:S(2)}, u32[]{:S(2)}) collective-permute-start(bf16[128,2048]{1,0:T(8,128)(2,1)S(1)} %bitcast.243), channel_id=1, source_target_pairs={{0,16},{4,20},{8,24},{12,28},{16,0},{20,4},{24,8},{28,12},{1,17},{... | collective-permute-start | bytes 1572872 | tf_op jit(solution)/shard_map/ppermute | solution.py:227
  36.5 12.5 %collective-permute-start.9 = (f16[4,32,1024]{2,1,0:T(8,128)(2,1)S(1)}, f16[4,32,1024]{2,1,0:T(8,128)(2,1)S(1)}, u32[]{:S(2)}, u32[]{:S(2)}) collective-permute-start(f16[4,32,1024]{2,1,0:T(8,128)(2,1)S(1)} %fusion.22), channel_id=1, source_target_pairs={{0,1},{1,2},{2,3},{3,0},{4,5},{5,6},{6,7},{7,4},{8,9},{9,10},{10,1... | collective-permute-start | bytes 786440 | tf_op jit(solution)/shard_map/ppermute | solution.py:230
  41.0 12.2 %collective-permute-start.13 = (f16[3,32,1024]{2,1,0:T(8,128)(2,1)S(1)}, f16[3,32,1024]{2,1,0:T(8,128)(2,1)S(1)}, u32[]{:S(2)}, u32[]{:S(2)}) collective-permute-start(f16[3,32,1024]{2,1,0:T(8,128)(2,1)S(1)} %fusion.38), channel_id=1, source_target_pairs={{0,1},{1,2},{2,3},{3,0},{4,5},{5,6},{6,7},{7,4},{8,9},{9,10},{10,1... | collective-permute-start | bytes 589832 | tf_op jit(solution)/shard_map/ppermute | solution.py:230
  43.4 13.6 %collective-permute-start.12 = (f16[3,32,1024]{2,1,0:T(8,128)(2,1)S(1)}, f16[3,32,1024]{2,1,0:T(8,128)(2,1)S(1)}, u32[]{:S(2)}, u32[]{:S(2)}) collective-permute-start(f16[3,32,1024]{2,1,0:T(8,128)(2,1)S(1)} %fusion.37), channel_id=1, source_target_pairs={{0,1},{1,2},{2,3},{3,0},{4,5},{5,6},{6,7},{7,4},{8,9},{9,10},{10,1... | collective-permute-start | bytes 589832 | tf_op jit(solution)/shard_map/ppermute | solution.py:230
  49.2 12.2 %collective-permute-start.17 = (bf16[128,2048]{1,0:T(8,128)(2,1)S(1)}, bf16[128,2048]{1,0:T(8,128)(2,1)S(1)}, u32[]{:S(2)}, u32[]{:S(2)}) collective-permute-start(bf16[128,2048]{1,0:T(8,128)(2,1)S(1)} %broadcast_select_fusion), channel_id=1, source_target_pairs={{0,16},{4,12},{8,24},{12,4},{16,0},{20,28},{24,8},{28,20},{1,17},{... | collective-permute-start | bytes 1572872 | tf_op jit(solution)/shard_map/ppermute | solution.py:227
  53.3 8.0 %collective-permute-start.18 = (f16[3,32,1024]{2,1,0:T(8,128)(2,1)S(1)}, f16[3,32,1024]{2,1,0:T(8,128)(2,1)S(1)}, u32[]{:S(2)}, u32[]{:S(2)}) collective-permute-start(f16[3,32,1024]{2,1,0:T(8,128)(2,1)S(1)} %fusion.43), channel_id=1, source_target_pairs={{0,1},{1,2},{2,3},{3,0},{4,5},{5,6},{6,7},{7,4},{8,9},{9,10},{10,1... | collective-permute-start | bytes 589832 | tf_op jit(solution)/shard_map/ppermute | solution.py:230
  61.5 4.1 %collective-permute-start.20 = (bf16[3,128,2048]{2,1,0:T(8,128)(2,1)S(1)}, bf16[3,128,2048]{2,1,0:T(8,128)(2,1)S(1)}, u32[]{:S(2)}, u32[]{:S(2)}) collective-permute-start(bf16[3,128,2048]{2,1,0:T(8,128)(2,1)S(1)} %pad_maximum_fusion.1), channel_id=1, source_target_pairs={{0,4},{4,0},{8,12},{12,8},{16,20},{20,16},{24,28},{28,24},{1,5},{5... | collective-permute-start | bytes 4718600 | tf_op jit(solution)/shard_map/ppermute | solution.py:227
  61.7 18.1 %collective-permute-start.16 = (f16[3,32,1024]{2,1,0:T(8,128)(2,1)S(1)}, f16[3,32,1024]{2,1,0:T(8,128)(2,1)S(1)}, u32[]{:S(2)}, u32[]{:S(2)}) collective-permute-start(f16[3,32,1024]{2,1,0:T(8,128)(2,1)S(1)} %fusion.41), channel_id=1, source_target_pairs={{0,1},{1,2},{2,3},{3,0},{4,5},{5,6},{6,7},{7,4},{8,9},{9,10},{10,1... | collective-permute-start | bytes 589832 | tf_op jit(solution)/shard_map/ppermute | solution.py:230
  61.8 18.1 %collective-permute-start.23 = (f16[3,32,1024]{2,1,0:T(8,128)(2,1)S(1)}, f16[3,32,1024]{2,1,0:T(8,128)(2,1)S(1)}, u32[]{:S(2)}, u32[]{:S(2)}) collective-permute-start(f16[3,32,1024]{2,1,0:T(8,128)(2,1)S(1)} %fusion.45), channel_id=1, source_target_pairs={{0,1},{1,2},{2,3},{3,0},{4,5},{5,6},{6,7},{7,4},{8,9},{9,10},{10,1... | collective-permute-start | bytes 589832 | tf_op jit(solution)/shard_map/ppermute | solution.py:230
  65.1 14.6 %collective-permute-start.19 = (f16[3,32,1024]{2,1,0:T(8,128)(2,1)S(1)}, f16[3,32,1024]{2,1,0:T(8,128)(2,1)S(1)}, u32[]{:S(2)}, u32[]{:S(2)}) collective-permute-start(f16[3,32,1024]{2,1,0:T(8,128)(2,1)S(1)} %fusion.61), channel_id=1, source_target_pairs={{0,1},{1,2},{2,3},{3,0},{4,5},{5,6},{6,7},{7,4},{8,9},{9,10},{10,1... | collective-permute-start | bytes 589832 | tf_op jit(solution)/shard_map/ppermute | solution.py:230
  67.6 15.9 %collective-permute-start.22 = (f16[3,32,1024]{2,1,0:T(8,128)(2,1)S(1)}, f16[3,32,1024]{2,1,0:T(8,128)(2,1)S(1)}, u32[]{:S(2)}, u32[]{:S(2)}) collective-permute-start(f16[3,32,1024]{2,1,0:T(8,128)(2,1)S(1)} %fusion.62), channel_id=1, source_target_pairs={{0,1},{1,2},{2,3},{3,0},{4,5},{5,6},{6,7},{7,4},{8,9},{9,10},{10,1... | collective-permute-start | bytes 589832 | tf_op jit(solution)/shard_map/ppermute | solution.py:230
  79.8 7.9 %collective-permute-start.21 = (f16[3,32,1024]{2,1,0:T(8,128)(2,1)S(1)}, f16[3,32,1024]{2,1,0:T(8,128)(2,1)S(1)}, u32[]{:S(2)}, u32[]{:S(2)}) collective-permute-start(f16[3,32,1024]{2,1,0:T(8,128)(2,1)S(1)} %fusion.31), channel_id=1, source_target_pairs={{0,1},{1,2},{2,3},{3,0},{4,5},{5,6},{6,7},{7,4},{8,9},{9,10},{10,1... | collective-permute-start | bytes 589832 | tf_op jit(solution)/shard_map/ppermute | solution.py:230
  80.3 7.6 %collective-permute-start.24 = (bf16[4,32,1024]{2,1,0:T(8,128)(2,1)S(1)}, bf16[4,32,1024]{2,1,0:T(8,128)(2,1)S(1)}, u32[]{:S(2)}, u32[]{:S(2)}) collective-permute-start(bf16[4,32,1024]{2,1,0:T(8,128)(2,1)S(1)} %bitcast.245), channel_id=1, source_target_pairs={{0,4},{4,0},{8,12},{12,8},{16,20},{20,16},{24,28},{28,24},{1,5},{5... | collective-permute-start | bytes 786440 | tf_op jit(solution)/shard_map/ppermute | solution.py:227
  83.6 9.7 %collective-permute-start.29 = (f16[3,32,1024]{2,1,0:T(8,128)(2,1)S(1)}, f16[3,32,1024]{2,1,0:T(8,128)(2,1)S(1)}, u32[]{:S(2)}, u32[]{:S(2)}) collective-permute-start(f16[3,32,1024]{2,1,0:T(8,128)(2,1)S(1)} %fusion.28), channel_id=1, source_target_pairs={{0,1},{1,2},{2,3},{3,0},{4,5},{5,6},{6,7},{7,4},{8,9},{9,10},{10,1... | collective-permute-start | bytes 589832 | tf_op jit(solution)/shard_map/ppermute | solution.py:230
  87.8 9.2 %collective-permute-start.25 = (f16[3,32,1024]{2,1,0:T(8,128)(2,1)S(1)}, f16[3,32,1024]{2,1,0:T(8,128)(2,1)S(1)}, u32[]{:S(2)}, u32[]{:S(2)}) collective-permute-start(f16[3,32,1024]{2,1,0:T(8,128)(2,1)S(1)} %fusion.34), channel_id=1, source_target_pairs={{0,1},{1,2},{2,3},{3,0},{4,5},{5,6},{6,7},{7,4},{8,9},{9,10},{10,1... | collective-permute-start | bytes 589832 | tf_op jit(solution)/shard_map/ppermute | solution.py:230
  87.9 5.4 %collective-permute-start.26 = (bf16[2,32,1024]{2,1,0:T(8,128)(2,1)S(1)}, bf16[2,32,1024]{2,1,0:T(8,128)(2,1)S(1)}, u32[]{:S(2)}, u32[]{:S(2)}) collective-permute-start(bf16[2,32,1024]{2,1,0:T(8,128)(2,1)S(1)} %get-tuple-element.194), channel_id=1, source_target_pairs={{0,8},{4,12},{8,0},{12,4},{16,24},{20,28},{24,16},{28,20},{1,9},{5... | collective-permute-start | bytes 393224 | tf_op jit(solution)/shard_map/ppermute | solution.py:227
  88.5 5.6 %collective-permute-start.27 = (bf16[2,32,1024]{2,1,0:T(8,128)(2,1)S(1)}, bf16[2,32,1024]{2,1,0:T(8,128)(2,1)S(1)}, u32[]{:S(2)}, u32[]{:S(2)}) collective-permute-start(bf16[2,32,1024]{2,1,0:T(8,128)(2,1)S(1)} %get-tuple-element.195), channel_id=1, source_target_pairs={{0,16},{4,20},{8,24},{12,28},{16,0},{20,4},{24,8},{28,12},{1,17},{... | collective-permute-start | bytes 393224 | tf_op jit(solution)/shard_map/ppermute | solution.py:227
  90.0 5.9 %collective-permute-start.28 = (bf16[2,32,1024]{2,1,0:T(8,128)(2,1)S(1)}, bf16[2,32,1024]{2,1,0:T(8,128)(2,1)S(1)}, u32[]{:S(2)}, u32[]{:S(2)}) collective-permute-start(bf16[2,32,1024]{2,1,0:T(8,128)(2,1)S(1)} %get-tuple-element.193), channel_id=1, source_target_pairs={{0,24},{4,28},{8,16},{12,20},{16,8},{20,12},{24,0},{28,4},{1,25},{... | collective-permute-start | bytes 393224 | tf_op jit(solution)/shard_map/ppermute | solution.py:227
  93.3 9.7 %collective-permute-start.30 = (f16[3,32,1024]{2,1,0:T(8,128)(2,1)S(1)}, f16[3,32,1024]{2,1,0:T(8,128)(2,1)S(1)}, u32[]{:S(2)}, u32[]{:S(2)}) collective-permute-start(f16[3,32,1024]{2,1,0:T(8,128)(2,1)S(1)} %fusion.26), channel_id=1, source_target_pairs={{0,1},{1,2},{2,3},{3,0},{4,5},{5,6},{6,7},{7,4},{8,9},{9,10},{10,1... | collective-permute-start | bytes 589832 | tf_op jit(solution)/shard_map/ppermute | solution.py:230
  96.0 15.6 %collective-permute-start.35 = (bf16[8,32,1024]{2,1,0:T(8,128)(2,1)S(1)}, bf16[8,32,1024]{2,1,0:T(8,128)(2,1)S(1)}, u32[]{:S(2)}, u32[]{:S(2)}) collective-permute-start(bf16[8,32,1024]{2,1,0:T(8,128)(2,1)S(1)} %constant_dynamic-update-slice_fusion.refs_0_), channel_id=1, source_target_pairs={{0,1},{1,2},{2,3},{3,0},{4,5},{5,6},{6,7},{7,4},{8,9},{9,10},{10,1... | collective-permute-start | bytes 1572872 | tf_op jit(solution)/shard_map/ppermute | solution.py:230
  105.0 6.6 %collective-permute-start.32 = (bf16[2,32,1024]{2,1,0:T(8,128)(2,1)S(1)}, bf16[2,32,1024]{2,1,0:T(8,128)(2,1)S(1)}, u32[]{:S(2)}, u32[]{:S(2)}) collective-permute-start(bf16[2,32,1024]{2,1,0:T(8,128)(2,1)S(1)} %get-tuple-element.186), channel_id=1, source_target_pairs={{0,8},{4,12},{8,0},{12,4},{16,24},{20,28},{24,16},{28,20},{1,9},{5... | collective-permute-start | bytes 393224 | tf_op jit(solution)/shard_map/ppermute | solution.py:227
  105.1 6.5 %collective-permute-start.33 = (bf16[2,32,1024]{2,1,0:T(8,128)(2,1)S(1)}, bf16[2,32,1024]{2,1,0:T(8,128)(2,1)S(1)}, u32[]{:S(2)}, u32[]{:S(2)}) collective-permute-start(bf16[2,32,1024]{2,1,0:T(8,128)(2,1)S(1)} %get-tuple-element.187), channel_id=1, source_target_pairs={{0,16},{4,20},{8,24},{12,28},{16,0},{20,4},{24,8},{28,12},{1,17},{... | collective-permute-start | bytes 393224 | tf_op jit(solution)/shard_map/ppermute | solution.py:227
  107.0 7.3 %collective-permute-start.34 = (bf16[2,32,1024]{2,1,0:T(8,128)(2,1)S(1)}, bf16[2,32,1024]{2,1,0:T(8,128)(2,1)S(1)}, u32[]{:S(2)}, u32[]{:S(2)}) collective-permute-start(bf16[2,32,1024]{2,1,0:T(8,128)(2,1)S(1)} %get-tuple-element.185), channel_id=1, source_target_pairs={{0,24},{4,28},{8,16},{12,20},{16,8},{20,12},{24,0},{28,4},{1,25},{... | collective-permute-start | bytes 393224 | tf_op jit(solution)/shard_map/ppermute | solution.py:227
  111.6 16.7 %collective-permute-start.37 = (bf16[8,32,1024]{2,1,0:T(8,128)(2,1)S(1)}, bf16[8,32,1024]{2,1,0:T(8,128)(2,1)S(1)}, u32[]{:S(2)}, u32[]{:S(2)}) collective-permute-start(bf16[8,32,1024]{2,1,0:T(8,128)(2,1)S(1)} %collective-permute-done.35.refs_1_), channel_id=1, source_target_pairs={{0,1},{1,2},{2,3},{3,0},{4,5},{5,6},{6,7},{7,4},{8,9},{9,10},{10,1... | collective-permute-start | bytes 1572872 | tf_op jit(solution)/shard_map/ppermute | solution.py:230
  114.4 25.1 %collective-permute-start.36 = (bf16[8,32,1024]{2,1,0:T(8,128)(2,1)S(1)}, bf16[8,32,1024]{2,1,0:T(8,128)(2,1)S(1)}, u32[]{:S(2)}, u32[]{:S(2)}) collective-permute-start(bf16[8,32,1024]{2,1,0:T(8,128)(2,1)S(1)} %constant_dynamic-update-slice_fusion.4.refs_0_), channel_id=1, source_target_pairs={{0,1},{1,2},{2,3},{3,0},{4,5},{5,6},{6,7},{7,4},{8,9},{9,10},{10,1... | collective-permute-start | bytes 1572872 | tf_op jit(solution)/shard_map/ppermute | solution.py:230
  128.3 22.5 %collective-permute-start.39 = (bf16[8,32,1024]{2,1,0:T(8,128)(2,1)S(1)}, bf16[8,32,1024]{2,1,0:T(8,128)(2,1)S(1)}, u32[]{:S(2)}, u32[]{:S(2)}) collective-permute-start(bf16[8,32,1024]{2,1,0:T(8,128)(2,1)S(1)} %collective-permute-done.37.refs_2_), channel_id=1, source_target_pairs={{0,1},{1,2},{2,3},{3,0},{4,5},{5,6},{6,7},{7,4},{8,9},{9,10},{10,1... | collective-permute-start | bytes 1572872 | tf_op jit(solution)/shard_map/ppermute | solution.py:230
  139.5 18.9 %collective-permute-start.38 = (bf16[8,32,1024]{2,1,0:T(8,128)(2,1)S(1)}, bf16[8,32,1024]{2,1,0:T(8,128)(2,1)S(1)}, u32[]{:S(2)}, u32[]{:S(2)}) collective-permute-start(bf16[8,32,1024]{2,1,0:T(8,128)(2,1)S(1)} %collective-permute-done.36.refs_1_), channel_id=1, source_target_pairs={{0,1},{1,2},{2,3},{3,0},{4,5},{5,6},{6,7},{7,4},{8,9},{9,10},{10,1... | collective-permute-start | bytes 1572872 | tf_op jit(solution)/shard_map/ppermute | solution.py:230
  158.4 15.3 %collective-permute-start.41 = (bf16[8,32,1024]{2,1,0:T(8,128)(2,1)S(1)}, bf16[8,32,1024]{2,1,0:T(8,128)(2,1)S(1)}, u32[]{:S(2)}, u32[]{:S(2)}) collective-permute-start(bf16[8,32,1024]{2,1,0:T(8,128)(2,1)S(1)} %collective-permute-done.38.refs_2_), channel_id=1, source_target_pairs={{0,1},{1,2},{2,3},{3,0},{4,5},{5,6},{6,7},{7,4},{8,9},{9,10},{10,1... | collective-permute-start | bytes 1572872 | tf_op jit(solution)/shard_map/ppermute | solution.py:230
  158.5 4.5 %collective-permute-start.42 = (f32[32,640]{1,0:T(8,128)S(1)}, f32[32,640]{1,0:T(8,128)S(1)}, u32[]{:S(2)}, u32[]{:S(2)}) collective-permute-start(f32[32,640]{1,0:T(8,128)S(1)} %get-tuple-element.212), channel_id=1, source_target_pairs={{0,8},{4,12},{8,0},{12,4},{16,24},{20,28},{24,16},{28,20},{1,9},{5... | collective-permute-start | bytes 245768 | tf_op jit(solution)/shard_map/ppermute | solution.py:227
  160.5 5.0 %collective-permute-start.43 = (f32[32,640]{1,0:T(8,128)S(1)}, f32[32,640]{1,0:T(8,128)S(1)}, u32[]{:S(2)}, u32[]{:S(2)}) collective-permute-start(f32[32,640]{1,0:T(8,128)S(1)} %get-tuple-element.211), channel_id=1, source_target_pairs={{0,16},{4,20},{8,24},{12,28},{16,0},{20,4},{24,8},{28,12},{1,17},{... | collective-permute-start | bytes 245768 | tf_op jit(solution)/shard_map/ppermute | solution.py:227
  165.6 4.5 %collective-permute-start.44 = (f32[32,640]{1,0:T(8,128)S(1)}, f32[32,640]{1,0:T(8,128)S(1)}, u32[]{:S(2)}, u32[]{:S(2)}) collective-permute-start(f32[32,640]{1,0:T(8,128)S(1)} %get-tuple-element.210.first_top), channel_id=1, source_target_pairs={{0,16},{4,20},{8,24},{12,28},{16,0},{20,4},{24,8},{28,12},{1,17},{... | collective-permute-start | bytes 245768 | tf_op jit(solution)/shard_map/ppermute | solution.py:227
  165.9 4.4 %collective-permute-start.45 = (f32[32,640]{1,0:T(8,128)S(1)}, f32[32,640]{1,0:T(8,128)S(1)}, u32[]{:S(2)}, u32[]{:S(2)}) collective-permute-start(f32[32,640]{1,0:T(8,128)S(1)} %get-tuple-element.209.first_bottom), channel_id=1, source_target_pairs={{0,8},{4,12},{8,0},{12,4},{16,24},{20,28},{24,16},{28,20},{1,9},{5... | collective-permute-start | bytes 245768 | tf_op jit(solution)/shard_map/ppermute | solution.py:227
  178.4 4.6 %collective-permute-start.47 = (f32[32,640]{1,0:T(8,128)S(1)}, f32[32,640]{1,0:T(8,128)S(1)}, u32[]{:S(2)}, u32[]{:S(2)}) collective-permute-start(f32[32,640]{1,0:T(8,128)S(1)} %get-tuple-element.208), channel_id=1, source_target_pairs={{0,8},{4,12},{8,0},{12,4},{16,24},{20,28},{24,16},{28,20},{1,9},{5... | collective-permute-start | bytes 245768 | tf_op jit(solution)/shard_map/ppermute | solution.py:227
  179.6 4.4 %collective-permute-start.48 = (f32[32,640]{1,0:T(8,128)S(1)}, f32[32,640]{1,0:T(8,128)S(1)}, u32[]{:S(2)}, u32[]{:S(2)}) collective-permute-start(f32[32,640]{1,0:T(8,128)S(1)} %get-tuple-element.207), channel_id=1, source_target_pairs={{0,16},{4,20},{8,24},{12,28},{16,0},{20,4},{24,8},{28,12},{1,17},{... | collective-permute-start | bytes 245768 | tf_op jit(solution)/shard_map/ppermute | solution.py:227
  180.6 6.4 %collective-permute-start.51 = (f32[64,512]{1,0:T(8,128)S(1)}, f32[64,512]{1,0:T(8,128)S(1)}, u32[]{:S(2)}, u32[]{:S(2)}) collective-permute-start(f32[64,512]{1,0:T(8,128)S(1)} %solve.2.mine), channel_id=1, source_target_pairs={{0,4},{4,0},{8,12},{12,8},{16,20},{20,16},{24,28},{28,24},{1,5},{5... | collective-permute-start | bytes 393224 | tf_op jit(solution)/shard_map/ppermute | solution.py:227
  184.0 5.3 %collective-permute-start.49 = (f32[32,640]{1,0:T(8,128)S(1)}, f32[32,640]{1,0:T(8,128)S(1)}, u32[]{:S(2)}, u32[]{:S(2)}) collective-permute-start(f32[32,640]{1,0:T(8,128)S(1)} %get-tuple-element.206.first_top), channel_id=1, source_target_pairs={{0,16},{4,20},{8,24},{12,28},{16,0},{20,4},{24,8},{28,12},{1,17},{... | collective-permute-start | bytes 245768 | tf_op jit(solution)/shard_map/ppermute | solution.py:227
  185.1 4.4 %collective-permute-start.50 = (f32[32,640]{1,0:T(8,128)S(1)}, f32[32,640]{1,0:T(8,128)S(1)}, u32[]{:S(2)}, u32[]{:S(2)}) collective-permute-start(f32[32,640]{1,0:T(8,128)S(1)} %get-tuple-element.205.first_bottom), channel_id=1, source_target_pairs={{0,8},{4,12},{8,0},{12,4},{16,24},{20,28},{24,16},{28,20},{1,9},{5... | collective-permute-start | bytes 245768 | tf_op jit(solution)/shard_map/ppermute | solution.py:227
  (15 other events, 169.7 us)

commit v4 on v3

--- a/solution.py
+++ b/solution.py
@@ -284,7 +284,8 @@
     siblings = exchange(ordered, 1)
 
     row_peak = jnp.max(jnp.abs(chol_factor), axis=1).astype(jnp.float32)
-    vols, note = gate(factor_vol), None
+    siblings = mark(gate(siblings))
+    vols, row_peak = gate(factor_vol, row_peak)
     bit = 1
     while bit < fac_size:
         note = mark(jnp.concatenate([vols, row_peak]))

time: 197 us -> 194 us (0.985)
  waiting for transfers between devices: 112 us -> 109 us
    ppermute x30, waiting for transfers between devices: 30 us -> 24.4 us  [exchange(): lax.ppermute(x, 'path', [(i, i ^ far[i & 1]) for i in range(path_size)])]
    ppermute x21, starting transfers between devices: 10.7 us -> 12.8 us  [pass_on(): lax.ppermute(x, 'fac', [(i, (i + hops) % fac_size) for i in range(fac_siz...]
  transfers between devices with their start and end apart: 53 -> 53, of which waited for: 33 -> 36; matrix products, arithmetic and copies ran while one was open for 9% -> 9% of each run, Pallas kernels for 7% -> 7%
where the time goes in v4:
time: 194 us
  waiting for transfers between devices  109 us (56%)
  starting transfers between devices  43.2 us (22%)
  Pallas kernels  22.2 us (11%)
  matrix products  11.7 us (6%)
  other arithmetic  3.91 us (2%)
  local copies, waits for them, and re-layouts  3.05 us (2%)
    ppermute x21, waiting for transfers between devices, pass_on(): lax.ppermute(x, 'fac', [(i, (i + hops) % fac_size) for i in range(fac_siz...  82.7 us
    ppermute x30, starting transfers between devices, exchange(): lax.ppermute(x, 'path', [(i, i ^ far[i & 1]) for i in range(path_size)])  26.1 us
    ppermute x30, waiting for transfers between devices, exchange(): lax.ppermute(x, 'path', [(i, i ^ far[i & 1]) for i in range(path_size)])  24.4 us
    ppermute x21, starting transfers between devices, pass_on(): lax.ppermute(x, 'fac', [(i, (i + hops) % fac_size) for i in range(fac_siz...  12.8 us
    dot_general x7, matrix products, dot(): lax.dot_general(a, b, dims, precision=precision, preferred_element_type=j...  11.7 us
    pallas_call x2, Pallas kernels, solve(): pl.pallas_call(functools.partial(solve_kernel, ridge), out_shape=jax.Shap...  6.72 us
    pallas_call x2, Pallas kernels, price(): pl.pallas_call(price_kernel, in_specs=[pl.BlockSpec(memory_space=pltpu.SM...  6.36 us
    pallas_call x2, Pallas kernels, start_price(): pl.pallas_call(start_price_kernel, in_specs=[pl.BlockSpec(memory_space=pl...  4.62 us
  transfers between devices with their start and end apart: 53, of which 36 were waited for; matrix products, arithmetic and copies ran while one was open for 9% of the time, Pallas kernels for 7%

profile of v4, /device:TPU:0, one launch (start us, length us, event | category | flops | bytes accessed | tf_op | source)
XLA Modules:
  0.0 193.9 jit_solution(6048299245001592030)
XLA Ops:
  3.0 2.5 %collective-permute-start.4 = (bf16[128,2048]{1,0:T(8,128)(2,1)}, bf16[128,2048]{1,0:T(8,128)(2,1)S(1)}, u32[]{:S(2)}, u32[]{:S(2)}) collective-permute-start(bf16[128,2048]{1,0:T(8,128)(2,1)} %bitcast.8), channel_id=1, source_target_pairs={{0,8},{4,12},{8,0},{12,4},{16,24},{20,28},{24,16},{28,20},{1,9},{5... | collective-permute-start | bytes 1572872 | tf_op jit(solution)/shard_map/ppermute | solution.py:227
  8.0 1.6 collective-permute-start.1
  9.8 1.9 collective-permute-done.1
  11.7 2.7 %collective-permute-start.2 = (f32[5120]{0:T(1024)S(1)}, f32[5120]{0:T(1024)S(1)}, u32[]{:S(2)}, u32[]{:S(2)}) collective-permute-start(f32[5120]{0:T(1024)S(1)} %pad_maximum_fusion.14), channel_id=1, source_target_pairs={{0,2},{1,3},{2,0},{3,1},{4,6},{5,7},{6,4},{7,5},{8,10},{9,11},{10,... | collective-permute-start | bytes 61448 | tf_op jit(solution)/shard_map/ppermute | solution.py:293
  14.4 2.4 %fusion.6 = f32[4,4,32,1024]{3,2,1,0:T(8,128)S(1)} fusion(bf16[4,4,32,2048]{3,2,1,0:T(8,128)(2,1)S(1)} %bitcast.220, bf16[1024,2048]{1,0:T(8,128)(2,1)S(1)} %copy-done.1), kind=kOutput, calls=%fused_computation.6 | convolution fusion | flops 2147483648 | bytes 8388608 | tf_op jit(solution)/shard_map/dot_general | solution.py:20
  16.9 1.6 collective-permute-start.3
  20.0 1.6 collective-permute-start.7
  22.9 2.8 %collective-permute-done.3 = f16[4,32,1024]{2,1,0:T(8,128)(2,1)S(1)} collective-permute-done((f16[4,32,1024]{2,1,0:T(8,128)(2,1)S(1)}, f16[4,32,1024]{2,1,0:T(8,128)(2,1)S(1)}, u32[]{:S(2)}, u32[]{:S(2)}) %collective-permute-start.3) | collective-permute-done | bytes 262176 | tf_op jit(solution)/shard_map/ppermute | solution.py:230
  27.2 2.0 %collective-permute-done.7 = bf16[128,2048]{1,0:T(8,128)(2,1)S(1)} collective-permute-done((bf16[128,2048]{1,0:T(8,128)(2,1)S(1)}, bf16[128,2048]{1,0:T(8,128)(2,1)S(1)}, u32[]{:S(2)}, u32[]{:S(2)}) %collective-permute-start.7) | collective-permute-done | bytes 524320 | tf_op jit(solution)/shard_map/ppermute | solution.py:227
  30.9 1.6 collective-permute-start.10
  34.7 1.6 collective-permute-start.9
  36.4 1.6 fusion.9
  38.1 1.6 collective-permute-start.13
  40.6 5.5 %collective-permute-done.9 = f16[4,32,1024]{2,1,0:T(8,128)(2,1)S(1)} collective-permute-done((f16[4,32,1024]{2,1,0:T(8,128)(2,1)S(1)}, f16[4,32,1024]{2,1,0:T(8,128)(2,1)S(1)}, u32[]{:S(2)}, u32[]{:S(2)}) %collective-permute-start.9) | collective-permute-done | bytes 262176 | tf_op jit(solution)/shard_map/ppermute | solution.py:230
  46.9 1.6 collective-permute-start.17
  48.5 1.8 collective-permute-done.13
  50.4 3.7 %collective-permute-done.12 = f16[3,32,1024]{2,1,0:T(8,128)(2,1)S(1)} collective-permute-done((f16[3,32,1024]{2,1,0:T(8,128)(2,1)S(1)}, f16[3,32,1024]{2,1,0:T(8,128)(2,1)S(1)}, u32[]{:S(2)}, u32[]{:S(2)}) %collective-permute-start.12) | collective-permute-done | bytes 196640 | tf_op jit(solution)/shard_map/ppermute | solution.py:230
  54.3 4.2 %collective-permute-done.18 = f16[3,32,1024]{2,1,0:T(8,128)(2,1)S(1)} collective-permute-done((f16[3,32,1024]{2,1,0:T(8,128)(2,1)S(1)}, f16[3,32,1024]{2,1,0:T(8,128)(2,1)S(1)}, u32[]{:S(2)}, u32[]{:S(2)}) %collective-permute-start.18) | collective-permute-done | bytes 196640 | tf_op jit(solution)/shard_map/ppermute | solution.py:230
  60.2 1.8 convolution_multiply_fusion.1
  62.2 1.6 collective-permute-start.19
  63.8 1.9 convolution_multiply_fusion
  65.9 2.2 %collective-permute-start.22 = (f16[3,32,1024]{2,1,0:T(8,128)(2,1)S(1)}, f16[3,32,1024]{2,1,0:T(8,128)(2,1)S(1)}, u32[]{:S(2)}, u32[]{:S(2)}) collective-permute-start(f16[3,32,1024]{2,1,0:T(8,128)(2,1)S(1)} %fusion.62), channel_id=1, source_target_pairs={{0,1},{1,2},{2,3},{3,0},{4,5},{5,6},{6,7},{7,4},{8,9},{9,10},{10,1... | collective-permute-start | bytes 589832 | tf_op jit(solution)/shard_map/ppermute | solution.py:230
  68.1 8.9 %collective-permute-done.19 = f16[3,32,1024]{2,1,0:T(8,128)(2,1)S(1)} collective-permute-done((f16[3,32,1024]{2,1,0:T(8,128)(2,1)S(1)}, f16[3,32,1024]{2,1,0:T(8,128)(2,1)S(1)}, u32[]{:S(2)}, u32[]{:S(2)}) %collective-permute-start.19) | collective-permute-done | bytes 196640 | tf_op jit(solution)/shard_map/ppermute | solution.py:230
  77.6 3.1 %collective-permute-done.22 = f16[3,32,1024]{2,1,0:T(8,128)(2,1)S(1)} collective-permute-done((f16[3,32,1024]{2,1,0:T(8,128)(2,1)S(1)}, f16[3,32,1024]{2,1,0:T(8,128)(2,1)S(1)}, u32[]{:S(2)}, u32[]{:S(2)}) %collective-permute-start.22) | collective-permute-done | bytes 196640 | tf_op jit(solution)/shard_map/ppermute | solution.py:230
  80.9 4.1 %collective-permute-done.21 = f16[3,32,1024]{2,1,0:T(8,128)(2,1)S(1)} collective-permute-done((f16[3,32,1024]{2,1,0:T(8,128)(2,1)S(1)}, f16[3,32,1024]{2,1,0:T(8,128)(2,1)S(1)}, u32[]{:S(2)}, u32[]{:S(2)}) %collective-permute-start.21) | collective-permute-done | bytes 196640 | tf_op jit(solution)/shard_map/ppermute | solution.py:230
  88.7 1.8 collective-permute-done.29
  91.4 1.8 collective-permute-done.28
  94.3 5.9 %collective-permute-done.30 = f16[3,32,1024]{2,1,0:T(8,128)(2,1)S(1)} collective-permute-done((f16[3,32,1024]{2,1,0:T(8,128)(2,1)S(1)}, f16[3,32,1024]{2,1,0:T(8,128)(2,1)S(1)}, u32[]{:S(2)}, u32[]{:S(2)}) %collective-permute-start.30) | collective-permute-done | bytes 196640 | tf_op jit(solution)/shard_map/ppermute | solution.py:230
  102.3 2.0 %collective-permute-start.33 = (bf16[2,32,1024]{2,1,0:T(8,128)(2,1)S(1)}, bf16[2,32,1024]{2,1,0:T(8,128)(2,1)S(1)}, u32[]{:S(2)}, u32[]{:S(2)}) collective-permute-start(bf16[2,32,1024]{2,1,0:T(8,128)(2,1)S(1)} %get-tuple-element.191), channel_id=1, source_target_pairs={{0,16},{4,20},{8,24},{12,28},{16,0},{20,4},{24,8},{28,12},{1,17},{... | collective-permute-start | bytes 393224 | tf_op jit(solution)/shard_map/ppermute | solution.py:227
  105.8 3.1 %collective-permute-done.35.refs_1_ = bf16[8,32,1024]{2,1,0:T(8,128)(2,1)S(1)} collective-permute-done((bf16[8,32,1024]{2,1,0:T(8,128)(2,1)S(1)}, bf16[8,32,1024]{2,1,0:T(8,128)(2,1)S(1)}, u32[]{:S(2)}, u32[]{:S(2)}) %collective-permute-start.35) | collective-permute-done | bytes 524320 | tf_op jit(solution)/shard_map/ppermute | solution.py:230
  108.8 2.8 %collective-permute-done.34 = bf16[2,32,1024]{2,1,0:T(8,128)(2,1)S(1)} collective-permute-done((bf16[2,32,1024]{2,1,0:T(8,128)(2,1)S(1)}, bf16[2,32,1024]{2,1,0:T(8,128)(2,1)S(1)}, u32[]{:S(2)}, u32[]{:S(2)}) %collective-permute-start.34) | collective-permute-done | bytes 131104 | tf_op jit(solution)/shard_map/ppermute | solution.py:227
  111.7 13.7 %collective-permute-done.37.refs_2_ = bf16[8,32,1024]{2,1,0:T(8,128)(2,1)S(1)} collective-permute-done((bf16[8,32,1024]{2,1,0:T(8,128)(2,1)S(1)}, bf16[8,32,1024]{2,1,0:T(8,128)(2,1)S(1)}, u32[]{:S(2)}, u32[]{:S(2)}) %collective-permute-start.37) | collective-permute-done | bytes 524320 | tf_op jit(solution)/shard_map/ppermute | solution.py:230
  125.5 11.2 %collective-permute-done.36.refs_1_ = bf16[8,32,1024]{2,1,0:T(8,128)(2,1)S(1)} collective-permute-done((bf16[8,32,1024]{2,1,0:T(8,128)(2,1)S(1)}, bf16[8,32,1024]{2,1,0:T(8,128)(2,1)S(1)}, u32[]{:S(2)}, u32[]{:S(2)}) %collective-permute-start.36) | collective-permute-done | bytes 524320 | tf_op jit(solution)/shard_map/ppermute | solution.py:230
  136.9 2.3 %start_price.2 = (f32[96,512]{1,0:T(8,128)S(1)}, f32[96,64]{1,0:T(8,128)S(1)}) custom-call(s32[10]{0:T(128)S(1)} %pad_add_fusion.place, bf16[8,32,1024]{2,1,0:T(8,128)(2,1)S(1)} %constant_dynamic-update-slice_fusion.1.refs_0_, bf16[8,32,1024]{2,1,0:T(8,128)(2,1)S(1)} %collective-permute-done.35.refs_1_, ...), custom_call_target="tpu_custom_call" | custom-call | flops 905969664 | bytes 9961472 | tf_op jit(solution)/shard_map/start_price/pallas_call | solution.py:74
  139.3 8.7 %collective-permute-done.39.piece = bf16[8,32,1024]{2,1,0:T(8,128)(2,1)S(1)} collective-permute-done((bf16[8,32,1024]{2,1,0:T(8,128)(2,1)S(1)}, bf16[8,32,1024]{2,1,0:T(8,128)(2,1)S(1)}, u32[]{:S(2)}, u32[]{:S(2)}) %collective-permute-start.39) | collective-permute-done | bytes 524320 | tf_op jit(solution)/shard_map/ppermute | solution.py:230
  148.0 3.2 %price.2 = (f32[64,640]{1,0:T(8,128)S(1)}, f32[64,640]{1,0:T(8,128)S(1)}, f32[2,64,64]{2,1,0:T(8,128)S(1)}) custom-call(s32[10]{0:T(128)S(1)} %pad_add_fusion.place, bf16[8,32,1024]{2,1,0:T(8,128)(2,1)S(1)} %collective-permute-done.39.piece, bf16[8,1024,512]{2,1,0:T(8,128)(2,1)S(1)} %bitcast.210, bf16[8,64,1024]{2,1,0:T(8,128)(2,1)S(1)} %bitcast.214, ...), custom_call_target="tpu_custom_call" | custom-call | flops 301989888 | bytes 8912896 | tf_op jit(solution)/shard_map/price/pallas_call | solution.py:97
  152.6 3.0 %collective-permute-done.38.refs_2_ = bf16[8,32,1024]{2,1,0:T(8,128)(2,1)S(1)} collective-permute-done((bf16[8,32,1024]{2,1,0:T(8,128)(2,1)S(1)}, bf16[8,32,1024]{2,1,0:T(8,128)(2,1)S(1)}, u32[]{:S(2)}, u32[]{:S(2)}) %collective-permute-start.38) | collective-permute-done | bytes 524320 | tf_op jit(solution)/shard_map/ppermute | solution.py:230
  155.7 2.2 %collective-permute-start.42 = (f32[32,640]{1,0:T(8,128)S(1)}, f32[32,640]{1,0:T(8,128)S(1)}, u32[]{:S(2)}, u32[]{:S(2)}) collective-permute-start(f32[32,640]{1,0:T(8,128)S(1)} %get-tuple-element.216), channel_id=1, source_target_pairs={{0,8},{4,12},{8,0},{12,4},{16,24},{20,28},{24,16},{28,20},{1,9},{5... | collective-permute-start | bytes 245768 | tf_op jit(solution)/shard_map/ppermute | solution.py:227
  158.2 2.2 %collective-permute-done.42 = f32[32,640]{1,0:T(8,128)S(1)} collective-permute-done((f32[32,640]{1,0:T(8,128)S(1)}, f32[32,640]{1,0:T(8,128)S(1)}, u32[]{:S(2)}, u32[]{:S(2)}) %collective-permute-start.42) | collective-permute-done | bytes 81952 | tf_op jit(solution)/shard_map/ppermute | solution.py:227
  160.3 2.7 %collective-permute-done.43 = f32[32,640]{1,0:T(8,128)S(1)} collective-permute-done((f32[32,640]{1,0:T(8,128)S(1)}, f32[32,640]{1,0:T(8,128)S(1)}, u32[]{:S(2)}, u32[]{:S(2)}) %collective-permute-start.43) | collective-permute-done | bytes 81952 | tf_op jit(solution)/shard_map/ppermute | solution.py:227
  164.2 2.3 %start_price.3 = (f32[96,512]{1,0:T(8,128)S(1)}, f32[96,64]{1,0:T(8,128)S(1)}) custom-call(s32[10]{0:T(128)S(1)} %pad_add_fusion.place, bf16[8,32,1024]{2,1,0:T(8,128)(2,1)S(1)} %constant_dynamic-update-slice_fusion.5.refs_0_, bf16[8,32,1024]{2,1,0:T(8,128)(2,1)S(1)} %collective-permute-done.36.refs_1_, ...), custom_call_target="tpu_custom_call" | custom-call | flops 905969664 | bytes 9961472 | tf_op jit(solution)/shard_map/start_price/pallas_call | solution.py:74
  167.8 3.4 %solve.2.mine = f32[64,512]{1,0:T(8,128)S(1)} custom-call(f32[32,640]{1,0:T(8,128)S(1)} %get-tuple-element.214.first_top, f32[32,640]{1,0:T(8,128)S(1)} %get-tuple-element.213.first_bottom, f32[32,640]{1,0:T(8,128)S(1)} %collective-permute-done.44.second_top, f32[32,640]{1,0:T(8,128)S(1)} %collective-permute-done.45.second_bottom), custom_call_target="tpu_custom_call" | custom-call | flops 25690112 | bytes 393216 | tf_op jit(solution)/shard_map/solve/pallas_call | solution.py:139
  171.2 3.2 %price.3 = (f32[64,640]{1,0:T(8,128)S(1)}, f32[64,640]{1,0:T(8,128)S(1)}, f32[2,64,64]{2,1,0:T(8,128)S(1)}) custom-call(s32[10]{0:T(128)S(1)} %pad_add_fusion.place, bf16[8,32,1024]{2,1,0:T(8,128)(2,1)S(1)} %collective-permute-done.41.piece, bf16[8,1024,512]{2,1,0:T(8,128)(2,1)S(1)} %bitcast.212, bf16[8,64,1024]{2,1,0:T(8,128)(2,1)S(1)} %bitcast.216, ...), custom_call_target="tpu_custom_call" | custom-call | flops 301989888 | bytes 8912896 | tf_op jit(solution)/shard_map/price/pallas_call | solution.py:97
  178.0 2.5 %collective-permute-done.47 = f32[32,640]{1,0:T(8,128)S(1)} collective-permute-done((f32[32,640]{1,0:T(8,128)S(1)}, f32[32,640]{1,0:T(8,128)S(1)}, u32[]{:S(2)}, u32[]{:S(2)}) %collective-permute-start.47) | collective-permute-done | bytes 81952 | tf_op jit(solution)/shard_map/ppermute | solution.py:227
  182.4 1.8 collective-permute-start.50
  184.5 2.2 %expose.2.refs_0_ = f32[4,64,1024]{2,1,0:T(8,128)} custom-call(s32[10]{0:T(128)S(1)} %pad_add_fusion.place, f32[2,64,64]{2,1,0:T(8,128)S(1)} %get-tuple-element.152.basis, f32[64,512]{1,0:T(8,128)S(1)} %solve.2.mine, f32[64,512]{1,0:T(8,128)S(1)} %collective-permute-done.51.other, bf16[512,1024]{1,0:T(8,128)(2,1)S(1)} %fusion.8.member), custom_call_target="tpu_custom_call" | custom-call | flops 402653184 | bytes 1048576 | tf_op jit(solution)/shard_map/expose/pallas_call | solution.py:185
  186.9 3.4 %solve.3.mine = f32[64,512]{1,0:T(8,128)S(1)} custom-call(f32[32,640]{1,0:T(8,128)S(1)} %get-tuple-element.210.first_top, f32[32,640]{1,0:T(8,128)S(1)} %get-tuple-element.209.first_bottom, f32[32,640]{1,0:T(8,128)S(1)} %collective-permute-done.49.second_top, f32[32,640]{1,0:T(8,128)S(1)} %collective-permute-done.50.second_bottom), custom_call_target="tpu_custom_call" | custom-call | flops 25690112 | bytes 393216 | tf_op jit(solution)/shard_map/solve/pallas_call | solution.py:139
  191.7 2.2 %expose.3 = f32[4,64,1024]{2,1,0:T(8,128)} custom-call(s32[10]{0:T(128)S(1)} %pad_add_fusion.place, f32[2,64,64]{2,1,0:T(8,128)S(1)} %get-tuple-element.146.basis, f32[64,512]{1,0:T(8,128)S(1)} %solve.3.mine, f32[64,512]{1,0:T(8,128)S(1)} %collective-permute-done.52.other, bf16[512,1024]{1,0:T(8,128)(2,1)S(1)} %fusion.8.member, ...), custom_call_target="tpu_custom_call", output_to_operand_aliasing={{}: (5, {})} | custom-call | flops 402653184 | bytes 1048576 | tf_op jit(solution)/shard_map/expose/pallas_call | solution.py:185
  (169 shorter events, 39.5 us)
Async XLA Ops:
  1.4 6.5 %collective-permute-start = (bf16[2,128,2048]{2,1,0:T(8,128)(2,1)S(1)}, bf16[2,128,2048]{2,1,0:T(8,128)(2,1)S(1)}, u32[]{:S(2)}, u32[]{:S(2)}) collective-permute-start(bf16[2,128,2048]{2,1,0:T(8,128)(2,1)S(1)} %bitcast.217), channel_id=1, source_target_pairs={{0,4},{4,0},{8,12},{12,8},{16,20},{20,16},{24,28},{28,24},{1,5},{5... | collective-permute-start | bytes 3145736 | tf_op jit(solution)/shard_map/ppermute | solution.py:227
  3.0 15.5 %collective-permute-start.4 = (bf16[128,2048]{1,0:T(8,128)(2,1)}, bf16[128,2048]{1,0:T(8,128)(2,1)S(1)}, u32[]{:S(2)}, u32[]{:S(2)}) collective-permute-start(bf16[128,2048]{1,0:T(8,128)(2,1)} %bitcast.8), channel_id=1, source_target_pairs={{0,8},{4,12},{8,0},{12,4},{16,24},{20,28},{24,16},{28,20},{1,9},{5... | collective-permute-start | bytes 1572872 | tf_op jit(solution)/shard_map/ppermute | solution.py:227
  5.5 14.3 %collective-permute-start.5 = (bf16[128,2048]{1,0:T(8,128)(2,1)}, bf16[128,2048]{1,0:T(8,128)(2,1)S(1)}, u32[]{:S(2)}, u32[]{:S(2)}) collective-permute-start(bf16[128,2048]{1,0:T(8,128)(2,1)} %bitcast.8), channel_id=1, source_target_pairs={{0,16},{4,20},{8,24},{12,28},{16,0},{20,4},{24,8},{28,12},{1,17},{... | collective-permute-start | bytes 1572872 | tf_op jit(solution)/shard_map/ppermute | solution.py:227
  11.7 5.0 %collective-permute-start.2 = (f32[5120]{0:T(1024)S(1)}, f32[5120]{0:T(1024)S(1)}, u32[]{:S(2)}, u32[]{:S(2)}) collective-permute-start(f32[5120]{0:T(1024)S(1)} %pad_maximum_fusion.14), channel_id=1, source_target_pairs={{0,2},{1,3},{2,0},{3,1},{4,6},{5,7},{6,4},{7,5},{8,10},{9,11},{10,... | collective-permute-start | bytes 61448 | tf_op jit(solution)/shard_map/ppermute | solution.py:293
  16.9 8.9 %collective-permute-start.3 = (f16[4,32,1024]{2,1,0:T(8,128)(2,1)S(1)}, f16[4,32,1024]{2,1,0:T(8,128)(2,1)S(1)}, u32[]{:S(2)}, u32[]{:S(2)}) collective-permute-start(f16[4,32,1024]{2,1,0:T(8,128)(2,1)S(1)} %fusion.16), channel_id=1, source_target_pairs={{0,1},{1,2},{2,3},{3,0},{4,5},{5,6},{6,7},{7,4},{8,9},{9,10},{10,1... | collective-permute-start | bytes 786440 | tf_op jit(solution)/shard_map/ppermute | solution.py:230
  19.8 6.1 %collective-permute-start.8 = (bf16[2,128,2048]{2,1,0:T(8,128)(2,1)S(1)}, bf16[2,128,2048]{2,1,0:T(8,128)(2,1)S(1)}, u32[]{:S(2)}, u32[]{:S(2)}) collective-permute-start(bf16[2,128,2048]{2,1,0:T(8,128)(2,1)S(1)} %pad_maximum_fusion.3), channel_id=1, source_target_pairs={{0,4},{4,0},{8,12},{12,8},{16,20},{20,16},{24,28},{28,24},{1,5},{5... | collective-permute-start | bytes 3145736 | tf_op jit(solution)/shard_map/ppermute | solution.py:227
  20.0 9.2 %collective-permute-start.7 = (bf16[128,2048]{1,0:T(8,128)(2,1)S(1)}, bf16[128,2048]{1,0:T(8,128)(2,1)S(1)}, u32[]{:S(2)}, u32[]{:S(2)}) collective-permute-start(bf16[128,2048]{1,0:T(8,128)(2,1)S(1)} %broadcast_select_fusion.1), channel_id=1, source_target_pairs={{0,16},{4,12},{8,24},{12,4},{16,0},{20,28},{24,8},{28,20},{1,17},{... | collective-permute-start | bytes 1572872 | tf_op jit(solution)/shard_map/ppermute | solution.py:227
  25.8 8.8 %collective-permute-start.6 = (f16[4,32,1024]{2,1,0:T(8,128)(2,1)S(1)}, f16[4,32,1024]{2,1,0:T(8,128)(2,1)S(1)}, u32[]{:S(2)}, u32[]{:S(2)}) collective-permute-start(f16[4,32,1024]{2,1,0:T(8,128)(2,1)S(1)} %fusion.19), channel_id=1, source_target_pairs={{0,1},{1,2},{2,3},{3,0},{4,5},{5,6},{6,7},{7,4},{8,9},{9,10},{10,1... | collective-permute-start | bytes 786440 | tf_op jit(solution)/shard_map/ppermute | solution.py:230
  30.8 5.6 %collective-permute-start.11 = (bf16[1,128,2048]{2,1,0:T(8,128)(2,1)S(1)}, bf16[1,128,2048]{2,1,0:T(8,128)(2,1)S(1)}, u32[]{:S(2)}, u32[]{:S(2)}) collective-permute-start(bf16[1,128,2048]{2,1,0:T(8,128)(2,1)S(1)} %bitcast.241), channel_id=1, source_target_pairs={{0,4},{4,0},{8,12},{12,8},{16,20},{20,16},{24,28},{28,24},{1,5},{5... | collective-permute-start | bytes 1572872 | tf_op jit(solution)/shard_map/ppermute | solution.py:227
  30.9 9.5 %collective-permute-start.10 = (f16[3,32,1024]{2,1,0:T(8,128)(2,1)S(1)}, f16[3,32,1024]{2,1,0:T(8,128)(2,1)S(1)}, u32[]{:S(2)}, u32[]{:S(2)}) collective-permute-start(f16[3,32,1024]{2,1,0:T(8,128)(2,1)S(1)} %fusion.35), channel_id=1, source_target_pairs={{0,1},{1,2},{2,3},{3,0},{4,5},{5,6},{6,7},{7,4},{8,9},{9,10},{10,1... | collective-permute-start | bytes 589832 | tf_op jit(solution)/shard_map/ppermute | solution.py:230
  32.6 14.0 %collective-permute-start.14 = (bf16[128,2048]{1,0:T(8,128)(2,1)S(1)}, bf16[128,2048]{1,0:T(8,128)(2,1)S(1)}, u32[]{:S(2)}, u32[]{:S(2)}) collective-permute-start(bf16[128,2048]{1,0:T(8,128)(2,1)S(1)} %bitcast.242), channel_id=1, source_target_pairs={{0,8},{4,12},{8,0},{12,4},{16,24},{20,28},{24,16},{28,20},{1,9},{5... | collective-permute-start | bytes 1572872 | tf_op jit(solution)/shard_map/ppermute | solution.py:227
  33.1 13.8 %collective-permute-start.15 = (bf16[128,2048]{1,0:T(8,128)(2,1)S(1)}, bf16[128,2048]{1,0:T(8,128)(2,1)S(1)}, u32[]{:S(2)}, u32[]{:S(2)}) collective-permute-start(bf16[128,2048]{1,0:T(8,128)(2,1)S(1)} %bitcast.243), channel_id=1, source_target_pairs={{0,16},{4,20},{8,24},{12,28},{16,0},{20,4},{24,8},{28,12},{1,17},{... | collective-permute-start | bytes 1572872 | tf_op jit(solution)/shard_map/ppermute | solution.py:227
  34.7 11.4 %collective-permute-start.9 = (f16[4,32,1024]{2,1,0:T(8,128)(2,1)S(1)}, f16[4,32,1024]{2,1,0:T(8,128)(2,1)S(1)}, u32[]{:S(2)}, u32[]{:S(2)}) collective-permute-start(f16[4,32,1024]{2,1,0:T(8,128)(2,1)S(1)} %fusion.22), channel_id=1, source_target_pairs={{0,1},{1,2},{2,3},{3,0},{4,5},{5,6},{6,7},{7,4},{8,9},{9,10},{10,1... | collective-permute-start | bytes 786440 | tf_op jit(solution)/shard_map/ppermute | solution.py:230
  38.1 12.2 %collective-permute-start.13 = (f16[3,32,1024]{2,1,0:T(8,128)(2,1)S(1)}, f16[3,32,1024]{2,1,0:T(8,128)(2,1)S(1)}, u32[]{:S(2)}, u32[]{:S(2)}) collective-permute-start(f16[3,32,1024]{2,1,0:T(8,128)(2,1)S(1)} %fusion.38), channel_id=1, source_target_pairs={{0,1},{1,2},{2,3},{3,0},{4,5},{5,6},{6,7},{7,4},{8,9},{9,10},{10,1... | collective-permute-start | bytes 589832 | tf_op jit(solution)/shard_map/ppermute | solution.py:230
  40.5 13.6 %collective-permute-start.12 = (f16[3,32,1024]{2,1,0:T(8,128)(2,1)S(1)}, f16[3,32,1024]{2,1,0:T(8,128)(2,1)S(1)}, u32[]{:S(2)}, u32[]{:S(2)}) collective-permute-start(f16[3,32,1024]{2,1,0:T(8,128)(2,1)S(1)} %fusion.37), channel_id=1, source_target_pairs={{0,1},{1,2},{2,3},{3,0},{4,5},{5,6},{6,7},{7,4},{8,9},{9,10},{10,1... | collective-permute-start | bytes 589832 | tf_op jit(solution)/shard_map/ppermute | solution.py:230
  46.9 11.7 %collective-permute-start.17 = (bf16[128,2048]{1,0:T(8,128)(2,1)S(1)}, bf16[128,2048]{1,0:T(8,128)(2,1)S(1)}, u32[]{:S(2)}, u32[]{:S(2)}) collective-permute-start(bf16[128,2048]{1,0:T(8,128)(2,1)S(1)} %broadcast_select_fusion), channel_id=1, source_target_pairs={{0,16},{4,12},{8,24},{12,4},{16,0},{20,28},{24,8},{28,20},{1,17},{... | collective-permute-start | bytes 1572872 | tf_op jit(solution)/shard_map/ppermute | solution.py:227
  50.4 8.1 %collective-permute-start.18 = (f16[3,32,1024]{2,1,0:T(8,128)(2,1)S(1)}, f16[3,32,1024]{2,1,0:T(8,128)(2,1)S(1)}, u32[]{:S(2)}, u32[]{:S(2)}) collective-permute-start(f16[3,32,1024]{2,1,0:T(8,128)(2,1)S(1)} %fusion.43), channel_id=1, source_target_pairs={{0,1},{1,2},{2,3},{3,0},{4,5},{5,6},{6,7},{7,4},{8,9},{9,10},{10,1... | collective-permute-start | bytes 589832 | tf_op jit(solution)/shard_map/ppermute | solution.py:230
  58.8 5.1 %collective-permute-start.20 = (bf16[3,128,2048]{2,1,0:T(8,128)(2,1)S(1)}, bf16[3,128,2048]{2,1,0:T(8,128)(2,1)S(1)}, u32[]{:S(2)}, u32[]{:S(2)}) collective-permute-start(bf16[3,128,2048]{2,1,0:T(8,128)(2,1)S(1)} %pad_maximum_fusion.1), channel_id=1, source_target_pairs={{0,4},{4,0},{8,12},{12,8},{16,20},{20,16},{24,28},{28,24},{1,5},{5... | collective-permute-start | bytes 4718600 | tf_op jit(solution)/shard_map/ppermute | solution.py:227
  59.0 18.1 %collective-permute-start.16 = (f16[3,32,1024]{2,1,0:T(8,128)(2,1)S(1)}, f16[3,32,1024]{2,1,0:T(8,128)(2,1)S(1)}, u32[]{:S(2)}, u32[]{:S(2)}) collective-permute-start(f16[3,32,1024]{2,1,0:T(8,128)(2,1)S(1)} %fusion.41), channel_id=1, source_target_pairs={{0,1},{1,2},{2,3},{3,0},{4,5},{5,6},{6,7},{7,4},{8,9},{9,10},{10,1... | collective-permute-start | bytes 589832 | tf_op jit(solution)/shard_map/ppermute | solution.py:230
  59.0 18.1 %collective-permute-start.23 = (f16[3,32,1024]{2,1,0:T(8,128)(2,1)S(1)}, f16[3,32,1024]{2,1,0:T(8,128)(2,1)S(1)}, u32[]{:S(2)}, u32[]{:S(2)}) collective-permute-start(f16[3,32,1024]{2,1,0:T(8,128)(2,1)S(1)} %fusion.45), channel_id=1, source_target_pairs={{0,1},{1,2},{2,3},{3,0},{4,5},{5,6},{6,7},{7,4},{8,9},{9,10},{10,1... | collective-permute-start | bytes 589832 | tf_op jit(solution)/shard_map/ppermute | solution.py:230
  62.2 14.8 %collective-permute-start.19 = (f16[3,32,1024]{2,1,0:T(8,128)(2,1)S(1)}, f16[3,32,1024]{2,1,0:T(8,128)(2,1)S(1)}, u32[]{:S(2)}, u32[]{:S(2)}) collective-permute-start(f16[3,32,1024]{2,1,0:T(8,128)(2,1)S(1)} %fusion.61), channel_id=1, source_target_pairs={{0,1},{1,2},{2,3},{3,0},{4,5},{5,6},{6,7},{7,4},{8,9},{9,10},{10,1... | collective-permute-start | bytes 589832 | tf_op jit(solution)/shard_map/ppermute | solution.py:230
  65.9 14.9 %collective-permute-start.22 = (f16[3,32,1024]{2,1,0:T(8,128)(2,1)S(1)}, f16[3,32,1024]{2,1,0:T(8,128)(2,1)S(1)}, u32[]{:S(2)}, u32[]{:S(2)}) collective-permute-start(f16[3,32,1024]{2,1,0:T(8,128)(2,1)S(1)} %fusion.62), channel_id=1, source_target_pairs={{0,1},{1,2},{2,3},{3,0},{4,5},{5,6},{6,7},{7,4},{8,9},{9,10},{10,1... | collective-permute-start | bytes 589832 | tf_op jit(solution)/shard_map/ppermute | solution.py:230
  77.0 7.9 %collective-permute-start.21 = (f16[3,32,1024]{2,1,0:T(8,128)(2,1)S(1)}, f16[3,32,1024]{2,1,0:T(8,128)(2,1)S(1)}, u32[]{:S(2)}, u32[]{:S(2)}) collective-permute-start(f16[3,32,1024]{2,1,0:T(8,128)(2,1)S(1)} %fusion.31), channel_id=1, source_target_pairs={{0,1},{1,2},{2,3},{3,0},{4,5},{5,6},{6,7},{7,4},{8,9},{9,10},{10,1... | collective-permute-start | bytes 589832 | tf_op jit(solution)/shard_map/ppermute | solution.py:230
  77.5 7.6 %collective-permute-start.24 = (bf16[4,32,1024]{2,1,0:T(8,128)(2,1)S(1)}, bf16[4,32,1024]{2,1,0:T(8,128)(2,1)S(1)}, u32[]{:S(2)}, u32[]{:S(2)}) collective-permute-start(bf16[4,32,1024]{2,1,0:T(8,128)(2,1)S(1)} %bitcast.245), channel_id=1, source_target_pairs={{0,4},{4,0},{8,12},{12,8},{16,20},{20,16},{24,28},{28,24},{1,5},{5... | collective-permute-start | bytes 786440 | tf_op jit(solution)/shard_map/ppermute | solution.py:227
  80.8 9.7 %collective-permute-start.29 = (f16[3,32,1024]{2,1,0:T(8,128)(2,1)S(1)}, f16[3,32,1024]{2,1,0:T(8,128)(2,1)S(1)}, u32[]{:S(2)}, u32[]{:S(2)}) collective-permute-start(f16[3,32,1024]{2,1,0:T(8,128)(2,1)S(1)} %fusion.28), channel_id=1, source_target_pairs={{0,1},{1,2},{2,3},{3,0},{4,5},{5,6},{6,7},{7,4},{8,9},{9,10},{10,1... | collective-permute-start | bytes 589832 | tf_op jit(solution)/shard_map/ppermute | solution.py:230
  85.0 9.2 %collective-permute-start.25 = (f16[3,32,1024]{2,1,0:T(8,128)(2,1)S(1)}, f16[3,32,1024]{2,1,0:T(8,128)(2,1)S(1)}, u32[]{:S(2)}, u32[]{:S(2)}) collective-permute-start(f16[3,32,1024]{2,1,0:T(8,128)(2,1)S(1)} %fusion.34), channel_id=1, source_target_pairs={{0,1},{1,2},{2,3},{3,0},{4,5},{5,6},{6,7},{7,4},{8,9},{9,10},{10,1... | collective-permute-start | bytes 589832 | tf_op jit(solution)/shard_map/ppermute | solution.py:230
  85.2 5.4 %collective-permute-start.26 = (bf16[2,32,1024]{2,1,0:T(8,128)(2,1)S(1)}, bf16[2,32,1024]{2,1,0:T(8,128)(2,1)S(1)}, u32[]{:S(2)}, u32[]{:S(2)}) collective-permute-start(bf16[2,32,1024]{2,1,0:T(8,128)(2,1)S(1)} %get-tuple-element.198), channel_id=1, source_target_pairs={{0,8},{4,12},{8,0},{12,4},{16,24},{20,28},{24,16},{28,20},{1,9},{5... | collective-permute-start | bytes 393224 | tf_op jit(solution)/shard_map/ppermute | solution.py:227
  85.8 5.5 %collective-permute-start.27 = (bf16[2,32,1024]{2,1,0:T(8,128)(2,1)S(1)}, bf16[2,32,1024]{2,1,0:T(8,128)(2,1)S(1)}, u32[]{:S(2)}, u32[]{:S(2)}) collective-permute-start(bf16[2,32,1024]{2,1,0:T(8,128)(2,1)S(1)} %get-tuple-element.199), channel_id=1, source_target_pairs={{0,16},{4,20},{8,24},{12,28},{16,0},{20,4},{24,8},{28,12},{1,17},{... | collective-permute-start | bytes 393224 | tf_op jit(solution)/shard_map/ppermute | solution.py:227
  87.3 5.9 %collective-permute-start.28 = (bf16[2,32,1024]{2,1,0:T(8,128)(2,1)S(1)}, bf16[2,32,1024]{2,1,0:T(8,128)(2,1)S(1)}, u32[]{:S(2)}, u32[]{:S(2)}) collective-permute-start(bf16[2,32,1024]{2,1,0:T(8,128)(2,1)S(1)} %get-tuple-element.197), channel_id=1, source_target_pairs={{0,24},{4,28},{8,16},{12,20},{16,8},{20,12},{24,0},{28,4},{1,25},{... | collective-permute-start | bytes 393224 | tf_op jit(solution)/shard_map/ppermute | solution.py:227
  90.5 9.7 %collective-permute-start.30 = (f16[3,32,1024]{2,1,0:T(8,128)(2,1)S(1)}, f16[3,32,1024]{2,1,0:T(8,128)(2,1)S(1)}, u32[]{:S(2)}, u32[]{:S(2)}) collective-permute-start(f16[3,32,1024]{2,1,0:T(8,128)(2,1)S(1)} %fusion.26), channel_id=1, source_target_pairs={{0,1},{1,2},{2,3},{3,0},{4,5},{5,6},{6,7},{7,4},{8,9},{9,10},{10,1... | collective-permute-start | bytes 589832 | tf_op jit(solution)/shard_map/ppermute | solution.py:230
  93.2 15.6 %collective-permute-start.35 = (bf16[8,32,1024]{2,1,0:T(8,128)(2,1)S(1)}, bf16[8,32,1024]{2,1,0:T(8,128)(2,1)S(1)}, u32[]{:S(2)}, u32[]{:S(2)}) collective-permute-start(bf16[8,32,1024]{2,1,0:T(8,128)(2,1)S(1)} %constant_dynamic-update-slice_fusion.1.refs_0_), channel_id=1, source_target_pairs={{0,1},{1,2},{2,3},{3,0},{4,5},{5,6},{6,7},{7,4},{8,9},{9,10},{10,1... | collective-permute-start | bytes 1572872 | tf_op jit(solution)/shard_map/ppermute | solution.py:230
  102.2 6.6 %collective-permute-start.32 = (bf16[2,32,1024]{2,1,0:T(8,128)(2,1)S(1)}, bf16[2,32,1024]{2,1,0:T(8,128)(2,1)S(1)}, u32[]{:S(2)}, u32[]{:S(2)}) collective-permute-start(bf16[2,32,1024]{2,1,0:T(8,128)(2,1)S(1)} %get-tuple-element.190), channel_id=1, source_target_pairs={{0,8},{4,12},{8,0},{12,4},{16,24},{20,28},{24,16},{28,20},{1,9},{5... | collective-permute-start | bytes 393224 | tf_op jit(solution)/shard_map/ppermute | solution.py:227
  102.3 6.5 %collective-permute-start.33 = (bf16[2,32,1024]{2,1,0:T(8,128)(2,1)S(1)}, bf16[2,32,1024]{2,1,0:T(8,128)(2,1)S(1)}, u32[]{:S(2)}, u32[]{:S(2)}) collective-permute-start(bf16[2,32,1024]{2,1,0:T(8,128)(2,1)S(1)} %get-tuple-element.191), channel_id=1, source_target_pairs={{0,16},{4,20},{8,24},{12,28},{16,0},{20,4},{24,8},{28,12},{1,17},{... | collective-permute-start | bytes 393224 | tf_op jit(solution)/shard_map/ppermute | solution.py:227
  104.3 7.3 %collective-permute-start.34 = (bf16[2,32,1024]{2,1,0:T(8,128)(2,1)S(1)}, bf16[2,32,1024]{2,1,0:T(8,128)(2,1)S(1)}, u32[]{:S(2)}, u32[]{:S(2)}) collective-permute-start(bf16[2,32,1024]{2,1,0:T(8,128)(2,1)S(1)} %get-tuple-element.189), channel_id=1, source_target_pairs={{0,24},{4,28},{8,16},{12,20},{16,8},{20,12},{24,0},{28,4},{1,25},{... | collective-permute-start | bytes 393224 | tf_op jit(solution)/shard_map/ppermute | solution.py:227
  108.8 16.7 %collective-permute-start.37 = (bf16[8,32,1024]{2,1,0:T(8,128)(2,1)S(1)}, bf16[8,32,1024]{2,1,0:T(8,128)(2,1)S(1)}, u32[]{:S(2)}, u32[]{:S(2)}) collective-permute-start(bf16[8,32,1024]{2,1,0:T(8,128)(2,1)S(1)} %collective-permute-done.35.refs_1_), channel_id=1, source_target_pairs={{0,1},{1,2},{2,3},{3,0},{4,5},{5,6},{6,7},{7,4},{8,9},{9,10},{10,1... | collective-permute-start | bytes 1572872 | tf_op jit(solution)/shard_map/ppermute | solution.py:230
  111.7 25.1 %collective-permute-start.36 = (bf16[8,32,1024]{2,1,0:T(8,128)(2,1)S(1)}, bf16[8,32,1024]{2,1,0:T(8,128)(2,1)S(1)}, u32[]{:S(2)}, u32[]{:S(2)}) collective-permute-start(bf16[8,32,1024]{2,1,0:T(8,128)(2,1)S(1)} %constant_dynamic-update-slice_fusion.5.refs_0_), channel_id=1, source_target_pairs={{0,1},{1,2},{2,3},{3,0},{4,5},{5,6},{6,7},{7,4},{8,9},{9,10},{10,1... | collective-permute-start | bytes 1572872 | tf_op jit(solution)/shard_map/ppermute | solution.py:230
  125.5 22.5 %collective-permute-start.39 = (bf16[8,32,1024]{2,1,0:T(8,128)(2,1)S(1)}, bf16[8,32,1024]{2,1,0:T(8,128)(2,1)S(1)}, u32[]{:S(2)}, u32[]{:S(2)}) collective-permute-start(bf16[8,32,1024]{2,1,0:T(8,128)(2,1)S(1)} %collective-permute-done.37.refs_2_), channel_id=1, source_target_pairs={{0,1},{1,2},{2,3},{3,0},{4,5},{5,6},{6,7},{7,4},{8,9},{9,10},{10,1... | collective-permute-start | bytes 1572872 | tf_op jit(solution)/shard_map/ppermute | solution.py:230
  136.7 18.9 %collective-permute-start.38 = (bf16[8,32,1024]{2,1,0:T(8,128)(2,1)S(1)}, bf16[8,32,1024]{2,1,0:T(8,128)(2,1)S(1)}, u32[]{:S(2)}, u32[]{:S(2)}) collective-permute-start(bf16[8,32,1024]{2,1,0:T(8,128)(2,1)S(1)} %collective-permute-done.36.refs_1_), channel_id=1, source_target_pairs={{0,1},{1,2},{2,3},{3,0},{4,5},{5,6},{6,7},{7,4},{8,9},{9,10},{10,1... | collective-permute-start | bytes 1572872 | tf_op jit(solution)/shard_map/ppermute | solution.py:230
  155.7 15.6 %collective-permute-start.41 = (bf16[8,32,1024]{2,1,0:T(8,128)(2,1)S(1)}, bf16[8,32,1024]{2,1,0:T(8,128)(2,1)S(1)}, u32[]{:S(2)}, u32[]{:S(2)}) collective-permute-start(bf16[8,32,1024]{2,1,0:T(8,128)(2,1)S(1)} %collective-permute-done.38.refs_2_), channel_id=1, source_target_pairs={{0,1},{1,2},{2,3},{3,0},{4,5},{5,6},{6,7},{7,4},{8,9},{9,10},{10,1... | collective-permute-start | bytes 1572872 | tf_op jit(solution)/shard_map/ppermute | solution.py:230
  155.7 4.6 %collective-permute-start.42 = (f32[32,640]{1,0:T(8,128)S(1)}, f32[32,640]{1,0:T(8,128)S(1)}, u32[]{:S(2)}, u32[]{:S(2)}) collective-permute-start(f32[32,640]{1,0:T(8,128)S(1)} %get-tuple-element.216), channel_id=1, source_target_pairs={{0,8},{4,12},{8,0},{12,4},{16,24},{20,28},{24,16},{28,20},{1,9},{5... | collective-permute-start | bytes 245768 | tf_op jit(solution)/shard_map/ppermute | solution.py:227
  157.9 5.1 %collective-permute-start.43 = (f32[32,640]{1,0:T(8,128)S(1)}, f32[32,640]{1,0:T(8,128)S(1)}, u32[]{:S(2)}, u32[]{:S(2)}) collective-permute-start(f32[32,640]{1,0:T(8,128)S(1)} %get-tuple-element.215), channel_id=1, source_target_pairs={{0,16},{4,20},{8,24},{12,28},{16,0},{20,4},{24,8},{28,12},{1,17},{... | collective-permute-start | bytes 245768 | tf_op jit(solution)/shard_map/ppermute | solution.py:227
  163.0 4.5 %collective-permute-start.44 = (f32[32,640]{1,0:T(8,128)S(1)}, f32[32,640]{1,0:T(8,128)S(1)}, u32[]{:S(2)}, u32[]{:S(2)}) collective-permute-start(f32[32,640]{1,0:T(8,128)S(1)} %get-tuple-element.214.first_top), channel_id=1, source_target_pairs={{0,16},{4,20},{8,24},{12,28},{16,0},{20,4},{24,8},{28,12},{1,17},{... | collective-permute-start | bytes 245768 | tf_op jit(solution)/shard_map/ppermute | solution.py:227
  163.4 4.4 %collective-permute-start.45 = (f32[32,640]{1,0:T(8,128)S(1)}, f32[32,640]{1,0:T(8,128)S(1)}, u32[]{:S(2)}, u32[]{:S(2)}) collective-permute-start(f32[32,640]{1,0:T(8,128)S(1)} %get-tuple-element.213.first_bottom), channel_id=1, source_target_pairs={{0,8},{4,12},{8,0},{12,4},{16,24},{20,28},{24,16},{28,20},{1,9},{5... | collective-permute-start | bytes 245768 | tf_op jit(solution)/shard_map/ppermute | solution.py:227
  175.9 4.6 %collective-permute-start.47 = (f32[32,640]{1,0:T(8,128)S(1)}, f32[32,640]{1,0:T(8,128)S(1)}, u32[]{:S(2)}, u32[]{:S(2)}) collective-permute-start(f32[32,640]{1,0:T(8,128)S(1)} %get-tuple-element.212), channel_id=1, source_target_pairs={{0,8},{4,12},{8,0},{12,4},{16,24},{20,28},{24,16},{28,20},{1,9},{5... | collective-permute-start | bytes 245768 | tf_op jit(solution)/shard_map/ppermute | solution.py:227
  176.8 4.4 %collective-permute-start.48 = (f32[32,640]{1,0:T(8,128)S(1)}, f32[32,640]{1,0:T(8,128)S(1)}, u32[]{:S(2)}, u32[]{:S(2)}) collective-permute-start(f32[32,640]{1,0:T(8,128)S(1)} %get-tuple-element.211), channel_id=1, source_target_pairs={{0,16},{4,20},{8,24},{12,28},{16,0},{20,4},{24,8},{28,12},{1,17},{... | collective-permute-start | bytes 245768 | tf_op jit(solution)/shard_map/ppermute | solution.py:227
  177.9 6.6 %collective-permute-start.51 = (f32[64,512]{1,0:T(8,128)S(1)}, f32[64,512]{1,0:T(8,128)S(1)}, u32[]{:S(2)}, u32[]{:S(2)}) collective-permute-start(f32[64,512]{1,0:T(8,128)S(1)} %solve.2.mine), channel_id=1, source_target_pairs={{0,4},{4,0},{8,12},{12,8},{16,20},{20,16},{24,28},{28,24},{1,5},{5... | collective-permute-start | bytes 393224 | tf_op jit(solution)/shard_map/ppermute | solution.py:227
  181.3 5.5 %collective-permute-start.49 = (f32[32,640]{1,0:T(8,128)S(1)}, f32[32,640]{1,0:T(8,128)S(1)}, u32[]{:S(2)}, u32[]{:S(2)}) collective-permute-start(f32[32,640]{1,0:T(8,128)S(1)} %get-tuple-element.210.first_top), channel_id=1, source_target_pairs={{0,16},{4,20},{8,24},{12,28},{16,0},{20,4},{24,8},{28,12},{1,17},{... | collective-permute-start | bytes 245768 | tf_op jit(solution)/shard_map/ppermute | solution.py:227
  182.4 4.4 %collective-permute-start.50 = (f32[32,640]{1,0:T(8,128)S(1)}, f32[32,640]{1,0:T(8,128)S(1)}, u32[]{:S(2)}, u32[]{:S(2)}) collective-permute-start(f32[32,640]{1,0:T(8,128)S(1)} %get-tuple-element.209.first_bottom), channel_id=1, source_target_pairs={{0,8},{4,12},{8,0},{12,4},{16,24},{20,28},{24,16},{28,20},{1,9},{5... | collective-permute-start | bytes 245768 | tf_op jit(solution)/shard_map/ppermute | solution.py:227
  (15 other events, 175.7 us)
